TPU v7x, 32 devices: a whole 2x2x4 slice. The times are simulated.
32 devices in a mesh: section: 4 (over y, core), dp: 8 (over z, x).
Axes of the slice: x: 2, y: 2, z: 4, core: 2. Of those that a mesh axis runs over, the one named last changes fastest.
Arguments:
- table: bfloat16 [32000, 512], P(('section', 'dp')), may hold values from -6 to 6
- piece_ids: int32 [1024, 8], P('dp'), may hold values from 0 to 31999
- piece_counts: int32 [1024], P('dp'), may hold values from 1 to 8
- vocab_size: int32 [1], replicated, may hold values from 768 to 1024
- norm_gain: float32 [4, 2, 512], P('section'), may hold values from 0.5 to 1.5
- shift_bias: float32 [4, 4, 512], P('section'), may hold values from -2.5 to 2.5
- up_bias: float32 [4, 2048], P('section'), may hold values from -2.5 to 2.5
- qkv_weight: bfloat16 [4, 512, 1536], P('section'), may hold values from -0.25 to 0.25
- out_weight: bfloat16 [4, 512, 512], P('section'), may hold values from -0.5 to 0.5
- up_weight: bfloat16 [4, 512, 2048], P('section'), may hold values from -0.25 to 0.25
- down_weight: bfloat16 [4, 2048, 512], P('section'), may hold values from -0.125 to 0.125
- proj_weight: bfloat16 [512, 2048], P(None, 'section'), may hold values from -0.25 to 0.25
- embed_cotangent: bfloat16 [1024, 2048], P('dp', 'section'), may hold values from -6 to 6
Outputs:
- embeddings: float32 [1024, 2048], P('dp', 'section')
- table_grad: float32 [32000, 512], P(('section', 'dp'))
- norm_gain_grad: float32 [4, 2, 512], P('section', None, 'dp')
- shift_bias_grad: float32 [4, 4, 512], P('section', None, 'dp')
- up_bias_grad: float32 [4, 2048], P('section', 'dp')
- qkv_grad: float32 [4, 512, 1536], P('section', 'dp')
- out_grad: float32 [4, 512, 512], P('section', 'dp')
- up_grad: float32 [4, 512, 2048], P('section', 'dp')
- down_grad: float32 [4, 2048, 512], P('section', 'dp')
- proj_grad: float32 [512, 2048], P('dp', 'section')
Inputs may be any that keep to these rules, and one draw needn't show every extreme that they name: Entries numbered vocab_size and above are padding. `piece_counts`: slots at or beyond an entry's count are padding.
All inputs are finite; a program needn't handle non-finite values.
Results may differ from a plain program's by a relative error of at most 0.024.
Values may be sent and summed in bfloat16 or wider, within the bound.
A program may use at most 192 MiB of HBM per device.

v0:
```python
import jax
import jax.numpy as jnp
from jax import lax
from jax.sharding import PartitionSpec as P

HEADS = 8
MB = 4


EPSILON = 1e-05
MASKED = -1e30
ROOT_HALF = 0.7071067811865476
DENSITY_SCALE = 0.3989422804014327


def shifted_2(value, axis, steps):
    count = lax.axis_size(axis)
    first, last = (max(0, -steps), min(count, count - steps))
    return lax.ppermute(value, axis, [(source, source + steps) for source in range(first, last)])


def from_root(block, axis, source):
    block = jnp.where(lax.axis_index(axis) == source, block, jnp.zeros_like(block))
    return lax.psum(block, axis)


def contract_rows(left, right):
    return lax.dot_general(
        left, right, (((0,), (0,)), ((), ())), preferred_element_type=jnp.float32
    )


def times_transposed(left, right):
    return lax.dot_general(
        left, right, (((1,), (1,)), ((), ())), preferred_element_type=jnp.float32
    )


def statistics(values):
    centered = values - jnp.mean(values, axis=-1, keepdims=True)
    inverse = lax.rsqrt(jnp.mean(centered * centered, axis=-1, keepdims=True) + EPSILON)
    return (centered * inverse, inverse)


def norm_backward(grad_out, gain, normed, inverse):
    weighted = grad_out * gain
    inner = (
        weighted
        - jnp.mean(weighted, axis=-1, keepdims=True)
        - normed * jnp.mean(weighted * normed, axis=-1, keepdims=True)
    )
    return (inner * inverse, jnp.sum(grad_out * normed, axis=0), jnp.sum(grad_out, axis=0))


def layer_forward(hidden_in, params, key_mask):
    gains, offsets, w_qkv, w_out, w_up, b_up, w_down = params
    micro_rows, model_width = hidden_in.shape
    entry_count, pieces = key_mask.shape
    head_size = model_width // HEADS
    score_scale = head_size ** (-0.5)
    normed_one, inverse_one = statistics(hidden_in.astype(jnp.float32))
    normed = (normed_one * gains[0] + offsets[0]).astype(jnp.bfloat16)
    joined = jnp.dot(normed, w_qkv, preferred_element_type=jnp.float32).astype(jnp.bfloat16)
    heads_split = joined.reshape(entry_count, pieces, 3, HEADS, head_size)
    scores = (
        jnp.einsum(
            "bihe,bjhe->bhij",
            heads_split[:, :, 0],
            heads_split[:, :, 1],
            preferred_element_type=jnp.float32,
        )
        * score_scale
    )
    scores = jnp.where(key_mask[:, None, None, :], scores, MASKED)
    shifted = jnp.exp(scores - jnp.max(scores, axis=-1, keepdims=True))
    attn_prob = shifted / jnp.sum(shifted, axis=-1, keepdims=True)
    mixed_heads = jnp.einsum(
        "bhij,bjhe->bihe",
        attn_prob.astype(jnp.bfloat16),
        heads_split[:, :, 2],
        preferred_element_type=jnp.float32,
    )
    mixed_heads = mixed_heads.reshape(micro_rows, model_width).astype(jnp.bfloat16)
    residual = (
        hidden_in.astype(jnp.float32)
        + jnp.dot(mixed_heads, w_out, preferred_element_type=jnp.float32)
        + offsets[1]
    )
    normed_two_hat, inverse_two = statistics(residual)
    normed_two = (normed_two_hat * gains[1] + offsets[2]).astype(jnp.bfloat16)
    pre_act = jnp.dot(normed_two, w_up, preferred_element_type=jnp.float32) + b_up
    activated = jax.nn.gelu(pre_act, approximate=False).astype(jnp.bfloat16)
    output = (
        residual + jnp.dot(activated, w_down, preferred_element_type=jnp.float32) + offsets[3]
    ).astype(jnp.bfloat16)
    stashed = (
        normed_one,
        inverse_one,
        normed,
        joined,
        attn_prob,
        mixed_heads,
        normed_two_hat,
        inverse_two,
        normed_two,
        pre_act,
        activated,
    )
    return (output, stashed)


def layer_backward(grad_out, stashed, params, key_mask):
    gains, offsets, w_qkv, w_out, w_up, b_up, w_down = params
    (
        normed_one,
        inverse_one,
        normed,
        joined,
        attn_prob,
        mixed_heads,
        normed_two_hat,
        inverse_two,
        normed_two,
        pre_act,
        activated,
    ) = stashed
    micro_rows, model_width = grad_out.shape
    entry_count, pieces = key_mask.shape
    head_size = model_width // HEADS
    score_scale = head_size ** (-0.5)
    grad_float = grad_out.astype(jnp.float32)
    grad_down = contract_rows(activated, grad_out)
    grad_shift_three = jnp.sum(grad_float, axis=0)
    grad_act = times_transposed(grad_out, w_down)
    cumulative = 0.5 * (1.0 + jax.scipy.special.erf(pre_act * ROOT_HALF))
    density = jnp.exp(-0.5 * pre_act * pre_act) * DENSITY_SCALE
    grad_pre = (grad_act * (cumulative + pre_act * density)).astype(jnp.bfloat16)
    grad_up = contract_rows(normed_two, grad_pre)
    grad_up_bias = jnp.sum(grad_pre.astype(jnp.float32), axis=0)
    grad_normed_two = times_transposed(grad_pre, w_up)
    grad_resid_norm, grad_gain_two, grad_shift_two = norm_backward(
        grad_normed_two, gains[1], normed_two_hat, inverse_two
    )
    grad_resid = grad_float + grad_resid_norm
    grad_branch = grad_resid.astype(jnp.bfloat16)
    grad_out_proj = contract_rows(mixed_heads, grad_branch)
    grad_shift_one = jnp.sum(grad_branch.astype(jnp.float32), axis=0)
    grad_mixed = times_transposed(grad_branch, w_out).astype(jnp.bfloat16)
    grad_mixed = grad_mixed.reshape(entry_count, pieces, HEADS, head_size)
    heads_split = joined.reshape(entry_count, pieces, 3, HEADS, head_size)
    queries = heads_split[:, :, 0]
    key_rows = heads_split[:, :, 1]
    value_rows = heads_split[:, :, 2]
    grad_prob = jnp.einsum(
        "bihe,bjhe->bhij", grad_mixed, value_rows, preferred_element_type=jnp.float32
    )
    grad_values = jnp.einsum(
        "bhij,bihe->bjhe",
        attn_prob.astype(jnp.bfloat16),
        grad_mixed,
        preferred_element_type=jnp.float32,
    )
    grad_scores = attn_prob * (grad_prob - jnp.sum(grad_prob * attn_prob, axis=-1, keepdims=True))
    grad_scores = grad_scores.astype(jnp.bfloat16)
    grad_queries = (
        jnp.einsum("bhij,bjhe->bihe", grad_scores, key_rows, preferred_element_type=jnp.float32)
        * score_scale
    )
    grad_keys = (
        jnp.einsum("bhij,bihe->bjhe", grad_scores, queries, preferred_element_type=jnp.float32)
        * score_scale
    )
    grad_joined = jnp.stack((grad_queries, grad_keys, grad_values), axis=2)
    grad_joined = grad_joined.reshape(micro_rows, 3 * model_width).astype(jnp.bfloat16)
    grad_qkv = contract_rows(normed, grad_joined)
    grad_normed = times_transposed(grad_joined, w_qkv)
    grad_in_norm, grad_gain_one, grad_shift_zero = norm_backward(
        grad_normed, gains[0], normed_one, inverse_one
    )
    grad_in = grad_resid + grad_in_norm
    gradients = (
        jnp.stack((grad_gain_one, grad_gain_two)),
        jnp.stack((grad_shift_zero, grad_shift_one, grad_shift_two, grad_shift_three)),
        grad_qkv,
        grad_out_proj,
        grad_up,
        grad_up_bias,
        grad_down,
    )
    return (grad_in, gradients)


def store(buffers, values, slot_index, usable):

    def place_one(buffer, fresh_value):
        previous = lax.dynamic_index_in_dim(buffer, slot_index, 0, keepdims=False)
        return lax.dynamic_update_index_in_dim(
            buffer, jnp.where(usable, fresh_value, previous), slot_index, 0
        )

    return jax.tree.map(place_one, buffers, values)


def fetch(buffers, slot_index):
    return jax.tree.map(
        lambda buffer: lax.dynamic_index_in_dim(buffer, slot_index, 0, keepdims=False), buffers
    )


def quarter_rows(flat_ids, span, section_index):
    local_ids = flat_ids - section_index * span
    inside = (local_ids >= 0) & (local_ids < span)
    return (jnp.clip(local_ids, 0, span - 1), inside)


def local(
    table,
    piece_ids,
    piece_counts,
    vocab_size,
    norm_gain,
    shift_bias,
    up_bias,
    qkv_weight,
    out_weight,
    up_weight,
    down_weight,
    proj_weight,
    embed_cotangent,
):
    sections = lax.axis_size("section")
    section_index = lax.axis_index("section")
    column = lax.axis_index("dp")
    entries, pieces = piece_ids.shape
    model_width = qkv_weight.shape[1]
    micro_count = MB
    per_micro = entries // micro_count
    micro_rows = per_micro * pieces
    tick_count = micro_count + sections - 1
    positions = column * entries + jnp.arange(entries, dtype=jnp.int32)
    live = (positions < vocab_size[0]).astype(jnp.float32)
    key_mask = jnp.arange(pieces, dtype=jnp.int32)[None, :] < piece_counts[:, None]
    share = key_mask.astype(jnp.float32) / piece_counts.astype(jnp.float32)[:, None]
    flat_ids = piece_ids.reshape(entries * pieces)
    quarter = lax.all_gather(table, "dp", axis=0, tiled=True)
    safe_ids, inside = quarter_rows(flat_ids, quarter.shape[0], section_index)
    picked = jnp.where(
        inside[:, None], jnp.take(quarter, safe_ids, axis=0).astype(jnp.float32), 0.0
    )
    embedded = lax.psum(picked.astype(jnp.bfloat16), "section")
    params = (
        norm_gain[0],
        shift_bias[0],
        qkv_weight[0],
        out_weight[0],
        up_weight[0],
        up_bias[0],
        down_weight[0],
    )
    inputs = embedded.reshape(micro_count, micro_rows, model_width)
    key_masks = key_mask.reshape(micro_count, per_micro, pieces)
    arriving = jnp.zeros((micro_rows, model_width), jnp.bfloat16)
    outputs = []
    buffers = ()
    for moment in range(tick_count):
        micro_index = moment - section_index
        usable = (micro_index >= 0) & (micro_index < micro_count)
        slot_index = jnp.clip(micro_index, 0, micro_count - 1)
        current = jnp.where(section_index == 0, inputs[min(moment, micro_count - 1)], arriving)
        mask_now = lax.dynamic_index_in_dim(key_masks, slot_index, 0, keepdims=False)
        result, stashed = layer_forward(current, params, mask_now)
        if moment == 0:
            buffers = jax.tree.map(
                lambda kept_item: jnp.zeros((micro_count,) + kept_item.shape, kept_item.dtype),
                stashed,
            )
        buffers = store(buffers, stashed, slot_index, usable)
        outputs.append(result)
        if moment + 1 < tick_count:
            arriving = shifted_2(result, "section", 1)
    finals = jnp.stack(outputs[sections - 1 :]).reshape(entries, pieces, model_width)
    pooled = jnp.sum(finals.astype(jnp.float32) * share[:, :, None], axis=1).astype(jnp.bfloat16)
    pooled = from_root(pooled, "section", sections - 1)
    embeddings = jnp.dot(pooled, proj_weight, preferred_element_type=jnp.float32) * live[:, None]
    cotangent = jnp.where(live[:, None] > 0, embed_cotangent, jnp.zeros_like(embed_cotangent))
    grad_proj = contract_rows(pooled, cotangent)
    pooled_grad = lax.psum(
        times_transposed(cotangent, proj_weight).astype(jnp.bfloat16), "section"
    ).astype(jnp.float32)
    seeds = (pooled_grad[:, None, :] * share[:, :, None]).astype(jnp.bfloat16)
    seeds = seeds.reshape(micro_count, micro_rows, model_width)
    totals = jax.tree.map(lambda param_item: jnp.zeros(param_item.shape, jnp.float32), params)
    returning = jnp.zeros((micro_rows, model_width), jnp.bfloat16)
    first_grads = []
    for moment in range(tick_count):
        micro_index = moment - (sections - 1 - section_index)
        usable = (micro_index >= 0) & (micro_index < micro_count)
        slot_index = jnp.clip(micro_index, 0, micro_count - 1)
        grad_here = jnp.where(
            section_index == sections - 1, seeds[min(moment, micro_count - 1)], returning
        )
        mask_now = lax.dynamic_index_in_dim(key_masks, slot_index, 0, keepdims=False)
        fetched = fetch(buffers, slot_index)
        grad_in, gradients = layer_backward(grad_here, fetched, params, mask_now)
        totals = jax.tree.map(
            lambda total_item, grad_item: total_item + jnp.where(usable, grad_item, 0.0),
            totals,
            gradients,
        )
        first_grads.append(grad_in)
        if moment + 1 < tick_count:
            returning = shifted_2(grad_in.astype(jnp.bfloat16), "section", -1)
    piece_grads = jnp.stack(first_grads[sections - 1 :]).reshape(entries * pieces, model_width)
    spread = from_root(piece_grads.astype(jnp.bfloat16), "section", 0).astype(piece_grads.dtype)
    partial_rows = jax.ops.segment_sum(
        jnp.where(inside[:, None], spread, 0.0), safe_ids, num_segments=quarter.shape[0]
    )
    table_grad = lax.psum_scatter(partial_rows, "dp", scatter_dimension=0, tiled=True)
    gain_total, shift_total, qkv_total, out_total, up_total, up_bias_total, down_total = totals
    reduced = (
        lax.psum_scatter(gain_total[None], "dp", scatter_dimension=2, tiled=True),
        lax.psum_scatter(shift_total[None], "dp", scatter_dimension=2, tiled=True),
        lax.psum_scatter(up_bias_total[None], "dp", scatter_dimension=1, tiled=True),
        lax.psum_scatter(qkv_total[None], "dp", scatter_dimension=1, tiled=True),
        lax.psum_scatter(out_total[None], "dp", scatter_dimension=1, tiled=True),
        lax.psum_scatter(up_total[None], "dp", scatter_dimension=1, tiled=True),
        lax.psum_scatter(down_total[None], "dp", scatter_dimension=1, tiled=True),
        lax.psum_scatter(grad_proj, "dp", scatter_dimension=0, tiled=True),
    )
    return (
        embeddings,
        table_grad,
        reduced[0],
        reduced[1],
        reduced[2],
        reduced[3],
        reduced[4],
        reduced[5],
        reduced[6],
        reduced[7],
    )


def solution(mesh):
    return jax.shard_map(
        local,
        mesh=mesh,
        in_specs=(
            P(("section", "dp"), None),
            P("dp", None),
            P("dp"),
            P(),
            P("section", None, None),
            P("section", None, None),
            P("section", None),
            P("section", None, None),
            P("section", None, None),
            P("section", None, None),
            P("section", None, None),
            P(None, "section"),
            P("dp", "section"),
        ),
        out_specs=(
            P("dp", "section"),
            P(("section", "dp"), None),
            P("section", None, "dp"),
            P("section", None, "dp"),
            P("section", "dp"),
            P("section", "dp", None),
            P("section", "dp", None),
            P("section", "dp", None),
            P("section", "dp", None),
            P("dp", "section"),
        ),
        check_vma=False,
    )
```

profile of v0, /device:TPU:0, one launch (start us, length us, event | category | flops | bytes accessed | tf_op | source)
XLA Modules:
  0.0 1718.5 jit_solution(6690888280776646747)
XLA Ops:
  14.8 120.6 %all-gather.2.cloned.1.call-done = bf16[8000,512]{1,0:T(8,128)(2,1)} async-done(((bf16[1000,512]{1,0:T(8,128)(2,1)}), bf16[8000,512]{1,0:T(8,128)(2,1)}) %all-gather.2.cloned.1.call-update) | async-done | bytes 8192016 | tf_op jit(solution)/shard_map/all_gather | solution.py:245
  135.3 9.5 gather_fusion
  149.9 33.5 %all-reduce.7.cloned.1.call-done = (bf16[1024,512]{1,0:T(8,128)(2,1)}, bf16[128,512]{1,0:T(8,128)(2,1)}) async-done(((bf16[1024,512]{1,0:T(8,128)(2,1)}, bf16[128,512]{1,0:T(8,128)(2,1)}), (bf16[1024,512]{1,0:T(8,128)(2,1)}, bf16[128,512]{1,0:T(8,128)(2,1)})) %all-reduce.7.cloned.1.call-update) | async-done | bytes 1179664 | tf_op jit(solution)/shard_map/psum | solution.py:250
  206.7 5.1 bitcast_dynamic-update-slice_fusion.13
  247.8 3.1 reshape.1902
  263.2 6.3 bitcast_dynamic-update-slice_fusion.12
  270.3 3.5 collective-permute-start.1
  281.3 3.3 constant_dynamic-slice_fusion.79
  302.1 3.1 reshape.1903
  317.4 6.3 bitcast_dynamic-update-slice_fusion.11
  334.3 3.3 constant_dynamic-slice_fusion.78
  356.4 3.1 reshape.1904
  371.8 6.3 bitcast_dynamic-update-slice_fusion.10
  388.7 3.3 constant_dynamic-slice_fusion.77
  406.9 3.1 reshape.1905
  422.3 6.3 bitcast_dynamic-update-slice_fusion.9
  437.6 3.3 constant_dynamic-slice_fusion.76
  456.2 3.1 reshape.1906
  471.5 6.3 bitcast_dynamic-update-slice_fusion.8
  486.2 3.3 constant_dynamic-slice_fusion.75
  504.9 3.2 reshape.1907
  522.4 7.1 bitcast_dynamic-update-slice_fusion.7
  536.4 3.2 convert_reduce_fusion.6
  546.9 5.2 constant_dynamic-slice_fusion.19
  552.1 3.3 reshape.1908
  564.7 3.4 convert_element_type.720
  574.0 3.1 reshape.1910
  585.2 3.1 reshape.1914
  590.8 3.1 reshape.1916
  596.4 3.1 reshape.1918
  624.8 3.4 convert_element_type.728
  628.2 3.3 fusion.511
  638.0 3.3 convert_reduce_fusion.4
  655.2 3.4 convert_element_type.736
  658.6 3.2 fusion.501
  666.8 4.1 collective-permute-done.8
  688.8 3.4 convert_element_type.744
  692.2 3.3 fusion.491
  700.5 4.1 collective-permute-done.9
  722.6 3.4 convert_element_type.751
  726.1 3.2 fusion.481
  734.3 4.1 collective-permute-done.10
  739.4 3.1 convert_reduce_fusion.1
  756.4 3.4 convert_element_type.758
  759.8 3.3 fusion.471
  768.1 4.1 collective-permute-done.11
  773.3 3.3 convert_reduce_fusion
  789.4 3.4 convert_element_type.765
  792.8 3.2 fusion.461
  818.4 3.2 convolution_select_fusion.5
  821.6 18.8 %all-reduce.5.cloned.1.call-done = (bf16[128,512]{1,0:T(8,128)(2,1)}, bf16[1024,512]{1,0:T(8,128)(2,1)}) async-done(((bf16[128,512]{1,0:T(8,128)(2,1)}, bf16[1024,512]{1,0:T(8,128)(2,1)}), (bf16[128,512]{1,0:T(8,128)(2,1)}, bf16[1024,512]{1,0:T(8,128)(2,1)})) %all-reduce.5.cloned.1.call-update) | async-done | bytes 1179664 | tf_op jit(solution)/shard_map/psum | solution.py:24
  851.8 3.4 fusion.15
  866.2 3.7 fusion.566
  869.9 5.0 add_bitcast_fusion.1
  886.1 6.0 add_bitcast_fusion
  892.8 14.3 scatter_custom_fusion
  908.7 60.3 %reduce-scatter.30.cloned.1.call-done = f32[64,4]{1,0:T(8,128)} async-done(((f32[512,4]{1,0:T(8,128)}), f32[64,4]{1,0:T(8,128)}) %reduce-scatter.30.cloned.1.call-update) | async-done | bytes 1040
  970.4 64.4 %reduce-scatter.32.cloned.1.call-done = f32[256,1]{1,0:T(8,128)} async-done(((f32[2048,1]{1,0:T(8,128)}), f32[256,1]{1,0:T(8,128)}) %reduce-scatter.32.cloned.1.call-update) | async-done | bytes 1040
  1037.3 64.4 %reduce-scatter.20.cloned.1.call-done = f32[1,64,512]{2,1,0:T(8,128)} async-done(((f32[1,512,512]{2,1,0:T(8,128)}), f32[1,64,512]{2,1,0:T(8,128)}) %reduce-scatter.20.cloned.1.call-update) | async-done | bytes 131088 | tf_op jit(solution)/shard_map/reduce_scatter | solution.py:325
  1101.8 66.5 %reduce-scatter.26.cloned.1.call-done = f32[64,512]{1,0:T(8,128)} async-done(((f32[512,512]{1,0:T(8,128)}), f32[64,512]{1,0:T(8,128)}) %reduce-scatter.26.cloned.1.call-update) | async-done | bytes 131088 | tf_op jit(solution)/shard_map/reduce_scatter | solution.py:328
  1168.3 78.1 %reduce-scatter.18.cloned.1.call-done = f32[1,64,1536]{2,1,0:T(8,128)} async-done(((f32[1,512,1536]{2,1,0:T(8,128)}), f32[1,64,1536]{2,1,0:T(8,128)}) %reduce-scatter.18.cloned.1.call-update) | async-done | bytes 393232 | tf_op jit(solution)/shard_map/reduce_scatter | solution.py:324
  1246.4 91.7 %reduce-scatter.22.cloned.1.call-done = f32[1,64,2048]{2,1,0:T(8,128)} async-done(((f32[1,512,2048]{2,1,0:T(8,128)}), f32[1,64,2048]{2,1,0:T(8,128)}) %reduce-scatter.22.cloned.1.call-update) | async-done | bytes 524304 | tf_op jit(solution)/shard_map/reduce_scatter | solution.py:326
  1338.1 92.1 %reduce-scatter.24.cloned.1.call-done = f32[1,256,512]{2,1,0:T(8,128)} async-done(((f32[1,2048,512]{2,1,0:T(8,128)}), f32[1,256,512]{2,1,0:T(8,128)}) %reduce-scatter.24.cloned.1.call-update) | async-done | bytes 524304 | tf_op jit(solution)/shard_map/reduce_scatter | solution.py:327
  1430.2 281.3 %reduce-scatter.16.cloned.1.call-done = f32[1000,512]{1,0:T(8,128)} async-done(((f32[8000,512]{1,0:T(8,128)}), f32[1000,512]{1,0:T(8,128)}) %reduce-scatter.16.cloned.1.call-update) | async-done | bytes 2048016 | tf_op jit(solution)/shard_map/reduce_scatter | solution.py:318
  (1035 shorter events, 506.9 us)
Async XLA Ops:
  7.2 199.3 %copy-start = (bf16[1,512,2048]{2,1,0:T(8,128)(2,1)S(1)}, bf16[1,512,2048]{2,1,0:T(8,128)(2,1)}, u32[]{:S(2)}) copy-start(bf16[1,512,2048]{2,1,0:T(8,128)(2,1)} %param.22) | copy-start | bytes 6291460
  7.2 128.1 %all-gather.2.cloned.1.call-start = ((), (), s32[]{:S(2)}) async-start(), calls=%async_computation.9 | async-start | bytes 9216000 | tf_op jit(solution)/shard_map/all_gather | solution.py:245
  7.9 175.5 %all-reduce.7.cloned.1.call-start = ((), (), s32[]{:S(2)}) async-start(), calls=%async_computation.20 | async-start | bytes 2359296 | tf_op jit(solution)/shard_map/psum | solution.py:250
  9.0 135.9 %copy-start.180 = (s32[1024]{0:T(1024)}, s32[1024]{0:T(1024)S(1)}, u32[]{:S(2)}) copy-start(s32[1024]{0:T(1024)S(1)} %min.59) | copy-start | bytes 12292
  11.3 133.5 %copy-start.213 = (pred[1024]{0:T(1024)(128)(4,1)}, pred[1024]{0:T(1024)(128)(4,1)S(1)}, u32[]{:S(2)}) copy-start(pred[1024]{0:T(1024)(128)(4,1)S(1)} %and.62) | copy-start | bytes 3076
  12.6 122.8 %copy-start.220 = (pred[128]{0:T(512)(128)(4,1)}, pred[128]{0:T(512)(128)(4,1)S(1)}, u32[]{:S(2)}) copy-start(pred[128]{0:T(512)(128)(4,1)S(1)} %get-tuple-element.122) | copy-start | bytes 388
  147.6 692.9 %all-reduce.5.cloned.1.call-start = ((), (), s32[]{:S(2)}) async-start(), calls=%async_computation.19 | async-start | bytes 2359296 | tf_op jit(solution)/shard_map/psum | solution.py:24
  213.9 30.6 %collective-permute-start = (bf16[256,512]{1,0:T(8,128)(2,1)}, bf16[256,512]{1,0:T(8,128)(2,1)S(1)}, u32[]{:S(2)}, u32[]{:S(2)}) collective-permute-start(bf16[256,512]{1,0:T(8,128)(2,1)} %fusion.344), channel_id=1, source_target_pairs={{0,8},{8,16},{16,24},{1,9},{9,17},{17,25},{2,10},{10,18},{18,26},{... | collective-permute-start | bytes 786440 | tf_op jit(solution)/shard_map/ppermute | solution.py:19
  220.6 8.0 copy-start.4
  234.2 7.3 copy-start.163
  270.3 28.5 %collective-permute-start.1 = (bf16[256,512]{1,0:T(8,128)(2,1)S(1)}, bf16[256,512]{1,0:T(8,128)(2,1)S(1)}, u32[]{:S(2)}, u32[]{:S(2)}) collective-permute-start(bf16[256,512]{1,0:T(8,128)(2,1)S(1)} %fusion.341), channel_id=1, source_target_pairs={{0,8},{8,16},{16,24},{1,9},{9,17},{17,25},{2,10},{10,18},{18,26},{... | collective-permute-start | bytes 786440 | tf_op jit(solution)/shard_map/ppermute | solution.py:19
  291.8 8.3 copy-start.273
  324.5 28.7 %collective-permute-start.2 = (bf16[256,512]{1,0:T(8,128)(2,1)S(1)}, bf16[256,512]{1,0:T(8,128)(2,1)S(1)}, u32[]{:S(2)}, u32[]{:S(2)}) collective-permute-start(bf16[256,512]{1,0:T(8,128)(2,1)S(1)} %fusion.338), channel_id=1, source_target_pairs={{0,8},{8,16},{16,24},{1,9},{9,17},{17,25},{2,10},{10,18},{18,26},{... | collective-permute-start | bytes 786440 | tf_op jit(solution)/shard_map/ppermute | solution.py:19
  338.9 8.4 copy-start.120
  347.4 7.2 copy-start.274
  378.9 7.3 copy-start.157
  378.9 24.8 %collective-permute-start.3 = (bf16[256,512]{1,0:T(8,128)(2,1)S(1)}, bf16[256,512]{1,0:T(8,128)(2,1)S(1)}, u32[]{:S(2)}, u32[]{:S(2)}) collective-permute-start(bf16[256,512]{1,0:T(8,128)(2,1)S(1)} %fusion.335), channel_id=1, source_target_pairs={{0,8},{8,16},{16,24},{1,9},{9,17},{17,25},{2,10},{10,18},{18,26},{... | collective-permute-start | bytes 786440 | tf_op jit(solution)/shard_map/ppermute | solution.py:19
  393.3 9.5 copy-start.110
  396.6 8.5 copy-start.275
  404.8 27.3 %copy-start.48 = (bf16[256,512]{1,0:T(8,128)(2,1)}, bf16[256,512]{1,0:T(8,128)(2,1)S(1)}, u32[]{:S(2)}) copy-start(bf16[256,512]{1,0:T(8,128)(2,1)S(1)} %get-tuple-element.115) | copy-start | bytes 786436
  422.0 13.0 copy-start.17
  422.0 13.0 copy-start.184
  422.2 22.2 %copy-start.202 = (f32[256]{0:T(256)}, f32[256]{0:T(256)S(1)}, u32[]{:S(2)}) copy-start(f32[256]{0:T(256)S(1)} %add_rsqrt_fusion.4) | copy-start | bytes 3076
  429.4 8.2 copy-start.159
  429.4 23.6 %collective-permute-start.4 = (bf16[256,512]{1,0:T(8,128)(2,1)S(1)}, bf16[256,512]{1,0:T(8,128)(2,1)S(1)}, u32[]{:S(2)}, u32[]{:S(2)}) collective-permute-start(bf16[256,512]{1,0:T(8,128)(2,1)S(1)} %fusion.332), channel_id=1, source_target_pairs={{0,8},{8,16},{16,24},{1,9},{9,17},{17,25},{2,10},{10,18},{18,26},{... | collective-permute-start | bytes 786440 | tf_op jit(solution)/shard_map/ppermute | solution.py:19
  471.3 12.4 copy-start.189
  471.5 21.6 %copy-start.207 = (f32[256]{0:T(256)}, f32[256]{0:T(256)S(1)}, u32[]{:S(2)}) copy-start(f32[256]{0:T(256)S(1)} %add_rsqrt_fusion.2) | copy-start | bytes 3076
  478.6 7.6 copy-start.161
  478.6 23.0 %collective-permute-start.5 = (bf16[256,512]{1,0:T(8,128)(2,1)S(1)}, bf16[256,512]{1,0:T(8,128)(2,1)S(1)}, u32[]{:S(2)}, u32[]{:S(2)}) collective-permute-start(bf16[256,512]{1,0:T(8,128)(2,1)S(1)} %fusion.329), channel_id=1, source_target_pairs={{0,8},{8,16},{16,24},{1,9},{9,17},{17,25},{2,10},{10,18},{18,26},{... | collective-permute-start | bytes 786440 | tf_op jit(solution)/shard_map/ppermute | solution.py:19
  522.2 11.4 copy-start.28
  522.2 11.3 copy-start.168
  522.4 20.3 %copy-start.175 = (f32[256]{0:T(256)}, f32[256]{0:T(256)S(1)}, u32[]{:S(2)}) copy-start(f32[256]{0:T(256)S(1)} %add_rsqrt_fusion) | copy-start | bytes 3076
  522.4 7.2 copy-start.257
  522.4 7.2 copy-start.264
  532.1 10.6 copy-start.16
  534.6 8.2 copy-start.8
  572.7 34.3 %collective-permute-start.6 = (bf16[256,512]{1,0:T(8,128)(2,1)}, bf16[256,512]{1,0:T(8,128)(2,1)}, u32[]{:S(2)}, u32[]{:S(2)}) collective-permute-start(bf16[256,512]{1,0:T(8,128)(2,1)} %fusion.520), channel_id=1, source_target_pairs={{8,0},{16,8},{24,16},{9,1},{17,9},{25,17},{10,2},{18,10},{26,18},{... | collective-permute-start | bytes 786440 | tf_op jit(solution)/shard_map/ppermute | solution.py:19
  632.7 4.2 collective-permute-start.7
  661.8 10.2 copy-start.267
  663.2 7.7 collective-permute-start.8
  696.8 8.9 copy-start.147
  696.8 8.9 copy-start.268
  696.8 7.8 collective-permute-start.9
  730.5 8.9 copy-start.149
  730.5 8.9 copy-start.269
  730.5 7.8 collective-permute-start.10
  764.3 8.9 copy-start.151
  764.3 8.9 copy-start.270
  764.4 7.8 collective-permute-start.11
  798.4 108.8 %reduce-scatter.28.cloned.1.call-start = ((), (), s32[]{:S(2)}) async-start(), calls=%async_computation.16 | async-start | bytes 294912
  803.8 165.3 %reduce-scatter.30.cloned.1.call-start = ((), (), s32[]{:S(2)}) async-start(), calls=%async_computation.17 | async-start | bytes 294912
  804.9 229.9 %reduce-scatter.32.cloned.1.call-start = ((), (), s32[]{:S(2)}) async-start(), calls=%async_computation.18 | async-start | bytes 1179648
  806.4 295.4 %reduce-scatter.20.cloned.1.call-start = ((), (), s32[]{:S(2)}) async-start(), calls=%async_computation.12 | async-start | bytes 1179648 | tf_op jit(solution)/shard_map/reduce_scatter | solution.py:325
  809.3 358.9 %reduce-scatter.26.cloned.1.call-start = ((), (), s32[]{:S(2)}) async-start(), calls=%async_computation.15 | async-start | bytes 1179648 | tf_op jit(solution)/shard_map/reduce_scatter | solution.py:328
  818.4 22.1 %copy-start.155 = (bf16[128,512]{1,0:T(8,128)(2,1)S(1)}, bf16[128,512]{1,0:T(8,128)(2,1)}, u32[]{:S(2)}) copy-start(bf16[128,512]{1,0:T(8,128)(2,1)} %param.25) | copy-start | bytes 393220
  818.4 22.1 %copy-start.221 = (pred[128]{0:T(512)(128)(4,1)S(1)}, pred[128]{0:T(512)(128)(4,1)}, u32[]{:S(2)}) copy-start(pred[128]{0:T(512)(128)(4,1)} %copy-done.220) | copy-start | bytes 388
  821.6 21.4 %copy-start.65 = (bf16[256,1536]{1,0:T(8,128)(2,1)S(1)}, bf16[256,1536]{1,0:T(8,128)(2,1)}, u32[]{:S(2)}) copy-start(bf16[256,1536]{1,0:T(8,128)(2,1)} %convert_element_type.736) | copy-start | bytes 2359300
  842.7 403.7 %reduce-scatter.18.cloned.1.call-start = ((), (), s32[]{:S(2)}) async-start(), calls=%async_computation.11 | async-start | bytes 3538944 | tf_op jit(solution)/shard_map/reduce_scatter | solution.py:324
  855.2 482.9 %reduce-scatter.22.cloned.1.call-start = ((), (), s32[]{:S(2)}) async-start(), calls=%async_computation.13 | async-start | bytes 4718592 | tf_op jit(solution)/shard_map/reduce_scatter | solution.py:326
  875.0 555.2 %reduce-scatter.24.cloned.1.call-start = ((), (), s32[]{:S(2)}) async-start(), calls=%async_computation.14 | async-start | bytes 4718592 | tf_op jit(solution)/shard_map/reduce_scatter | solution.py:327
  892.2 819.3 %reduce-scatter.16.cloned.1.call-start = ((), (), s32[]{:S(2)}) async-start(), calls=%async_computation.10 | async-start | bytes 18432000 | tf_op jit(solution)/shard_map/reduce_scatter | solution.py:318
  907.2 129.2 %copy-start.83 = (bf16[512,512]{1,0:T(8,128)(2,1)S(1)}, bf16[512,512]{1,0:T(8,128)(2,1)}, u32[]{:S(2)}) copy-start(bf16[512,512]{1,0:T(8,128)(2,1)} %param.24) | copy-start | bytes 1572868
  907.2 129.2 %copy-start.154 = (bf16[128,512]{1,0:T(8,128)(2,1)S(1)}, bf16[128,512]{1,0:T(8,128)(2,1)}, u32[]{:S(2)}) copy-start(bf16[128,512]{1,0:T(8,128)(2,1)} %get-tuple-element.66) | copy-start | bytes 393220
  907.2 129.2 %copy-start.224 = (f32[128]{0:T(128)S(1)}, f32[128]{0:T(128)}, u32[]{:S(2)}) copy-start(f32[128]{0:T(128)} %get-tuple-element.123) | copy-start | bytes 1540
  (244 other events, 808.7 us)
Sparse Core Ops, SparseCore 0:
  10.2 125.0 all-gather.1
  147.7 35.6 all-reduce.6
  798.5 41.8 all-reduce.4
  844.2 61.3 reduce-scatter.27
  908.7 60.2 reduce-scatter.29
  972.3 62.5 reduce-scatter.31
  1039.2 62.5 reduce-scatter.19
  1105.8 62.4 reduce-scatter.25
  1172.9 73.4 reduce-scatter.17
  1250.9 87.1 reduce-scatter.21
  1342.3 87.7 reduce-scatter.23
  1435.1 276.3 reduce-scatter.15
where the time goes:
time: 1730 us; the launch traced here: 1720 us
  waiting for transfers between devices  990 us (57%)
  local copies, waits for them, and re-layouts  283 us (16%)
  matrix products  270 us (16%)
  other arithmetic  132 us (8%)
  starting transfers between devices  23.9 us (1%)
  between operations  18.9 us (1%)
    reduce_scatter x1, waiting for transfers between devices, local(): lax.psum_scatter(partial_rows, 'dp', scatter_dimension=0, tiled=True)  281 us
    unnamed x15, waiting for transfers between devices  126 us
    all_gather x1, waiting for transfers between devices, local(): quarter = lax.all_gather(table, 'dp', axis=0, tiled=True)  121 us
    dynamic_slice x48, local copies, waits for them, and re-layouts, place_one(): previous = lax.dynamic_index_in_dim(buffer, slot_index, 0, keepdims=False)  92.2 us
    reduce_scatter x1, waiting for transfers between devices, local(): lax.psum_scatter(down_total[None], 'dp', scatter_dimension=1, tiled=True)  92.1 us
    reduce_scatter x1, waiting for transfers between devices, local(): lax.psum_scatter(up_total[None], 'dp', scatter_dimension=1, tiled=True)  91.7 us
    reduce_scatter x1, waiting for transfers between devices, local(): lax.psum_scatter(qkv_total[None], 'dp', scatter_dimension=1, tiled=True)  78.1 us
    reduce_scatter x1, waiting for transfers between devices, local(): lax.psum_scatter(grad_proj, 'dp', scatter_dimension=0, tiled=True)  66.5 us
  transfers between devices with their start and end apart: 24, of which 16 were waited for; matrix products, arithmetic and copies ran while one was open for 17% of the time, Pallas kernels for 0%

commit v1 on v0

v1 whole, which is shorter than its diff:
```python
import functools
import jax
import jax.numpy as jnp
from jax import lax
from jax.experimental import pallas as pl
from jax.experimental.pallas import tpu as pltpu
from jax.sharding import PartitionSpec as P

HEADS = 8
LANES = 128
EPSILON = 1e-05
MASKED = -1e30
ROOT_HALF = 0.7071067811865476
DENSITY_SCALE = 0.3989422804014327
MESH = pl.DeviceIdType.MESH
F32 = jnp.float32
BF16 = jnp.bfloat16
MICRO = 128
VMEM_BYTES = 60 * 2**20


def dot_nn(left, right):
    return lax.dot_general(left, right, (((1,), (0,)), ((), ())), preferred_element_type=F32)


def dot_nt(left, right):
    return lax.dot_general(left, right, (((1,), (1,)), ((), ())), preferred_element_type=F32)


def dot_tn(left, right):
    return lax.dot_general(left, right, (((0,), (0,)), ((), ())), preferred_element_type=F32)


def statistics(values):
    centered = values - jnp.mean(values, axis=-1, keepdims=True)
    inverse = lax.rsqrt(jnp.mean(centered * centered, axis=-1, keepdims=True) + EPSILON)
    return centered * inverse, inverse


def norm_backward(weighted, normed, inverse):
    return inverse * (
        weighted
        - jnp.mean(weighted, axis=-1, keepdims=True)
        - normed * jnp.mean(weighted * normed, axis=-1, keepdims=True)
    )


def column_sum(values):
    return jnp.sum(values, axis=0, keepdims=True)


def entry_masks():
    lane = lax.broadcasted_iota(jnp.int32, (8, LANES), 1) // 8
    return [lane == e for e in range(LANES // 8)]


def compress(tall, masks):
    tall = tall.reshape(2, LANES // 8, 8, LANES)
    kept = []
    for h in range(2):
        one = tall[h, 0]
        for e in range(1, LANES // 8):
            one = jnp.where(masks[e], tall[h, e], one)
        kept.append(one)
    return kept


def expand(flat, masks):
    zero = jnp.zeros_like(flat)
    return jnp.concatenate([jnp.where(mask, flat, zero) for mask in masks], axis=0).astype(BF16)


def half_masks():
    lane = lax.broadcasted_iota(jnp.int32, (1, LANES), 1)
    low = jnp.where(lane < LANES // 2, 1.0, 0.0)
    return low.astype(BF16), (1.0 - low).astype(BF16)


def by_head(pair, halves):
    return jnp.concatenate([pair * halves[0], pair * halves[1]], axis=0)


def head_mask(count_row):
    return lax.broadcasted_iota(jnp.int32, (8, LANES), 0) < count_row


def pool_matrix(count_row):
    lane = lax.broadcasted_iota(jnp.int32, (LANES // 8, LANES), 1)
    entry = lax.broadcasted_iota(jnp.int32, (LANES // 8, LANES), 0)
    return jnp.where((lane // 8 == entry) & (lane % 8 < count_row), 1.0, 0.0)


def trunk_kernel(
    micros, width, hidden,
    x0, counts, pool_grad, gains, shifts, up_bias, w_qkv, w_out, w_up, w_down,
    a_out, dqkv_out, att_out, dbr_out, h_out, dpre_out, act_out, dy_out, dx_out, pooled_out, vec_out, upb_out,
    x_in, x_mid, resid, prob, y_out, dy_in,
    f_send, f_recv, b_send, b_recv,
):
    section = lax.axis_index("section")
    column = lax.axis_index("dp")
    stage = section // 2
    other = (lax.rem(section + 2, 4), column)
    blocks = MICRO // LANES
    score_scale = (width // HEADS) ** (-0.5)
    tiles = hidden // width

    barrier = pltpu.get_barrier_semaphore()
    pl.semaphore_signal(barrier, inc=1, device_id=other, device_id_type=MESH)
    pl.semaphore_wait(barrier, 1)

    def rows_of(m):
        return pl.ds(pl.multiple_of(m * MICRO, MICRO), MICRO)

    def forward_copy(m):
        return pltpu.make_async_remote_copy(
            y_out.at[rows_of(m)], x_in.at[rows_of(m)], f_send.at[m], f_recv.at[m],
            device_id=other, device_id_type=MESH)

    def backward_copy(m):
        return pltpu.make_async_remote_copy(
            y_out.at[rows_of(m)], dy_in.at[rows_of(m)], b_send.at[m], b_recv.at[m],
            device_id=other, device_id_type=MESH)

    def count_row(m, b):
        return counts[pl.ds(m * blocks + b, 1), :]

    vec_out[...] = jnp.zeros_like(vec_out)
    upb_out[...] = jnp.zeros_like(upb_out)

    def layer_forward(layer, m, x):
        rows = rows_of(m)
        masks, halves = entry_masks(), half_masks()
        xf = x.astype(F32)
        normed, _ = statistics(xf)
        a = (normed * gains[layer, pl.ds(0, 1), :] + shifts[layer, pl.ds(0, 1), :]).astype(BF16)
        a_out[layer, rows, :] = a
        for t in range(3):
            cols = slice(t * width, (t + 1) * width)
            dqkv_out[layer, rows, cols] = dot_nn(a, w_qkv[layer, :, cols]).astype(BF16)
        for b in range(blocks):
            block = pl.ds(pl.multiple_of(m * MICRO + b * LANES, LANES), LANES)
            keys_on = head_mask(count_row(m, b))
            for pair in range(HEADS // 2):
                cols = slice(pair * LANES, (pair + 1) * LANES)
                q = dqkv_out[layer, block, cols]
                k = dqkv_out[layer, block, slice(width + pair * LANES, width + (pair + 1) * LANES)]
                v = dqkv_out[layer, block, slice(2 * width + pair * LANES, 2 * width + (pair + 1) * LANES)]
                flats = compress(dot_nt(by_head(k, halves), q), masks)
                wide = []
                for h in range(2):
                    s = jnp.where(keys_on, flats[h] * score_scale, MASKED)
                    e = jnp.exp(s - jnp.max(s, axis=0, keepdims=True))
                    p = e / jnp.sum(e, axis=0, keepdims=True)
                    prob[layer, m * blocks + b, pl.ds((2 * pair + h) * 8, 8), :] = p
                    wide.append(expand(p, masks))
                mixed = dot_tn(jnp.concatenate(wide, axis=0), by_head(v, halves))
                att_out[layer, block, cols] = mixed.astype(BF16)
        res = xf + dot_nn(att_out[layer, rows, :], w_out[layer]) + shifts[layer, pl.ds(1, 1), :]
        resid[layer, rows, :] = res
        normed_two, _ = statistics(res)
        h_in = (normed_two * gains[layer, pl.ds(1, 1), :] + shifts[layer, pl.ds(2, 1), :]).astype(BF16)
        h_out[layer, rows, :] = h_in
        total = res + shifts[layer, pl.ds(3, 1), :]
        for t in range(tiles):
            cols = slice(t * width, (t + 1) * width)
            pre = dot_nn(h_in, w_up[layer, :, cols]) + up_bias[layer, :, cols]
            dpre_out[layer, rows, cols] = pre.astype(BF16)
            act = (pre * (0.5 * (1.0 + lax.erf(pre * ROOT_HALF)))).astype(BF16)
            total = total + dot_nn(act, w_down[layer, cols, :])
        return total.astype(BF16)

    def layer_backward(layer, m, dy):
        rows = rows_of(m)
        masks, halves = entry_masks(), half_masks()
        dyf = dy.astype(F32)
        vec_out[layer, pl.ds(5, 1), :] += column_sum(dyf)
        d_hidden = jnp.zeros((MICRO, width), F32)
        for t in range(tiles):
            cols = slice(t * width, (t + 1) * width)
            d_act = dot_nt(dy, w_down[layer, cols, :])
            pre = dpre_out[layer, rows, cols].astype(F32)
            phi = 0.5 * (1.0 + lax.erf(pre * ROOT_HALF))
            density = jnp.exp(-0.5 * pre * pre) * DENSITY_SCALE
            act_out[layer, rows, cols] = (pre * phi).astype(BF16)
            d_pre = (d_act * (phi + pre * density)).astype(BF16)
            dpre_out[layer, rows, cols] = d_pre
            upb_out[layer, :, cols] += column_sum(d_pre.astype(F32))
            d_hidden = d_hidden + dot_nt(d_pre, w_up[layer, :, cols])
        normed_two, inverse_two = statistics(resid[layer, rows, :])
        vec_out[layer, pl.ds(1, 1), :] += column_sum(d_hidden * normed_two)
        vec_out[layer, pl.ds(4, 1), :] += column_sum(d_hidden)
        d_resid = dyf + norm_backward(d_hidden * gains[layer, pl.ds(1, 1), :], normed_two, inverse_two)
        d_branch = d_resid.astype(BF16)
        dbr_out[layer, rows, :] = d_branch
        vec_out[layer, pl.ds(3, 1), :] += column_sum(d_branch.astype(F32))
        d_att = dot_nt(d_branch, w_out[layer]).astype(BF16)
        for b in range(blocks):
            block = pl.ds(pl.multiple_of(m * MICRO + b * LANES, LANES), LANES)
            for pair in range(HEADS // 2):
                c_q = slice(pair * LANES, (pair + 1) * LANES)
                c_k = slice(width + pair * LANES, width + (pair + 1) * LANES)
                c_v = slice(2 * width + pair * LANES, 2 * width + (pair + 1) * LANES)
                q = dqkv_out[layer, block, c_q]
                k = dqkv_out[layer, block, c_k]
                v = dqkv_out[layer, block, c_v]
                da = d_att[b * LANES:(b + 1) * LANES, c_q]
                flats = compress(dot_nt(by_head(v, halves), da), masks)
                wide_p, wide_s = [], []
                for h in range(2):
                    p = prob[layer, m * blocks + b, pl.ds((2 * pair + h) * 8, 8), :]
                    ds = p * (flats[h] - jnp.sum(flats[h] * p, axis=0, keepdims=True))
                    wide_p.append(expand(p, masks))
                    wide_s.append(expand(ds, masks))
                d_v = dot_nn(jnp.concatenate(wide_p, axis=1), by_head(da, halves))
                d_k = dot_nn(jnp.concatenate(wide_s, axis=1), by_head(q, halves)) * score_scale
                d_q = dot_tn(jnp.concatenate(wide_s, axis=0), by_head(k, halves)) * score_scale
                dqkv_out[layer, block, c_q] = d_q.astype(BF16)
                dqkv_out[layer, block, c_k] = d_k.astype(BF16)
                dqkv_out[layer, block, c_v] = d_v.astype(BF16)
        d_a = jnp.zeros((MICRO, width), F32)
        for t in range(3):
            cols = slice(t * width, (t + 1) * width)
            d_a = d_a + dot_nt(dqkv_out[layer, rows, cols], w_qkv[layer, :, cols])
        x = jnp.where(layer == 0, x_in[rows, :], x_mid[rows, :])
        normed, inverse = statistics(x.astype(F32))
        vec_out[layer, pl.ds(0, 1), :] += column_sum(d_a * normed)
        vec_out[layer, pl.ds(2, 1), :] += column_sum(d_a)
        dx = d_resid + norm_backward(d_a * gains[layer, pl.ds(0, 1), :], normed, inverse)
        return dx.astype(BF16)

    @pl.when(stage == 0)
    def _():
        x_in[...] = x0[...]

    def forward_step(m, carry):
        rows = rows_of(m)

        @pl.when(stage == 1)
        def _():
            forward_copy(m).wait_recv()

        x = lax.fori_loop(0, 2, lambda layer, x: forward_layer(layer, m, x), x_in[rows, :])
        y_out[rows, :] = x

        @pl.when(stage == 0)
        def _():
            forward_copy(m).start()

        @pl.when(stage == 1)
        def _():
            for b in range(blocks):
                matrix = pool_matrix(count_row(m, b))
                summed = dot_nn(matrix.astype(BF16), x[b * LANES:(b + 1) * LANES, :])
                mean = summed / jnp.sum(matrix, axis=1, keepdims=True)
                entries = pl.ds(pl.multiple_of((m * blocks + b) * (LANES // 8), LANES // 8), LANES // 8)
                pooled_out[entries, :] = mean.astype(BF16)
        return carry

    def forward_layer(layer, m, x):
        @pl.when(layer == 1)
        def _():
            x_mid[rows_of(m), :] = x

        return layer_forward(layer, m, x)

    lax.fori_loop(0, micros, forward_step, 0)

    @pl.when(stage == 0)
    def _():
        for m in range(micros):
            forward_copy(m).wait_send()

    def backward_step(m, carry):
        rows = rows_of(m)

        @pl.when(stage == 0)
        def _():
            backward_copy(m).wait_recv()
            dy_out[1, rows, :] = dy_in[rows, :]

        @pl.when(stage == 1)
        def _():
            for b in range(blocks):
                matrix = pool_matrix(count_row(m, b))
                entries = pl.ds(pl.multiple_of((m * blocks + b) * (LANES // 8), LANES // 8), LANES // 8)
                share = (pool_grad[entries, :] / jnp.sum(matrix, axis=1, keepdims=True)).astype(BF16)
                block = pl.ds(pl.multiple_of(m * MICRO + b * LANES, LANES), LANES)
                dy_out[1, block, :] = dot_tn(matrix.astype(BF16), share).astype(BF16)

        def step(i, dy):
            layer = 1 - i

            @pl.when(i == 1)
            def _():
                dy_out[0, rows, :] = dy

            return layer_backward(layer, m, dy)

        dx = lax.fori_loop(0, 2, step, dy_out[1, rows, :])
        dx_out[rows, :] = dx

        @pl.when(stage == 1)
        def _():
            y_out[rows, :] = dx
            backward_copy(m).start()
        return carry

    lax.fori_loop(0, micros, backward_step, 0)

    @pl.when(stage == 1)
    def _():
        for m in range(micros):
            backward_copy(m).wait_send()


def trunk(x0, counts, pool_grad, gains, shifts, up_bias, w_qkv, w_out, w_up, w_down):
    rows, width = x0.shape
    hidden = w_up.shape[2]
    micros = rows // MICRO
    vmem = pl.BlockSpec(memory_space=pltpu.VMEM)
    shape = jax.ShapeDtypeStruct
    outs = [
        shape((2, rows, width), BF16), shape((2, rows, 3 * width), BF16), shape((2, rows, width), BF16),
        shape((2, rows, width), BF16), shape((2, rows, width), BF16), shape((2, rows, hidden), BF16),
        shape((2, rows, hidden), BF16), shape((2, rows, width), BF16), shape((rows, width), BF16),
        shape((rows // 8, width), BF16), shape((2, 8, width), F32), shape((2, 1, hidden), F32),
    ]
    return pl.pallas_call(
        functools.partial(trunk_kernel, micros, width, hidden),
        out_shape=outs,
        in_specs=[vmem] * 10,
        out_specs=[vmem] * len(outs),
        scratch_shapes=[
            pltpu.VMEM((rows, width), BF16), pltpu.VMEM((rows, width), BF16), pltpu.VMEM((2, rows, width), F32),
            pltpu.VMEM((2, rows // LANES, 8 * HEADS, LANES), F32), pltpu.VMEM((rows, width), BF16),
            pltpu.VMEM((rows, width), BF16),
        ] + [pltpu.SemaphoreType.DMA((micros,))] * 4,
        compiler_params=pltpu.CompilerParams(collective_id=1, has_side_effects=True, vmem_limit_bytes=VMEM_BYTES),
    )(x0, counts, pool_grad, gains, shifts, up_bias, w_qkv, w_out, w_up, w_down)


def contract_rows(left, right):
    return lax.dot_general(left, right, (((0,), (0,)), ((), ())), preferred_element_type=F32)


def local(table, piece_ids, piece_counts, vocab_size, norm_gain, shift_bias, up_bias, qkv_weight, out_weight,
          up_weight, down_weight, proj_weight, embed_cotangent):
    section = lax.axis_index("section")
    column = lax.axis_index("dp")
    columns = lax.axis_size("dp")
    core = lax.rem(section, 2)
    entries, pieces = piece_ids.shape
    width = qkv_weight.shape[1]
    half = entries // 2
    positions = column * entries + jnp.arange(entries, dtype=jnp.int32)
    live = positions < vocab_size[0]
    flat_ids = piece_ids.reshape(entries * pieces)
    quarter = lax.all_gather(table, "dp", axis=0, tiled=True)
    span = quarter.shape[0]
    local_ids = flat_ids - section * span
    inside = (local_ids >= 0) & (local_ids < span)
    safe_ids = jnp.clip(local_ids, 0, span - 1)
    picked = jnp.where(inside[:, None], jnp.take(quarter, safe_ids, axis=0), 0)
    embedded = lax.psum(picked, "section")
    x0 = lax.dynamic_slice_in_dim(embedded, core * half * pieces, half * pieces, 0)
    cotangent = jnp.where(live[:, None], embed_cotangent, jnp.zeros_like(embed_cotangent))
    pool_grad = lax.psum(dot_nt(cotangent, proj_weight).astype(BF16), "section").astype(F32)
    pool_half = lax.dynamic_slice_in_dim(pool_grad, core * half, half, 0)
    my_counts = lax.dynamic_slice_in_dim(piece_counts, core * half, half, 0)
    count_rows = jnp.repeat(my_counts, pieces).reshape(-1, LANES)

    def both(value):
        swapped = lax.ppermute(value, "section", [(0, 1), (1, 0), (2, 3), (3, 2)])
        return jnp.where(core == 0, jnp.concatenate([value, swapped]), jnp.concatenate([swapped, value]))

    gains, shifts, bias = both(norm_gain), both(shift_bias), both(up_bias)[:, None, :]
    w_qkv, w_out, w_up, w_down = both(qkv_weight), both(out_weight), both(up_weight), both(down_weight)
    a, dqkv, att, dbr, h, dpre, act, dy, dx, pooled, vec, upb = trunk(
        x0, count_rows, pool_half, gains, shifts, bias, w_qkv, w_out, w_up, w_down)
    whole_pooled = lax.all_gather(pooled, "section", axis=0, tiled=True)[2 * half:]
    embeddings = jnp.dot(whole_pooled, proj_weight, preferred_element_type=F32) * live[:, None].astype(F32)
    grad_proj = contract_rows(whole_pooled, cotangent)

    def mine(value):
        own = lax.dynamic_index_in_dim(value, core, 0)
        gone = lax.dynamic_index_in_dim(value, 1 - core, 0)
        return own + lax.ppermute(gone, "section", [(0, 1), (1, 0), (2, 3), (3, 2)])

    batched = lambda left, right: lax.dot_general(
        left, right, (((1,), (1,)), ((0,), (0,))), preferred_element_type=F32)
    g_qkv, g_out, g_up, g_down = mine(batched(a, dqkv)), mine(batched(att, dbr)), mine(batched(h, dpre)), mine(batched(act, dy))
    vec, upb = mine(vec), mine(upb)
    scatter = lambda value, axis: lax.psum_scatter(value, "dp", scatter_dimension=axis, tiled=True)
    low = lambda value, axis: scatter(value.astype(BF16), axis).astype(F32)
    spread = jnp.where(section < 2, dx, jnp.zeros_like(dx))
    spread = lax.all_gather(spread, "section", axis=0, tiled=True)[: 2 * half * pieces].astype(F32)
    partial = jax.ops.segment_sum(jnp.where(inside[:, None], spread, 0.0), safe_ids, num_segments=span)
    table_grad = scatter(partial, 0)
    return (
        embeddings, table_grad, scatter(vec[:, 0:2], 2), scatter(vec[:, 2:6], 2), scatter(upb[:, 0], 1),
        low(g_qkv, 1), low(g_out, 1), low(g_up, 1), low(g_down, 1), low(grad_proj, 0),
    )


def solution(mesh):
    return jax.shard_map(
        local,
        mesh=mesh,
        in_specs=(
            P(("section", "dp"), None), P("dp", None), P("dp"), P(), P("section", None, None),
            P("section", None, None), P("section", None), P("section", None, None), P("section", None, None),
            P("section", None, None), P("section", None, None), P(None, "section"), P("dp", "section"),
        ),
        out_specs=(
            P("dp", "section"), P(("section", "dp"), None), P("section", None, "dp"), P("section", None, "dp"),
            P("section", "dp"), P("section", "dp", None), P("section", "dp", None), P("section", "dp", None),
            P("section", "dp", None), P("dp", "section"),
        ),
        check_vma=False,
    )
```

time: 1730 us -> 1110 us (0.64)
  matrix products: 270 us -> 17.8 us
  local copies, waits for them, and re-layouts: 283 us -> 34.6 us
  waiting for transfers between devices: 990 us -> 883 us
  Pallas kernels: 0 us -> 84.1 us
  other arithmetic: 132 us -> 67.7 us
  starting transfers between devices: 23.9 us -> 4.47 us
    dot_general x93 -> x6, matrix products: 182 us -> 16.6 us  [the longest x4 13.8 us: local(): lax.dot_general(left, right, (((1,), (1,)), ((0,), (0,))), preferred_elem...]
    dynamic_slice x51 -> x8, local copies, waits for them, and re-layouts: 97.5 us -> 11.1 us  [the longest x6 8.48 us: mine(): gone = lax.dynamic_index_in_dim(value, 1 - core, 0)]
    pallas_call x0 -> x1, Pallas kernels: none -> 84.1 us  [trunk(): pl.pallas_call(functools.partial(trunk_kernel, micros, width, hidden), ou...]
    reduce_scatter x6, waiting for transfers between devices: 674 us -> 608 us  [local(): lax.psum_scatter(value, 'dp', scatter_dimension=axis, tiled=True)]
    dot_general x29 -> x1, matrix products: 66.5 us -> 1.14 us  [contract_rows(): lax.dot_general(left, right, (((0,), (0,)), ((), ())), preferred_element_...]
    dynamic_update_slice x57 -> x0, other arithmetic: 63.9 us -> none  [place_one(): lax.dynamic_update_index_in_dim(buffer, jnp.where(usable, fresh_value, pr...]
    reshape x21 -> x0, local copies, waits for them, and re-layouts: 55.6 us -> none  [the longest x7 21.6 us: layer_backward(): heads_split = joined.reshape(entry_count, pieces, 3, HEADS, head_size)]
    convert_element_type x27 -> x0, local copies, waits for them, and re-layouts: 41.8 us -> none  [the longest x7 23.8 us: layer_backward(): grad_joined.reshape(micro_rows, 3 * model_width).astype(jnp.bfloat16)]
  transfers between devices with their start and end apart: 24 -> 25, of which waited for: 16 -> 14; matrix products, arithmetic and copies ran while one was open for 17% -> 10% of each run, Pallas kernels for 0% -> 0%
where the time goes in v1:
time: 1110 us
  waiting for transfers between devices  883 us (80%)
  Pallas kernels  84.1 us (8%)
  other arithmetic  67.7 us (6%)
  local copies, waits for them, and re-layouts  34.6 us (3%)
  matrix products  17.8 us (2%)
  between operations  15.2 us (1%)
    reduce_scatter x6, waiting for transfers between devices, local(): lax.psum_scatter(value, 'dp', scatter_dimension=axis, tiled=True)  608 us
    unnamed x15, waiting for transfers between devices  135 us
    all_gather x1, waiting for transfers between devices, local(): quarter = lax.all_gather(table, 'dp', axis=0, tiled=True)  107 us
    pallas_call x1, Pallas kernels, trunk(): pl.pallas_call(functools.partial(trunk_kernel, micros, width, hidden), ou...  84.1 us
    convert_element_type x9, other arithmetic, local(): low = lambda value, axis: scatter(value.astype(BF16), axis).astype(F32)  26 us
    psum x1, waiting for transfers between devices, local(): embedded = lax.psum(picked, 'section')  25.2 us
  transfers between devices with their start and end apart: 25, of which 14 were waited for; matrix products, arithmetic and copies ran while one was open for 10% of the time, Pallas kernels for 0%

profile of v1, /device:TPU:0, one launch (start us, length us, event | category | flops | bytes accessed | tf_op | source)
XLA Modules:
  0.0 1112.7 jit_solution(8869714004623575565)
XLA Ops:
  7.2 0.7 all-gather.3.cloned.1.call-update
  8.0 0.5 collective-permute-start.5
  9.5 0.7 subtract_clamp_fusion
  11.2 1.9 convolution_convert_fusion.1
  13.1 0.7 compare_and_fusion.1
  14.0 0.7 dynamic_slice.52
  14.9 0.7 broadcast_in_dim.68.counts
  15.7 1.4 maximum_select_fusion.5.gains
  17.1 1.4 collective-permute-done.1
  18.9 1.4 maximum_select_fusion.4.shifts
  20.3 1.4 broadcast_select_fusion.4.up_bias
  21.7 2.5 maximum_select_fusion.3.w_out
  24.2 3.8 maximum_select_fusion.2.w_qkv
  28.0 107.4 %all-gather.3.cloned.1.call-done = bf16[8000,512]{1,0:T(8,128)(2,1)} async-done(((bf16[1000,512]{1,0:T(8,128)(2,1)}), bf16[8000,512]{1,0:T(8,128)(2,1)}) %all-gather.3.cloned.1.call-update) | async-done | bytes 8192016 | tf_op jit(solution)/shard_map/all_gather | solution.py:359
  135.3 8.4 gather_fusion
  143.7 1.6 select_select_fusion
  145.4 6.0 maximum_select_fusion.w_up
  151.4 4.5 maximum_select_fusion.1.w_down
  156.0 25.2 %all-reduce.3.cloned.1.call-done = (bf16[1024,512]{1,0:T(8,128)(2,1)}, bf16[128,512]{1,0:T(8,128)(2,1)}) async-done(((bf16[1024,512]{1,0:T(8,128)(2,1)}, bf16[128,512]{1,0:T(8,128)(2,1)}), (bf16[1024,512]{1,0:T(8,128)(2,1)}, bf16[128,512]{1,0:T(8,128)(2,1)})) %all-reduce.3.cloned.1.call-update) | async-done | bytes 1179664 | tf_op jit(solution)/shard_map/psum | solution.py:365
  181.2 1.5 dynamic-slice_convert_fusion.pool_grad
  182.7 1.9 constant_dynamic-slice_fusion.6.x0
  184.6 84.1 %shard_map.204 = (bf16[2,512,512]{2,1,0:T(8,128)(2,1)}, bf16[2,512,1536]{2,1,0:T(8,128)(2,1)}, bf16[2,512,512]{2,1,0:T(8,128)(2,1)}, bf16[2,512,512]{2,1,0:T(8,1...) custom-call(bf16[512,512]{1,0:T(8,128)(2,1)} %constant_dynamic-slice, ...), custom_call_target="tpu_custom_call" | custom-call | tf_op jit(solution)/shard_map/pallas_call | solution.py:329
  268.7 1.9 broadcast_select_fusion
  270.8 2.4 fusion.13
  273.3 1.0 constant_dynamic-slice_fusion.2
  274.4 1.9 fusion.12
  276.2 2.7 copy-done.3
  278.9 1.8 constant_dynamic-slice_fusion.3
  281.8 4.7 collective-permute-done.8
  286.5 1.4 copy.49
  288.0 0.9 copy.45
  288.9 5.8 all_gather.10
  294.7 0.9 copy.47
  295.7 1.1 convolution_convert_fusion
  296.9 4.9 fusion.15
  301.8 2.8 constant_dynamic-slice_fusion
  304.6 1.9 copy-done.2
  306.8 2.2 add_convert_fusion.3
  309.1 4.5 add_convert_fusion.2
  313.7 4.6 fusion.14
  318.3 2.8 constant_dynamic-slice_fusion.1
  321.1 1.7 copy-done.1
  323.0 5.6 add_convert_fusion
  328.7 1.6 collective-permute-done.11
  330.3 5.4 add_convert_fusion.1
  336.1 14.3 %scatter_custom_fusion = f32[8000,512]{1,0:T(8,128)} fusion(s32[1024]{0:T(1024)S(1)} %min.16, f32[]{:T(128)} %constant.86.clone.1, bf16[2048,512]{1,0:T(8,128)(2,1)} %all-gather.5.cloned.1.call-done, pred[1024]{0:T(1024)(128)(4,1)S(1)} %and.21), kind=kCustom, calls=%fused_computation.2 | custom fusion | flops 1572864 | bytes 17434624 | tf_op jit(solution)/shard_map/scatter-add | solution.py:398
  350.4 0.9 convolution_multiply_fusion
  351.4 8.8 reduce-scatter.32.cloned.1.call-done
  360.1 1.5 copy.50
  361.7 62.8 %reduce-scatter.28.cloned.1.call-done = f32[64,2]{1,0:T(8,128)} async-done(((f32[512,2]{1,0:T(8,128)}), f32[64,2]{1,0:T(8,128)}) %reduce-scatter.28.cloned.1.call-update) | async-done | bytes 528
  424.5 1.4 copy.46
  425.9 62.5 %reduce-scatter.30.cloned.1.call-done = f32[64,4]{1,0:T(8,128)} async-done(((f32[512,4]{1,0:T(8,128)}), f32[64,4]{1,0:T(8,128)}) %reduce-scatter.30.cloned.1.call-update) | async-done | bytes 1040
  488.3 1.4 copy.48
  489.7 63.3 %reduce-scatter.26.cloned.1.call-done = bf16[64,512]{1,0:T(8,128)(2,1)} async-done(((bf16[512,512]{1,0:T(8,128)(2,1)}), bf16[64,512]{1,0:T(8,128)(2,1)}) %reduce-scatter.26.cloned.1.call-update) | async-done | bytes 65552 | tf_op jit(solution)/shard_map/reduce_scatter | solution.py:394
  553.0 1.5 convert_element_type.62
  554.5 63.3 %reduce-scatter.20.cloned.1.call-done = bf16[1,64,512]{2,1,0:T(8,128)(2,1)} async-done(((bf16[1,512,512]{2,1,0:T(8,128)(2,1)}), bf16[1,64,512]{2,1,0:T(8,128)(2,1)}) %reduce-scatter.20.cloned.1.call-update) | async-done | bytes 65552 | tf_op jit(solution)/shard_map/reduce_scatter | solution.py:394
  617.8 1.5 convert_element_type.56
  619.3 66.2 %reduce-scatter.18.cloned.1.call-done = bf16[1,64,1536]{2,1,0:T(8,128)(2,1)} async-done(((bf16[1,512,1536]{2,1,0:T(8,128)(2,1)}), bf16[1,64,1536]{2,1,0:T(8,128)(2,1)}) %reduce-scatter.18.cloned.1.call-update) | async-done | bytes 196624 | tf_op jit(solution)/shard_map/reduce_scatter | solution.py:394
  685.5 1.7 convert_element_type.54
  687.2 68.2 %reduce-scatter.24.cloned.1.call-done = bf16[1,256,512]{2,1,0:T(8,128)(2,1)} async-done(((bf16[1,2048,512]{2,1,0:T(8,128)(2,1)}), bf16[1,256,512]{2,1,0:T(8,128)(2,1)}) %reduce-scatter.24.cloned.1.call-update) | async-done | bytes 262160 | tf_op jit(solution)/shard_map/reduce_scatter | solution.py:394
  755.4 1.8 convert_element_type.60
  757.3 68.5 %reduce-scatter.22.cloned.1.call-done = bf16[1,64,2048]{2,1,0:T(8,128)(2,1)} async-done(((bf16[1,512,2048]{2,1,0:T(8,128)(2,1)}), bf16[1,64,2048]{2,1,0:T(8,128)(2,1)}) %reduce-scatter.22.cloned.1.call-update) | async-done | bytes 262160 | tf_op jit(solution)/shard_map/reduce_scatter | solution.py:394
  825.7 1.8 convert_element_type.58
  827.5 278.3 %reduce-scatter.16.cloned.1.call-done = f32[1000,512]{1,0:T(8,128)} async-done(((f32[8000,512]{1,0:T(8,128)}), f32[1000,512]{1,0:T(8,128)}) %reduce-scatter.16.cloned.1.call-update) | async-done | bytes 2048016 | tf_op jit(solution)/shard_map/reduce_scatter | solution.py:394
  (86 shorter events, 5.0 us)
Async XLA Ops:
  7.2 4.0 copy-start
  7.2 17.0 %copy-start.7 = (bf16[1,512,1536]{2,1,0:T(8,128)(2,1)S(1)}, bf16[1,512,1536]{2,1,0:T(8,128)(2,1)}, u32[]{:S(2)}) copy-start(bf16[1,512,1536]{2,1,0:T(8,128)(2,1)} %param.20) | copy-start | bytes 4718596
  7.2 128.1 %all-gather.3.cloned.1.call-start = ((), (), s32[]{:S(2)}) async-start(), calls=%async_computation.9 | async-start | bytes 9216000 | tf_op jit(solution)/shard_map/all_gather | solution.py:359
  7.9 173.2 %all-reduce.3.cloned.1.call-start = ((), (), s32[]{:S(2)}) async-start(), calls=%async_computation.20 | async-start | bytes 2359296 | tf_op jit(solution)/shard_map/psum | solution.py:365
  8.0 137.4 %collective-permute-start.5 = (bf16[1,512,2048]{2,1,0:T(8,128)(2,1)}, bf16[1,512,2048]{2,1,0:T(8,128)(2,1)}, u32[]{:S(2)}, u32[]{:S(2)}) collective-permute-start(bf16[1,512,2048]{2,1,0:T(8,128)(2,1)} %param.22), channel_id=1, source_target_pairs={{0,8},{8,0},{16,24},{24,16},{1,9},{9,1},{17,25},{25,17},{2,10},{10... | collective-permute-start | bytes 6291464 | tf_op jit(solution)/shard_map/ppermute | solution.py:374
  8.5 142.9 %collective-permute-start.6 = (bf16[1,2048,512]{2,1,0:T(8,128)(2,1)}, bf16[1,2048,512]{2,1,0:T(8,128)(2,1)}, u32[]{:S(2)}, u32[]{:S(2)}) collective-permute-start(bf16[1,2048,512]{2,1,0:T(8,128)(2,1)} %param.23), channel_id=1, source_target_pairs={{0,8},{8,0},{16,24},{24,16},{1,9},{9,1},{17,25},{25,17},{2,10},{10... | collective-permute-start | bytes 6291464 | tf_op jit(solution)/shard_map/ppermute | solution.py:374
  8.6 15.6 %collective-permute-start.3 = (bf16[1,512,1536]{2,1,0:T(8,128)(2,1)}, bf16[1,512,1536]{2,1,0:T(8,128)(2,1)}, u32[]{:S(2)}, u32[]{:S(2)}) collective-permute-start(bf16[1,512,1536]{2,1,0:T(8,128)(2,1)} %param.20), channel_id=1, source_target_pairs={{0,8},{8,0},{16,24},{24,16},{1,9},{9,1},{17,25},{25,17},{2,10},{10... | collective-permute-start | bytes 4718600 | tf_op jit(solution)/shard_map/ppermute | solution.py:374
  9.0 12.7 %collective-permute-start.4 = (bf16[1,512,512]{2,1,0:T(8,128)(2,1)}, bf16[1,512,512]{2,1,0:T(8,128)(2,1)S(1)}, u32[]{:S(2)}, u32[]{:S(2)}) collective-permute-start(bf16[1,512,512]{2,1,0:T(8,128)(2,1)} %param.21), channel_id=1, source_target_pairs={{0,8},{8,0},{16,24},{24,16},{1,9},{9,1},{17,25},{25,17},{2,10},{10... | collective-permute-start | bytes 1572872 | tf_op jit(solution)/shard_map/ppermute | solution.py:374
  9.1 6.5 collective-permute-start
  15.6 2.9 collective-permute-start.1
  18.5 1.8 collective-permute-start.2
  145.3 6.1 copy-start.6
  145.4 190.7 %all-gather.5.cloned.1.call-start = ((), (), s32[]{:S(2)}) async-start(), calls=%async_computation.10 | async-start | bytes 2621440 | tf_op jit(solution)/shard_map/all_gather | solution.py:397
  270.6 89.5 %reduce-scatter.32.cloned.1.call-start = ((), (), s32[]{:S(2)}) async-start(), calls=%async_computation.19 | async-start | bytes 1179648
  270.8 3.5 copy-start.4
  270.8 3.5 copy-start.8
  274.3 32.5 %collective-permute-start.10 = (f32[1,512,512]{2,1,0:T(8,128)}, f32[1,512,512]{2,1,0:T(8,128)}, u32[]{:S(2)}, u32[]{:S(2)}) collective-permute-start(f32[1,512,512]{2,1,0:T(8,128)} %constant_dynamic-slice_fusion.2), channel_id=1, source_target_pairs={{0,8},{8,0},{16,24},{24,16},{1,9},{9,1},{17,25},{25,17},{2,10},{10... | collective-permute-start | bytes 3145736 | tf_op jit(solution)/shard_map/ppermute | solution.py:388
  276.2 2.7 copy-start.3
  278.9 2.4 copy-start.12
  278.9 2.4 copy-start.11
  278.9 10.0 copy-start.10
  278.9 16.7 %copy-start.9 = (bf16[128,512]{1,0:T(8,128)(2,1)S(1)}, bf16[128,512]{1,0:T(8,128)(2,1)}, u32[]{:S(2)}) copy-start(bf16[128,512]{1,0:T(8,128)(2,1)} %param.25) | copy-start | bytes 393220
  280.8 28.3 %collective-permute-start.9 = (f32[1,512,1536]{2,1,0:T(8,128)}, f32[1,512,1536]{2,1,0:T(8,128)}, u32[]{:S(2)}, u32[]{:S(2)}) collective-permute-start(f32[1,512,1536]{2,1,0:T(8,128)} %constant_dynamic-slice_fusion.3), channel_id=1, source_target_pairs={{0,8},{8,0},{16,24},{24,16},{1,9},{9,1},{17,25},{25,17},{2,10},{10... | collective-permute-start | bytes 9437192 | tf_op jit(solution)/shard_map/ppermute | solution.py:388
  281.3 5.2 collective-permute-start.8
  281.4 6.6 collective-permute-start.7
  287.9 136.6 %reduce-scatter.28.cloned.1.call-start = ((), (), s32[]{:S(2)}) async-start(), calls=%async_computation.17 | async-start | bytes 294912
  288.9 199.5 %reduce-scatter.30.cloned.1.call-start = ((), (), s32[]{:S(2)}) async-start(), calls=%async_computation.18 | async-start | bytes 294912
  295.6 257.4 %reduce-scatter.26.cloned.1.call-start = ((), (), s32[]{:S(2)}) async-start(), calls=%async_computation.16 | async-start | bytes 589824 | tf_op jit(solution)/shard_map/reduce_scatter | solution.py:394
  296.8 321.0 %reduce-scatter.20.cloned.1.call-start = ((), (), s32[]{:S(2)}) async-start(), calls=%async_computation.13 | async-start | bytes 589824 | tf_op jit(solution)/shard_map/reduce_scatter | solution.py:394
  301.8 4.7 copy-start.2
  306.5 16.6 %collective-permute-start.12 = (f32[1,2048,512]{2,1,0:T(8,128)}, f32[1,2048,512]{2,1,0:T(8,128)}, u32[]{:S(2)}, u32[]{:S(2)}) collective-permute-start(f32[1,2048,512]{2,1,0:T(8,128)} %constant_dynamic-slice_fusion), channel_id=1, source_target_pairs={{0,8},{8,0},{16,24},{24,16},{1,9},{9,1},{17,25},{25,17},{2,10},{10... | collective-permute-start | bytes 12582920 | tf_op jit(solution)/shard_map/ppermute | solution.py:388
  309.0 4.7 copy-start.5
  309.0 376.5 %reduce-scatter.18.cloned.1.call-start = ((), (), s32[]{:S(2)}) async-start(), calls=%async_computation.12 | async-start | bytes 1769472 | tf_op jit(solution)/shard_map/reduce_scatter | solution.py:394
  313.6 441.8 %reduce-scatter.24.cloned.1.call-start = ((), (), s32[]{:S(2)}) async-start(), calls=%async_computation.15 | async-start | bytes 2359296 | tf_op jit(solution)/shard_map/reduce_scatter | solution.py:394
  318.3 4.5 copy-start.1
  322.8 7.5 collective-permute-start.11
  328.7 497.1 %reduce-scatter.22.cloned.1.call-start = ((), (), s32[]{:S(2)}) async-start(), calls=%async_computation.14 | async-start | bytes 2359296 | tf_op jit(solution)/shard_map/reduce_scatter | solution.py:394
  335.8 770.0 %reduce-scatter.16.cloned.1.call-start = ((), (), s32[]{:S(2)}) async-start(), calls=%async_computation.11 | async-start | bytes 18432000 | tf_op jit(solution)/shard_map/reduce_scatter | solution.py:394
Sparse Core Ops, SparseCore 0:
  10.2 125.0 all-gather.2
  145.5 35.6 all-reduce.2
  270.7 22.5 all-gather.4
  296.6 63.4 reduce-scatter.31
  364.2 60.2 reduce-scatter.27
  428.0 60.2 reduce-scatter.29
  492.0 60.9 reduce-scatter.25
  556.9 60.8 reduce-scatter.19
  621.6 63.8 reduce-scatter.17
  688.9 66.5 reduce-scatter.23
  759.0 66.7 reduce-scatter.21
  830.2 275.6 reduce-scatter.15

commit v2 on v1

--- a/solution.py
+++ b/solution.py
@@ -92,10 +92,17 @@
 
 def trunk_kernel(
     micros, width, hidden,
-    x0, counts, pool_grad, gains, shifts, up_bias, w_qkv, w_out, w_up, w_down,
+    x0, counts, pool_grad, *refs
+):
+    own, theirs, refs = refs[:7], refs[7:14], refs[14:]
+    trunk_body(micros, width, hidden, x0, counts, pool_grad, own, theirs, *refs)
+
+
+def trunk_body(
+    micros, width, hidden, x0, counts, pool_grad, own, theirs,
     a_out, dqkv_out, att_out, dbr_out, h_out, dpre_out, act_out, dy_out, dx_out, pooled_out, vec_out, upb_out,
-    x_in, x_mid, resid, prob, y_out, dy_in,
-    f_send, f_recv, b_send, b_recv,
+    gains, shifts, up_bias, w_qkv, w_out, w_up, w_down, x_in, x_mid, resid, prob, y_out, dy_in,
+    f_send, f_recv, b_send, b_recv, p_sem,
 ):
     section = lax.axis_index("section")
     column = lax.axis_index("dp")
@@ -105,6 +112,25 @@
     score_scale = (width // HEADS) ** (-0.5)
     tiles = hidden // width
 
+    core = lax.rem(section, 2)
+    params = (gains, shifts, up_bias, w_qkv, w_out, w_up, w_down)
+
+    def fetch(i, source, layer):
+        return pltpu.make_async_copy(source[i].at[0], params[i].at[layer], p_sem.at[i, layer])
+
+    for first in range(2):
+        @pl.when(core == first)
+        def _(first=first):
+            for layer in range(2):
+                for i in range(len(params)):
+                    fetch(i, own if layer == first else theirs, layer).start()
+
+    def need(m, layer, *indices):
+        @pl.when(m == 0)
+        def _():
+            for i in indices:
+                fetch(i, own, layer).wait()
+
     barrier = pltpu.get_barrier_semaphore()
     pl.semaphore_signal(barrier, inc=1, device_id=other, device_id_type=MESH)
     pl.semaphore_wait(barrier, 1)
@@ -133,6 +159,7 @@
         masks, halves = entry_masks(), half_masks()
         xf = x.astype(F32)
         normed, _ = statistics(xf)
+        need(m, layer, 0, 1, 3)
         a = (normed * gains[layer, pl.ds(0, 1), :] + shifts[layer, pl.ds(0, 1), :]).astype(BF16)
         a_out[layer, rows, :] = a
         for t in range(3):
@@ -156,11 +183,13 @@
                     wide.append(expand(p, masks))
                 mixed = dot_tn(jnp.concatenate(wide, axis=0), by_head(v, halves))
                 att_out[layer, block, cols] = mixed.astype(BF16)
+        need(m, layer, 4)
         res = xf + dot_nn(att_out[layer, rows, :], w_out[layer]) + shifts[layer, pl.ds(1, 1), :]
         resid[layer, rows, :] = res
         normed_two, _ = statistics(res)
         h_in = (normed_two * gains[layer, pl.ds(1, 1), :] + shifts[layer, pl.ds(2, 1), :]).astype(BF16)
         h_out[layer, rows, :] = h_in
+        need(m, layer, 2, 5, 6)
         total = res + shifts[layer, pl.ds(3, 1), :]
         for t in range(tiles):
             cols = slice(t * width, (t + 1) * width)
@@ -314,9 +343,9 @@
             backward_copy(m).wait_send()
 
 
-def trunk(x0, counts, pool_grad, gains, shifts, up_bias, w_qkv, w_out, w_up, w_down):
+def trunk(x0, counts, pool_grad, own, theirs):
     rows, width = x0.shape
-    hidden = w_up.shape[2]
+    hidden = own[5].shape[2]
     micros = rows // MICRO
     vmem = pl.BlockSpec(memory_space=pltpu.VMEM)
     shape = jax.ShapeDtypeStruct
@@ -329,78 +358,758 @@
     return pl.pallas_call(
         functools.partial(trunk_kernel, micros, width, hidden),
         out_shape=outs,
-        in_specs=[vmem] * 10,
+        in_specs=[vmem] * 3 + [pl.BlockSpec(memory_space=pl.ANY)] * 14,
         out_specs=[vmem] * len(outs),
-        scratch_shapes=[
+        scratch_shapes=[pltpu.VMEM((2,) + p.shape[1:], p.dtype) for p in own] + [
             pltpu.VMEM((rows, width), BF16), pltpu.VMEM((rows, width), BF16), pltpu.VMEM((2, rows, width), F32),
             pltpu.VMEM((2, rows // LANES, 8 * HEADS, LANES), F32), pltpu.VMEM((rows, width), BF16),
             pltpu.VMEM((rows, width), BF16),
-        ] + [pltpu.SemaphoreType.DMA((micros,))] * 4,
+        ] + [pltpu.SemaphoreType.DMA((micros,))] * 4 + [pltpu.SemaphoreType.DMA((7, 2))],
         compiler_params=pltpu.CompilerParams(collective_id=1, has_side_effects=True, vmem_limit_bytes=VMEM_BYTES),
-    )(x0, counts, pool_grad, gains, shifts, up_bias, w_qkv, w_out, w_up, w_down)
-
-
-def contract_rows(left, right):
-    return lax.dot_general(left, right, (((0,), (0,)), ((), ())), preferred_element_type=F32)
+    )(x0, counts, pool_grad, *own, *theirs)
+
+
+def capacity_of(slots, owners):
+    return max(16, -(-2 * slots // owners // 16) * 16)
+
+
+def ones_where(condition):
+    return jnp.where(condition, 1.0, 0.0).astype(BF16)
+
+
+def iota(shape, axis):
+    return lax.broadcasted_iota(jnp.int32, shape, axis)
+
+
+def positions(used, chunks):
+    rows = LANES
+    through = ones_where(iota((LANES, LANES), 0) <= iota((LANES, LANES), 1))
+    above = ones_where(
+        (iota((rows, rows), 0) // 8 == iota((rows, rows), 1) // 8) & (iota((rows, rows), 1) < iota((rows, rows), 0)))
+    every = jnp.ones((LANES, LANES), BF16)
+    out = []
+    for chunk in range(chunks):
+        part = used[chunk * rows:(chunk + 1) * rows, :].astype(BF16)
+        before = dot_nn(dot_nn(above, part).astype(BF16), every)
+        out.append(dot_nn(part, through) + before)
+    return jnp.concatenate(out, axis=0)
+
+
+def in_round(place, used, turn, capacity):
+    place = place - (turn * capacity).astype(F32)
+    return jnp.where((used > 0) & (place >= 1) & (place <= capacity), place, 0.0)
+
+
+def owner_plan(ids_all, picks, used_rows, base, span, turn, capacity, lists):
+    slots = ids_all.shape[2]
+    blocks = -(-span // LANES)
+
+    def count(d, carry):
+        rel = ids_all[d // 2, pl.ds(lax.rem(d, 2), 1), :] - base
+        high = jnp.where((rel >= 0) & (rel < span), rel >> 7, -1)
+        counts = dot_nt(ones_where(iota((8, slots), 0) == high), ones_where(iota((LANES, slots), 0) == (rel & 127)))
+        used_rows[pl.ds(pl.multiple_of(d * 8, 8), 8), :] = jnp.where(counts > 0, 1.0, 0.0)
+        return carry
+
+    lax.fori_loop(0, lists, count, 0)
+    used = used_rows[pl.ds(0, lists * 8), :]
+    used_rows[pl.ds(0, lists * 8), :] = in_round(positions(used, lists * 8 // LANES), used, turn, capacity)
+
+    def spread(d, carry):
+        place = used_rows[pl.ds(pl.multiple_of(d * 8, 8), 8), :]
+        wanted = (iota((capacity, LANES), 0) + 1).astype(F32)
+        for block in range(blocks):
+            picks[pl.ds(pl.multiple_of(d * capacity, 16), capacity), block * LANES:(block + 1) * LANES] = ones_where(
+                place[block:block + 1, :] == wanted)
+        return carry
+
+    lax.fori_loop(0, lists, spread, 0)
+
+
+def slot_codes(ids_row, span):
+    value = ids_row.astype(F32)
+    owner = jnp.floor((value + 0.5) * (1.0 / span))
+    rel = value - owner * span
+    high = jnp.floor(rel * (1.0 / LANES))
+    return owner, owner * 8 + high, rel - high * LANES
+
+
+def owner_counts(ids_row, span, owners):
+    slots = ids_row.shape[1]
+    owner, row, lane = slot_codes(ids_row, span)
+    rows = ones_where(iota((owners * 8, slots), 0).astype(F32) == row)
+    lanes = ones_where(iota((LANES, slots), 0).astype(F32) == lane)
+    return owner, rows, lanes, jnp.where(dot_nt(rows, lanes) > 0, 1.0, 0.0)
+
+
+def slot_plan(ids_row, match, span, owners, turn, capacity):
+    slots = ids_row.shape[1]
+    owner, rows, lanes, used = owner_counts(ids_row, span, owners)
+    place = in_round(positions(used, owners * 8 // LANES), used, turn, capacity)
+    mine = jnp.sum(dot_tn(place.astype(BF16), rows) * lanes.astype(F32), axis=0, keepdims=True)
+    target = jnp.where(mine > 0, owner * capacity + mine - 1, -1.0)
+    for owner_at in range(0, owners, 4):
+        index = (iota((4 * capacity, slots), 0) + owner_at * capacity).astype(F32)
+        match[owner_at * capacity:(owner_at + 4) * capacity, :] = ones_where(index == target)
+
+
+def most_distinct(ids_all, span, owners, lists):
+    def one(d, most):
+        _, _, _, used = owner_counts(ids_all[d // 2, pl.ds(lax.rem(d, 2), 1), :], span, owners)
+        per_row = jnp.sum(used, axis=1, keepdims=True)
+        per_owner = jnp.sum(per_row.reshape(owners, 8, 1), axis=1)
+        return jnp.maximum(most, jnp.max(per_owner))
+
+    return lax.fori_loop(0, lists, one, jnp.float32(0))
+
+
+def device_at(index, columns):
+    return (index // columns, lax.rem(index, columns))
+
+
+def remote(src, dst, send, recv, peer):
+    return pltpu.make_async_remote_copy(src, dst, send, recv, device_id=peer, device_id_type=MESH)
+
+
+def lookup_rounds(columns, me, packed, landed, send, recv):
+    lists, owners = 2 * columns, 4 * columns
+
+    def target(d):
+        return lax.rem(d, 2) * columns + d // 2
+
+    def copy(d):
+        return remote(packed.at[d], landed.at[me], send.at[d], recv.at[me], device_at(target(d), columns))
+
+    def start(i, carry):
+        d = lax.rem(i + 2 * lax.rem(me, columns), lists)
+
+        @pl.when(target(d) != me)
+        def _():
+            copy(d).start()
+
+        @pl.when(target(d) == me)
+        def _():
+            landed[me] = packed[d]
+        return carry
+
+    def arrive(o, carry):
+        @pl.when(o != me)
+        def _():
+            remote(packed.at[0], landed.at[o], send.at[0], recv.at[o], device_at(o, columns)).wait_recv()
+        return carry
+
+    def left(d, carry):
+        @pl.when(target(d) != me)
+        def _():
+            copy(d).wait_send()
+        return carry
+
+    return (lambda: lax.fori_loop(0, lists, start, 0), lambda: lax.fori_loop(0, owners, arrive, 0),
+            lambda: lax.fori_loop(0, lists, left, 0))
+
+
+def return_rounds(columns, me, parts, landed, send, recv):
+    lists, owners = 2 * columns, 4 * columns
+    slot = lax.rem(me, columns) * 2 + me // columns
+
+    def copy(o):
+        return remote(parts.at[o], landed.at[slot], send.at[o], recv.at[slot], device_at(o, columns))
+
+    def start(i, carry):
+        o = lax.rem(i + me, owners)
+
+        @pl.when(o != me)
+        def _():
+            copy(o).start()
+
+        @pl.when(o == me)
+        def _():
+            landed[slot] = parts[me]
+        return carry
+
+    def arrive(d, carry):
+        source = lax.rem(d, 2) * columns + d // 2
+
+        @pl.when(source != me)
+        def _():
+            remote(parts.at[0], landed.at[d], send.at[0], recv.at[d], device_at(source, columns)).wait_recv()
+        return carry
+
+    def left(o, carry):
+        @pl.when(o != me)
+        def _():
+            copy(o).wait_send()
+        return carry
+
+    return (lambda: lax.fori_loop(0, owners, start, 0), lambda: lax.fori_loop(0, lists, arrive, 0),
+            lambda: lax.fori_loop(0, owners, left, 0))
+
+
+def greet_all(columns, me, others):
+    barrier = pltpu.get_barrier_semaphore()
+
+    def greet(o, carry):
+        @pl.when(o != me)
+        def _():
+            pl.semaphore_signal(barrier, inc=1, device_id=device_at(o, columns), device_id_type=MESH)
+        return carry
+
+    lax.fori_loop(0, others, greet, 0)
+    return barrier
+
+
+def pack_rows(table, padded, picks, packed, span, capacity, lists):
+    padded[pl.ds(0, span), :] = table[...]
+    for d in range(0, lists, 4):
+        rows = dot_nn(picks[d * capacity:(d + 4) * capacity, :], padded[...]).astype(BF16)
+        packed[d:d + 4] = rows.reshape(4, capacity, rows.shape[1])
+
+
+def lookup_kernel(
+    columns, capacity,
+    ids, table, cot_in, proj, vocab, gain_in, shift_in, bias_in, qkv_in, out_in, up_in, down_in,
+    x_out, match, picks, ids_all, most_out, pool_out, gain_all, shift_all, bias_all, qkv_all, out_all, up_all, down_all,
+    used_rows, padded, packed, landed, pool_send, pool_parts,
+    i_send, i_recv, t_send, t_recv, w_send, w_recv, g_send, g_recv,
+):
+    section = lax.axis_index("section")
+    column = lax.axis_index("dp")
+    core = lax.rem(section, 2)
+    me = section * columns + column
+    owners, lists = 4 * columns, 2 * columns
+    span, width = table.shape
+    entries = cot_in.shape[0]
+    core_peer = (section + 1 - 2 * core, column)
+    barrier = greet_all(columns, me, owners)
+    ids_all[column] = ids[...]
+    padded[...] = jnp.zeros_like(padded)
+    pl.semaphore_wait(barrier, owners - 1)
+
+    def ids_copy(d):
+        return remote(ids, ids_all.at[column], i_send.at[d - 1], i_recv.at[column],
+                      (section, lax.rem(column + d, columns)))
+
+    for d in range(1, columns):
+        ids_copy(d).start()
+    pairs = ((gain_in, gain_all), (shift_in, shift_all), (bias_in, bias_all),
+             (qkv_in, qkv_all), (out_in, out_all), (up_in, up_all), (down_in, down_all))
+    weight_copies = [
+        remote(src, dst, w_send.at[i], w_recv.at[i], core_peer) for i, (src, dst) in enumerate(pairs)]
+    for copy in weight_copies:
+        copy.start()
+
+    position = column * entries + iota((entries, cot_in.shape[1]), 0)
+    cot = jnp.where(position < vocab[0], cot_in[...].astype(F32), 0.0).astype(BF16)
+    part = dot_nt(cot, proj[...]).astype(BF16)
+    pool_send[...] = part.reshape(2, entries // 2, width)
+
+    def pool_copy(k):
+        return remote(pool_send.at[k], pool_parts.at[section], g_send.at[k], g_recv.at[section], (2 + k, column))
+
+    for k in range(2):
+        @pl.when(section != 2 + k)
+        def _(k=k):
+            pool_copy(k).start()
+
+        @pl.when(section == 2 + k)
+        def _(k=k):
+            pool_parts[section] = pool_send[k]
+
+    for d in range(1, columns):
+        source = lax.rem(column + d, columns)
+        remote(ids, ids_all.at[source], i_send.at[d - 1], i_recv.at[source], (section, source)).wait_recv()
+    turn = jnp.int32(0)
+    owner_plan(ids_all, picks, used_rows, me * span, span, turn, capacity, lists)
+    pack_rows(table, padded, picks, packed, span, capacity, lists)
+    start, arrive, left = lookup_rounds(columns, me, packed, landed, t_send, t_recv)
+    start()
+
+    @pl.when(section < 2)
+    def _():
+        slot_plan(ids_all[column, pl.ds(core, 1), :], match, span, owners, turn, capacity)
+
+    most_out[...] = jnp.full(most_out.shape, most_distinct(ids_all, span, owners, lists), F32)
+
+    @pl.when(section >= 2)
+    def _():
+        total = pool_parts[section].astype(F32)
+        for d in range(1, 4):
+            source = lax.rem(section + d, 4)
+            remote(pool_send.at[0], pool_parts.at[source], g_send.at[0], g_recv.at[source],
+                   (source, column)).wait_recv()
+            total = total + pool_parts[source].astype(F32)
+        pool_out[...] = total
+
+    @pl.when(section < 2)
+    def _():
+        arrive()
+        x_out[...] = dot_tn(match[...], landed[...].reshape(owners * capacity, width)).astype(BF16)
+
+    left()
+    for k in range(2):
+        @pl.when(section != 2 + k)
+        def _(k=k):
+            pool_copy(k).wait_send()
+    for d in range(1, columns):
+        ids_copy(d).wait_send()
+    for copy in weight_copies:
+        copy.wait()
+
+
+def lookup(columns, ids, table, cot, proj, vocab, gain, shift, bias, w_qkv, w_out, w_up, w_down):
+    slots = ids.shape[1]
+    span, width = table.shape
+    owners, lists = 4 * columns, 2 * columns
+    capacity = capacity_of(slots, owners)
+    padded_span = -(-span // LANES) * LANES
+    entries = cot.shape[0]
+    vmem = pl.BlockSpec(memory_space=pltpu.VMEM)
+    smem = pl.BlockSpec(memory_space=pltpu.SMEM)
+    hbm = pl.BlockSpec(memory_space=pl.ANY)
+    shape = jax.ShapeDtypeStruct
+    params = (gain, shift, bias, w_qkv, w_out, w_up, w_down)
+    outs = [
+        shape((slots, width), BF16), shape((owners * capacity, slots), BF16),
+        shape((lists * capacity, padded_span), BF16), shape((columns, 2, slots), jnp.int32), shape((8, LANES), F32),
+        shape((entries // 2, width), F32),
+    ] + [shape(p.shape, p.dtype) for p in params]
+    sem = pltpu.SemaphoreType.DMA
+    return pl.pallas_call(
+        functools.partial(lookup_kernel, columns, capacity),
+        out_shape=outs,
+        in_specs=[vmem] * 4 + [smem] + [hbm] * 7,
+        out_specs=[vmem] * 6 + [hbm] * 7,
+        scratch_shapes=[
+            pltpu.VMEM((max(lists, owners) * 8, LANES), F32), pltpu.VMEM((padded_span, width), BF16),
+            pltpu.VMEM((lists, capacity, width), BF16), pltpu.VMEM((owners, capacity, width), BF16),
+            pltpu.VMEM((2, entries // 2, width), BF16), pltpu.VMEM((4, entries // 2, width), BF16),
+            sem((columns - 1,)), sem((columns,)), sem((lists,)), sem((owners,)), sem((7,)), sem((7,)),
+            sem((2,)), sem((4,)),
+        ],
+        compiler_params=pltpu.CompilerParams(collective_id=3, has_side_effects=True, vmem_limit_bytes=VMEM_BYTES),
+    )(ids, table, cot, proj, vocab, *params)
+
+
+def more_lookup_kernel(columns, capacity, turn, ids_all, table, x_out, match, picks, used_rows, padded, packed, landed,
+                       t_send, t_recv):
+    section = lax.axis_index("section")
+    column = lax.axis_index("dp")
+    me = section * columns + column
+    owners, lists = 4 * columns, 2 * columns
+    span, width = table.shape
+    barrier = pltpu.get_barrier_semaphore()
+
+    @pl.when(section < 2)
+    def _():
+        greet_all(columns, me, owners)
+        pl.semaphore_wait(barrier, lists - 1)
+
+    @pl.when(section >= 2)
+    def _():
+        pl.semaphore_wait(barrier, lists)
+
+    padded[...] = jnp.zeros_like(padded)
+    owner_plan(ids_all, picks, used_rows, me * span, span, turn[0], capacity, lists)
+    pack_rows(table, padded, picks, packed, span, capacity, lists)
+    start, arrive, left = lookup_rounds(columns, me, packed, landed, t_send, t_recv)
+    start()
+    x_out[...] = jnp.zeros_like(x_out)
+
+    @pl.when(section < 2)
+    def _():
+        slot_plan(ids_all[column, pl.ds(lax.rem(section, 2), 1), :], match, span, owners, turn[0], capacity)
+        arrive()
+        x_out[...] = dot_tn(match[...], landed[...].reshape(owners * capacity, width)).astype(BF16)
+
+    left()
+
+
+def more_lookup(columns, turn, ids_all, table):
+    slots = ids_all.shape[2]
+    span, width = table.shape
+    owners, lists = 4 * columns, 2 * columns
+    capacity = capacity_of(slots, owners)
+    padded_span = -(-span // LANES) * LANES
+    vmem = pl.BlockSpec(memory_space=pltpu.VMEM)
+    sem = pltpu.SemaphoreType.DMA
+    return pl.pallas_call(
+        functools.partial(more_lookup_kernel, columns, capacity),
+        out_shape=jax.ShapeDtypeStruct((slots, width), BF16),
+        in_specs=[pl.BlockSpec(memory_space=pltpu.SMEM), vmem, vmem],
+        out_specs=vmem,
+        scratch_shapes=[
+            pltpu.VMEM((owners * capacity, slots), BF16), pltpu.VMEM((lists * capacity, padded_span), BF16),
+            pltpu.VMEM((max(lists, owners) * 8, LANES), F32), pltpu.VMEM((padded_span, width), BF16),
+            pltpu.VMEM((lists, capacity, width), BF16), pltpu.VMEM((owners, capacity, width), BF16),
+            sem((lists,)), sem((owners,)),
+        ],
+        compiler_params=pltpu.CompilerParams(collective_id=4, has_side_effects=True, vmem_limit_bytes=VMEM_BYTES),
+    )(turn, ids_all, table)
+
+
+def return_parts(match, dx, parts, owners, capacity):
+    for o in range(0, owners, 4):
+        rows = dot_nn(match[o * capacity:(o + 4) * capacity, :], dx[...]).astype(BF16)
+        parts[o:o + 4] = rows.reshape(4, capacity, rows.shape[1])
+
+
+def more_return_kernel(columns, capacity, turn, ids_all, dx, held, grad_out, match, picks, used_rows, parts, landed,
+                       t_send, t_recv):
+    section = lax.axis_index("section")
+    column = lax.axis_index("dp")
+    me = section * columns + column
+    owners, lists = 4 * columns, 2 * columns
+    span, width = held.shape
+    slots = ids_all.shape[2]
+    barrier = greet_all(columns, me, lists)
+
+    @pl.when(section < 2)
+    def _():
+        pl.semaphore_wait(barrier, owners - 1)
+
+    start, arrive, left = return_rounds(columns, me, parts, landed, t_send, t_recv)
+
+    @pl.when(section < 2)
+    def _():
+        slot_plan(ids_all[column, pl.ds(lax.rem(section, 2), 1), :], match, span, owners, turn[0], capacity)
+        return_parts(match, dx, parts, owners, capacity)
+        start()
+
+    owner_plan(ids_all, picks, used_rows, me * span, span, turn[0], capacity, lists)
+    arrive()
+    grad = dot_tn(picks[...], landed[...].reshape(lists * capacity, width))
+    grad_out[...] = held[...] + grad[:span]
+
+    @pl.when(section < 2)
+    def _():
+        left()
+
+
+def more_return(columns, turn, ids_all, dx, held):
+    slots = ids_all.shape[2]
+    span, width = held.shape
+    owners, lists = 4 * columns, 2 * columns
+    capacity = capacity_of(slots, owners)
+    padded_span = -(-span // LANES) * LANES
+    vmem = pl.BlockSpec(memory_space=pltpu.VMEM)
+    sem = pltpu.SemaphoreType.DMA
+    return pl.pallas_call(
+        functools.partial(more_return_kernel, columns, capacity),
+        out_shape=jax.ShapeDtypeStruct((span, width), F32),
+        in_specs=[pl.BlockSpec(memory_space=pltpu.SMEM), vmem, vmem, vmem],
+        out_specs=vmem,
+        scratch_shapes=[
+            pltpu.VMEM((owners * capacity, slots), BF16), pltpu.VMEM((lists * capacity, padded_span), BF16),
+            pltpu.VMEM((max(lists, owners) * 8, LANES), F32),
+            pltpu.VMEM((owners, capacity, width), BF16), pltpu.VMEM((lists, capacity, width), BF16),
+            sem((owners,)), sem((lists,)),
+        ],
+        compiler_params=pltpu.CompilerParams(collective_id=5, has_side_effects=True, vmem_limit_bytes=VMEM_BYTES),
+    )(turn, ids_all, dx, held)
+
+
+LAG_X = 2
+LAG_Z = 4
+TABLE_STEP = 9
+
+
+def reduce_kernel(
+    columns, width, hidden,
+    a, dqkv, att, dbr, h_in, dpre, act, dy, vec, upb, pooled, cot_in, proj, dx, match, picks, vocab,
+    emb_out, gain_out, shift_out, upb_out, qkv_out, out_out, up_out, down_out, proj_out, table_out,
+    s0_send, s0_recv, sums, s1_recv, z_recv, v_buf, pool_all, cot, parts, landed,
+    c_send, c_recv, x_send, x_recv, zs_send, zs_recv, v_send, v_recv, p_send, p_recv, t_send, t_recv,
+):
+    section = lax.axis_index("section")
+    column = lax.axis_index("dp")
+    core = lax.rem(section, 2)
+    depth = columns // 2
+    side, place = lax.rem(column, 2), column // 2
+    piece = width // columns
+    tiles = hidden // width
+    units = 3 + 1 + tiles + tiles
+    core_peer = (section + 1 - 2 * core, column)
+    side_peer = (section, column + 1 - 2 * side)
+
+    def place_at(d):
+        return lax.rem(place + d, depth)
+
+    def place_peer(d):
+        return (section, place_at(d) * 2 + side)
+
+    def section_peer(d):
+        return (lax.rem(section + d, 4), column)
+
+    owners, lists = 4 * columns, 2 * columns
+    capacity = parts.shape[1]
+    me = section * columns + column
+    barrier = greet_all(columns, me, owners)
+    pl.semaphore_wait(barrier, owners - 1)
+    start, arrive, left = return_rounds(columns, me, parts, landed, t_send, t_recv)
+
+    @pl.when(section < 2)
+    def _():
+        return_parts(match, dx, parts, owners, capacity)
+        start()
+
+    def pool_copy(d):
+        return remote(pooled, pool_all.at[core], p_send.at[d - 1], p_recv.at[core], section_peer(d))
+
+    def pool_arrival(k):
+        return remote(pooled, pool_all.at[k], p_send.at[0], p_recv.at[k], core_peer)
+
+    @pl.when(section >= 2)
+    def _():
+        for d in range(1, 4):
+            pool_copy(d).start()
+        pool_all[core] = pooled[...]
+
+    def vec_copy(slot, peer, index):
+        return remote(v_buf.at[slot], v_buf.at[index], v_send.at[index], v_recv.at[index], peer)
+
+    def vec_of(layer):
+        return vec[layer], upb[layer]
+
+    def put_vec(slot, layer):
+        rows, bias = vec_of(layer)
+        v_buf[slot, :, slice(0, width)] = rows
+        for t in range(2):
+            v_buf[slot, pl.ds(6 + t, 1), :] = bias[:, t * (hidden // 2):(t + 1) * (hidden // 2)]
+
+    put_vec(0, 1 - core)
+    vec_copy(0, core_peer, 2).start()
+    put_vec(1, core)
+
+    def core_copy(u):
+        return remote(s0_send.at[u], s0_recv.at[u], c_send.at[u], c_recv.at[u], core_peer)
+
+    def side_copy(u):
+        return remote(sums.at[u, 1 - side], s1_recv.at[u], x_send.at[u], x_recv.at[u], side_peer)
+
+    def place_copy(u, d):
+        return remote(s1_recv.at[u, place_at(d)], z_recv.at[u, d - 1], zs_send.at[u, d - 1], zs_recv.at[u, d - 1],
+                      place_peer(d))
+
+    def cut(value, q):
+        return value[q * piece:(q + 1) * piece, :]
+
+    def product(layer, u):
+        if u < 3:
+            return dot_tn(a[layer], dqkv[layer, :, u * width:(u + 1) * width])
+        if u == 3:
+            return dot_tn(att[layer], dbr[layer])
+        t = u - 4
+        return dot_tn(h_in[layer], dpre[layer, :, t * width:(t + 1) * width])
+
+    def send_other(u):
+        value = product(1 - core, u).astype(BF16)
+        for q in range(columns):
+            s0_send[u, q % 2, q // 2] = cut(value, q)
+        core_copy(u).start()
+
+    def add_own(u):
+        value = product(core, u)
+        core_copy(u).wait_recv()
+        for q in range(columns):
+            sums[u, q % 2, q // 2] = (cut(value, q) + s0_recv[u, q % 2, q // 2].astype(F32)).astype(BF16)
+
+    first_down = 4 + tiles
+
+    def down_product(layer, i):
+        return dot_tn(act[layer, :, i * width:(i + 1) * width], dy[layer])
+
+    def down_parts(i):
+        for j in range(columns):
+            yield j, first_down + j % tiles, i * columns // tiles + j // tiles
+
+    def down_other():
+        for i in range(tiles):
+            value = down_product(1 - core, i).astype(BF16)
+            for j, u, q in down_parts(i):
+                s0_send[u, q % 2, q // 2] = cut(value, j)
+        for u in range(first_down, units):
+            core_copy(u).start()
+
+    def down_own():
+        for i in range(tiles):
+            value = down_product(core, i)
+            if i == 0:
+                for u in range(first_down, units):
+                    core_copy(u).wait_recv()
+            for j, u, q in down_parts(i):
+                sums[u, q % 2, q // 2] = (cut(value, j) + s0_recv[u, q % 2, q // 2].astype(F32)).astype(BF16)
+
+    def project():
+        @pl.when(section >= 2)
+        def _():
+            pool_arrival(1 - core).wait_recv()
+
+        @pl.when(section < 2)
+        def _():
+            pool_arrival(0).wait_recv()
+            pool_arrival(1).wait_recv()
+
+        entries = cot_in.shape[0]
+        position = column * entries + lax.broadcasted_iota(jnp.int32, (entries, width), 0)
+        live = position < vocab[0]
+        cot[...] = jnp.where(live, cot_in[...].astype(F32), 0.0).astype(BF16)
+        rows = pool_all[...].reshape(entries, width)
+        emb_out[...] = jnp.where(live, dot_nn(rows, proj[...]), 0.0)
+        value = dot_tn(rows, cot[...]).astype(BF16)
+        for q in range(columns):
+            sums[units, q % 2, q // 2] = cut(value, q)
+
+    def middle(u):
+        side_copy(u).wait_recv()
+        s1_recv[u] = (s1_recv[u].astype(F32) + sums[u, side].astype(F32)).astype(BF16)
+        for d in range(1, depth):
+            place_copy(u, d).start()
+
+    def finish(u):
+        total = s1_recv[u, place].astype(F32)
+        for d in range(1, depth):
+            place_copy(u, d).wait_recv()
+            total = total + z_recv[u, d - 1].astype(F32)
+        if u < 3:
+            qkv_out[0, :, u * width:(u + 1) * width] = total
+        elif u == 3:
+            out_out[0] = total
+        elif u < first_down:
+            up_out[0, :, (u - 4) * width:(u - 3) * width] = total
+        elif u < units:
+            t = u - first_down
+            down_out[0, t * piece:(t + 1) * piece, :] = total
+        else:
+            proj_out[...] = total
+
+    def vec_step(k):
+        if k == 0:
+            vec_copy(0, core_peer, 2).wait_recv()
+            v_buf[1] = v_buf[1] + v_buf[2]
+            vec_copy(1, side_peer, 3).start()
+        if k == 1:
+            vec_copy(1, side_peer, 3).wait_recv()
+            v_buf[4] = v_buf[1] + v_buf[3]
+            for d in range(1, depth):
+                vec_copy(4, place_peer(d), 4 + d).start()
+        if k == 2:
+            total = v_buf[4]
+            for d in range(1, depth):
+                vec_copy(4, place_peer(d), 4 + d).wait_recv()
+                total = total + v_buf[4 + d]
+            lanes = width // columns
+            share = hidden // columns
+            for q in range(columns):
+                @pl.when(column == q)
+                def _(q=q):
+                    gain_out[0] = total[0:2, q * lanes:(q + 1) * lanes]
+                    shift_out[0] = total[2:6, q * lanes:(q + 1) * lanes]
+                    row, start = divmod(q * share, hidden // 2)
+                    upb_out[...] = total[6 + row:7 + row, start:start + share]
+
+    for step in range(units + 1 + LAG_Z):
+        if step < first_down:
+            send_other(step)
+            add_own(step)
+        elif step == first_down:
+            down_other()
+            down_own()
+        elif step == units:
+            project()
+        if step <= units:
+            side_copy(step).start()
+        if step == TABLE_STEP:
+            arrive()
+            grad = dot_tn(picks[...], landed[...].reshape(lists * capacity, width))
+            table_out[...] = grad[:table_out.shape[0]]
+        if step in (1, 3, 5):
+            vec_step((step - 1) // 2)
+        if 0 <= step - LAG_X <= units:
+            middle(step - LAG_X)
+        if 0 <= step - LAG_Z <= units:
+            finish(step - LAG_Z)
+
+    @pl.when(section < 2)
+    def _():
+        left()
+
+    vec_copy(0, core_peer, 2).wait_send()
+    vec_copy(1, side_peer, 3).wait_send()
+    for d in range(1, depth):
+        vec_copy(4, place_peer(d), 4 + d).wait_send()
+    for u in range(units):
+        core_copy(u).wait_send()
+    for u in range(units + 1):
+        side_copy(u).wait_send()
+        for d in range(1, depth):
+            place_copy(u, d).wait_send()
+
+    @pl.when(section >= 2)
+    def _():
+        for d in range(1, 4):
+            pool_copy(d).wait_send()
+
+
+def reduce_all(columns, a, dqkv, att, dbr, h_in, dpre, act, dy, vec, upb, pooled, cot, proj, dx, match, picks, span, vocab):
+    width, hidden = a.shape[2], dpre.shape[2]
+    entries, out_width = cot.shape
+    piece, depth, tiles = width // columns, columns // 2, hidden // width
+    units = 4 + 2 * tiles
+    capacity = match.shape[0] // (4 * columns)
+    vmem = pl.BlockSpec(memory_space=pltpu.VMEM)
+    smem = pl.BlockSpec(memory_space=pltpu.SMEM)
+    shape = jax.ShapeDtypeStruct
+    outs = [
+        shape((entries, out_width), F32), shape((1, 2, piece), F32), shape((1, 4, piece), F32),
+        shape((1, hidden // columns), F32), shape((1, piece, 3 * width), F32), shape((1, piece, width), F32),
+        shape((1, piece, hidden), F32), shape((1, tiles * piece, width), F32), shape((piece, out_width), F32),
+        shape((span, width), F32),
+    ]
+    sem = pltpu.SemaphoreType.DMA
+    return pl.pallas_call(
+        functools.partial(reduce_kernel, columns, width, hidden),
+        out_shape=outs,
+        in_specs=[vmem] * 16 + [smem],
+        out_specs=[vmem] * len(outs),
+        scratch_shapes=[
+            pltpu.VMEM((units, 2, depth, piece, width), BF16), pltpu.VMEM((units, 2, depth, piece, width), BF16),
+            pltpu.VMEM((units + 1, 2, depth, piece, width), BF16), pltpu.VMEM((units + 1, depth, piece, width), BF16),
+            pltpu.VMEM((units + 1, depth - 1, piece, width), BF16), pltpu.VMEM((4 + depth, 8, hidden // 2), F32),
+            pltpu.VMEM((2, entries // 2, width), BF16), pltpu.VMEM((entries, out_width), BF16),
+            pltpu.VMEM((4 * columns, capacity, width), BF16), pltpu.VMEM((2 * columns, capacity, width), BF16),
+            sem((units,)), sem((units,)), sem((units + 1,)), sem((units + 1,)),
+            sem((units + 1, depth - 1)), sem((units + 1, depth - 1)), sem((4 + depth,)), sem((4 + depth,)),
+            sem((3,)), sem((2,)), sem((4 * columns,)), sem((2 * columns,)),
+        ],
+        compiler_params=pltpu.CompilerParams(collective_id=2, has_side_effects=True, vmem_limit_bytes=VMEM_BYTES),
+    )(a, dqkv, att, dbr, h_in, dpre, act, dy, vec, upb, pooled, cot, proj, dx, match, picks, vocab)
 
 
 def local(table, piece_ids, piece_counts, vocab_size, norm_gain, shift_bias, up_bias, qkv_weight, out_weight,
           up_weight, down_weight, proj_weight, embed_cotangent):
     section = lax.axis_index("section")
-    column = lax.axis_index("dp")
     columns = lax.axis_size("dp")
     core = lax.rem(section, 2)
     entries, pieces = piece_ids.shape
-    width = qkv_weight.shape[1]
     half = entries // 2
-    positions = column * entries + jnp.arange(entries, dtype=jnp.int32)
-    live = positions < vocab_size[0]
-    flat_ids = piece_ids.reshape(entries * pieces)
-    quarter = lax.all_gather(table, "dp", axis=0, tiled=True)
-    span = quarter.shape[0]
-    local_ids = flat_ids - section * span
-    inside = (local_ids >= 0) & (local_ids < span)
-    safe_ids = jnp.clip(local_ids, 0, span - 1)
-    picked = jnp.where(inside[:, None], jnp.take(quarter, safe_ids, axis=0), 0)
-    embedded = lax.psum(picked, "section")
-    x0 = lax.dynamic_slice_in_dim(embedded, core * half * pieces, half * pieces, 0)
-    cotangent = jnp.where(live[:, None], embed_cotangent, jnp.zeros_like(embed_cotangent))
-    pool_grad = lax.psum(dot_nt(cotangent, proj_weight).astype(BF16), "section").astype(F32)
-    pool_half = lax.dynamic_slice_in_dim(pool_grad, core * half, half, 0)
+    ids = piece_ids.reshape(2, half * pieces)
     my_counts = lax.dynamic_slice_in_dim(piece_counts, core * half, half, 0)
     count_rows = jnp.repeat(my_counts, pieces).reshape(-1, LANES)
-
-    def both(value):
-        swapped = lax.ppermute(value, "section", [(0, 1), (1, 0), (2, 3), (3, 2)])
-        return jnp.where(core == 0, jnp.concatenate([value, swapped]), jnp.concatenate([swapped, value]))
-
-    gains, shifts, bias = both(norm_gain), both(shift_bias), both(up_bias)[:, None, :]
-    w_qkv, w_out, w_up, w_down = both(qkv_weight), both(out_weight), both(up_weight), both(down_weight)
+    own = (norm_gain, shift_bias, up_bias[:, None, :], qkv_weight, out_weight, up_weight, down_weight)
+    x0, match, picks, ids_all, most, pool_grad, *theirs = lookup(
+        columns, ids, table, embed_cotangent, proj_weight, vocab_size, *own)
+    capacity = match.shape[0] // (4 * columns)
+    turns = (most[0, 0].astype(jnp.int32) + capacity - 1) // capacity
+    x0 = lax.fori_loop(
+        1, turns, lambda turn, x: x + more_lookup(columns, turn.reshape(1), ids_all, table), x0)
     a, dqkv, att, dbr, h, dpre, act, dy, dx, pooled, vec, upb = trunk(
-        x0, count_rows, pool_half, gains, shifts, bias, w_qkv, w_out, w_up, w_down)
-    whole_pooled = lax.all_gather(pooled, "section", axis=0, tiled=True)[2 * half:]
-    embeddings = jnp.dot(whole_pooled, proj_weight, preferred_element_type=F32) * live[:, None].astype(F32)
-    grad_proj = contract_rows(whole_pooled, cotangent)
-
-    def mine(value):
-        own = lax.dynamic_index_in_dim(value, core, 0)
-        gone = lax.dynamic_index_in_dim(value, 1 - core, 0)
-        return own + lax.ppermute(gone, "section", [(0, 1), (1, 0), (2, 3), (3, 2)])
-
-    batched = lambda left, right: lax.dot_general(
-        left, right, (((1,), (1,)), ((0,), (0,))), preferred_element_type=F32)
-    g_qkv, g_out, g_up, g_down = mine(batched(a, dqkv)), mine(batched(att, dbr)), mine(batched(h, dpre)), mine(batched(act, dy))
-    vec, upb = mine(vec), mine(upb)
-    scatter = lambda value, axis: lax.psum_scatter(value, "dp", scatter_dimension=axis, tiled=True)
-    low = lambda value, axis: scatter(value.astype(BF16), axis).astype(F32)
-    spread = jnp.where(section < 2, dx, jnp.zeros_like(dx))
-    spread = lax.all_gather(spread, "section", axis=0, tiled=True)[: 2 * half * pieces].astype(F32)
-    partial = jax.ops.segment_sum(jnp.where(inside[:, None], spread, 0.0), safe_ids, num_segments=span)
-    table_grad = scatter(partial, 0)
-    return (
-        embeddings, table_grad, scatter(vec[:, 0:2], 2), scatter(vec[:, 2:6], 2), scatter(upb[:, 0], 1),
-        low(g_qkv, 1), low(g_out, 1), low(g_up, 1), low(g_down, 1), low(grad_proj, 0),
-    )
+        x0, count_rows, pool_grad, own, theirs)
+    emb, g_gain, g_shift, g_bias, g_qkv, g_out, g_up, g_down, g_proj, g_table = reduce_all(
+        columns, a, dqkv, att, dbr, h, dpre, act, dy, vec, upb, pooled, embed_cotangent, proj_weight, dx, match, picks,
+        table.shape[0], vocab_size)
+    g_table = lax.fori_loop(
+        1, turns, lambda turn, held: more_return(columns, turn.reshape(1), ids_all, dx, held), g_table)
+    return emb, g_table, g_gain, g_shift, g_bias, g_qkv, g_out, g_up, g_down, g_proj
 
 
 def solution(mesh):

time: 1110 us -> 243 us (0.22)
  waiting for transfers between devices: 883 us -> 0 us
  Pallas kernels: 84.1 us -> 228 us
  other arithmetic: 67.7 us -> 0 us
  local copies, waits for them, and re-layouts: 34.6 us -> 12.5 us
  matrix products: 17.8 us -> 0 us
  between operations: 15.2 us -> 2.07 us
    reduce_scatter x6 -> x0, waiting for transfers between devices: 608 us -> none  [local(): lax.psum_scatter(value, 'dp', scatter_dimension=axis, tiled=True)]
    pallas_call x0 -> x2, Pallas kernels: none -> 145 us  [the longest x1 115 us: reduce_all(): pl.pallas_call(functools.partial(reduce_kernel, columns, width, hidden),...]
    unnamed x15 -> x0, waiting for transfers between devices: 135 us -> none
    all_gather x2 -> x0, waiting for transfers between devices: 107 us -> none  [the longest x1 107 us: local(): quarter = lax.all_gather(table, 'dp', axis=0, tiled=True)]
    convert_element_type x11 -> x0, other arithmetic: 27.5 us -> none  [the longest x9 26 us: local(): low = lambda value, axis: scatter(value.astype(BF16), axis).astype(F32)]
    psum x1 -> x0, waiting for transfers between devices: 25.2 us -> none  [local(): embedded = lax.psum(picked, 'section')]
    select_n x10 -> x0, other arithmetic: 24.5 us -> none  [the longest x7 21 us: both(): jnp.where(core == 0, jnp.concatenate([value, swapped]), jnp.concatenate([...]
    dot_general x7 -> x0, matrix products: 17.8 us -> none  [the longest x4 13.8 us: local(): lax.dot_general(left, right, (((1,), (1,)), ((0,), (0,))), preferred_elem...]
  transfers between devices with their start and end apart: 25 -> 0, of which waited for: 14 -> 0; matrix products, arithmetic and copies ran while one was open for 10% -> 0% of each run, Pallas kernels for 0% -> 0%
where the time goes in v2:
time: 243 us
  Pallas kernels  228 us (94%)
  local copies, waits for them, and re-layouts  12.5 us (5%)
    pallas_call x1, Pallas kernels, reduce_all(): pl.pallas_call(functools.partial(reduce_kernel, columns, width, hidden),...  115 us
    pallas_call x1, Pallas kernels, trunk(): pl.pallas_call(functools.partial(trunk_kernel, micros, width, hidden), ou...  83.3 us
    pallas_call x1, Pallas kernels, lookup(): pl.pallas_call(functools.partial(lookup_kernel, columns, capacity), out_s...  30.2 us
    unnamed x33, local copies, waits for them, and re-layouts  9.72 us

profile of v2, /device:TPU:0, one launch (start us, length us, event | category | flops | bytes accessed | tf_op | source)
XLA Modules:
  0.0 243.0 jit_solution(14505194755353106994)
XLA Ops:
  1.3 0.8 copy.24
  2.1 0.7 reshape.34.ids
  2.8 0.0 copy-start
  2.8 30.2 %shard_map.204 = (bf16[512,512]{1,0:T(8,128)(2,1)S(1)}, bf16[1024,512]{1,0:T(8,128)(2,1)}, bf16[512,1024]{1,0:T(8,128)(2,1)}, s32[8,2,512]{2,1,0:T(2,128)S(1)}, ...) custom-call(s32[2,512]{1,0:T(2,128)} %reshape.34.ids, ...), custom_call_target="tpu_custom_call" | custom-call | tf_op jit(solution)/shard_map/pallas_call | solution.py:677
  32.9 1.2 slice.3
  34.8 0.0 copy-done
  34.8 0.0 copy-start.10
  34.9 0.6 copy-done.10
  35.5 0.1 dynamic_slice.3
  35.6 0.1 broadcast_in_dim.11
  35.6 0.1 broadcast_in_dim.12
  35.7 0.7 broadcast_in_dim.13.counts
  36.4 83.3 %shard_map.205 = (bf16[2,512,512]{2,1,0:T(8,128)(2,1)}, bf16[2,512,1536]{2,1,0:T(8,128)(2,1)}, bf16[2,512,512]{2,1,0:T(8,128)(2,1)}, bf16[2,512,512]{2,1,0:T(8,1...) custom-call(bf16[512,512]{1,0:T(8,128)(2,1)S(1)} %get-tuple-element., ...), custom_call_target="tpu_custom_call" | custom-call | tf_op jit(solution)/shard_map/pallas_call | solution.py:358
  119.7 115.0 %shard_map.206 = (f32[128,512]{1,0:T(8,128)}, f32[1,2,64]{2,1,0:T(2,128)}, f32[1,4,64]{2,1,0:T(4,128)}, f32[1,256]{1,0:T(1,128)}, f32[1,64,1536]{2,1,0:T(8,128)}...) custom-call(bf16[2,512,512]{2,1,0:T(8,128)(2,1)} %get-tuple-element., ...), custom_call_target="tpu_custom_call" | custom-call | tf_op jit(solution)/shard_map/pallas_call | solution.py:1069
  234.7 0.0 copy-start.4
  234.7 0.9 copy-done.4
  235.6 0.7 copy.50
  236.3 0.0 copy-start.9
  236.3 0.0 copy-start.7
  236.3 0.0 copy-start.8
  236.3 0.0 copy-start.3
  236.3 0.0 copy-start.6
  236.4 0.0 copy-start.2
  236.4 1.3 copy.51
  237.7 0.0 copy-done.9
  237.7 0.0 copy-start.1
  237.7 0.0 copy-start.5
  237.7 0.6 copy.52
  238.2 0.0 copy-done.7
  238.2 0.6 copy.53
  238.8 0.0 copy-done.8
  238.8 0.6 copy.54
  239.4 0.0 copy-done.3
  239.4 0.7 copy.55
  240.1 0.0 copy-done.6
  240.1 0.7 copy.56
  240.8 0.0 copy-done.2
  240.8 0.8 copy.57
  241.6 0.0 copy-done.1
  241.6 0.8 copy.58
  242.4 0.0 copy-done.5
  242.4 0.7 copy.59
  (2 shorter events, 0.0 us)
Async XLA Ops:
  2.8 32.0 %copy-start = (bf16[1000,512]{1,0:T(8,128)(2,1)S(1)}, bf16[1000,512]{1,0:T(8,128)(2,1)}, u32[]{:S(2)}) copy-start(bf16[1000,512]{1,0:T(8,128)(2,1)} %table.1) | copy-start | bytes 3072004
  34.8 0.7 copy-start.10
  234.7 1.0 copy-start.4
  236.3 1.3 copy-start.9
  236.3 1.9 copy-start.7
  236.3 2.5 %copy-start.8 = (f32[1,256]{1,0:T(1,128)S(1)}, f32[1,256]{1,0:T(1,128)}, u32[]{:S(2)}) copy-start(f32[1,256]{1,0:T(1,128)} %get-tuple-element.272) | copy-start | bytes 3076
  236.3 3.0 %copy-start.3 = (f32[1,64,1536]{2,1,0:T(8,128)S(1)}, f32[1,64,1536]{2,1,0:T(8,128)}, u32[]{:S(2)}) copy-start(f32[1,64,1536]{2,1,0:T(8,128)} %get-tuple-element.273) | copy-start | bytes 1179652
  236.3 3.8 %copy-start.6 = (f32[1,64,512]{2,1,0:T(8,128)S(1)}, f32[1,64,512]{2,1,0:T(8,128)}, u32[]{:S(2)}) copy-start(f32[1,64,512]{2,1,0:T(8,128)} %get-tuple-element.274) | copy-start | bytes 393220
  236.4 4.4 %copy-start.2 = (f32[1,64,2048]{2,1,0:T(8,128)S(1)}, f32[1,64,2048]{2,1,0:T(8,128)}, u32[]{:S(2)}) copy-start(f32[1,64,2048]{2,1,0:T(8,128)} %get-tuple-element.275) | copy-start | bytes 1572868
  237.7 3.9 %copy-start.1 = (f32[1,256,512]{2,1,0:T(8,128)S(1)}, f32[1,256,512]{2,1,0:T(8,128)}, u32[]{:S(2)}) copy-start(f32[1,256,512]{2,1,0:T(8,128)} %get-tuple-element.276) | copy-start | bytes 1572868
  237.7 4.7 %copy-start.5 = (f32[64,512]{1,0:T(8,128)S(1)}, f32[64,512]{1,0:T(8,128)}, u32[]{:S(2)}) copy-start(f32[64,512]{1,0:T(8,128)} %get-tuple-element.277) | copy-start | bytes 393220

commit v3 on v1

v3 whole, which is shorter than its diff:
```python
import functools
import jax
import jax.numpy as jnp
from jax import lax
from jax.experimental import pallas as pl
from jax.experimental.pallas import tpu as pltpu
from jax.sharding import PartitionSpec as P

HEADS = 8
LANES = 128
EPSILON = 1e-05
MASKED = -1e30
ROOT_HALF = 0.7071067811865476
DENSITY_SCALE = 0.3989422804014327
MESH = pl.DeviceIdType.MESH
F32 = jnp.float32
BF16 = jnp.bfloat16
MICRO = 256
VMEM_BYTES = 60 * 2**20


def dot_nn(left, right):
    return lax.dot_general(left, right, (((1,), (0,)), ((), ())), preferred_element_type=F32)


def dot_nt(left, right):
    return lax.dot_general(left, right, (((1,), (1,)), ((), ())), preferred_element_type=F32)


def dot_tn(left, right):
    return lax.dot_general(left, right, (((0,), (0,)), ((), ())), preferred_element_type=F32)


def statistics(values):
    centered = values - jnp.mean(values, axis=-1, keepdims=True)
    inverse = lax.rsqrt(jnp.mean(centered * centered, axis=-1, keepdims=True) + EPSILON)
    return centered * inverse, inverse


def norm_backward(weighted, normed, inverse):
    return inverse * (
        weighted
        - jnp.mean(weighted, axis=-1, keepdims=True)
        - normed * jnp.mean(weighted * normed, axis=-1, keepdims=True)
    )


def column_sum(values):
    return jnp.sum(values, axis=0, keepdims=True)


def entry_masks():
    lane = lax.broadcasted_iota(jnp.int32, (8, LANES), 1) // 8
    return [lane == e for e in range(LANES // 8)]


def compress(tall, masks):
    tall = tall.reshape(2, LANES // 8, 8, LANES)
    kept = []
    for h in range(2):
        one = tall[h, 0]
        for e in range(1, LANES // 8):
            one = jnp.where(masks[e], tall[h, e], one)
        kept.append(one)
    return kept


def expand(flat, masks):
    zero = jnp.zeros_like(flat)
    return jnp.concatenate([jnp.where(mask, flat, zero) for mask in masks], axis=0).astype(BF16)


def half_masks():
    lane = lax.broadcasted_iota(jnp.int32, (1, LANES), 1)
    low = jnp.where(lane < LANES // 2, 1.0, 0.0)
    return low.astype(BF16), (1.0 - low).astype(BF16)


def by_head(pair, halves):
    return jnp.concatenate([pair * halves[0], pair * halves[1]], axis=0)


def head_mask(count_row):
    return lax.broadcasted_iota(jnp.int32, (8, LANES), 0) < count_row


def pool_matrix(count_row):
    lane = lax.broadcasted_iota(jnp.int32, (LANES // 8, LANES), 1)
    entry = lax.broadcasted_iota(jnp.int32, (LANES // 8, LANES), 0)
    return jnp.where((lane // 8 == entry) & (lane % 8 < count_row), 1.0, 0.0)


def capacity_of(slots, owners):
    return max(16, -(-2 * slots // owners // 16) * 16)


def ones_where(condition):
    return jnp.where(condition, 1.0, 0.0).astype(BF16)


def iota(shape, axis):
    return lax.broadcasted_iota(jnp.int32, shape, axis)


def positions(used):
    rows = min(LANES, used.shape[0])
    chunks = used.shape[0] // rows
    through = ones_where(iota((LANES, LANES), 0) <= iota((LANES, LANES), 1))
    above = ones_where(
        (iota((rows, rows), 0) // 8 == iota((rows, rows), 1) // 8) & (iota((rows, rows), 1) < iota((rows, rows), 0)))
    every = jnp.ones((LANES, LANES), BF16)
    out = []
    for chunk in range(chunks):
        part = used[chunk * rows:(chunk + 1) * rows, :].astype(BF16)
        before = dot_nn(dot_nn(above, part).astype(BF16), every)
        out.append(dot_nn(part, through) + before)
    return jnp.concatenate(out, axis=0)


def in_round(place, used, turn, capacity):
    place = place - (turn * capacity).astype(F32)
    return jnp.where((used > 0) & (place >= 1) & (place <= capacity), place, 0.0)


def owner_plan(ids_all, picks, used_rows, base, span, turn, capacity, lists):
    slots = ids_all.shape[2]
    blocks = -(-span // LANES)

    def count(d, carry):
        rel = ids_all[d // 2, pl.ds(lax.rem(d, 2), 1), :] - base
        high = jnp.where((rel >= 0) & (rel < span), rel >> 7, -1)
        counts = dot_nt(ones_where(iota((8, slots), 0) == high), ones_where(iota((LANES, slots), 0) == (rel & 127)))
        used_rows[pl.ds(pl.multiple_of(d * 8, 8), 8), :] = jnp.where(counts > 0, 1.0, 0.0)
        return carry

    lax.fori_loop(0, lists, count, 0)
    used = used_rows[pl.ds(0, lists * 8), :]
    used_rows[pl.ds(0, lists * 8), :] = in_round(positions(used), used, turn, capacity)

    def spread(d, carry):
        place = used_rows[pl.ds(pl.multiple_of(d * 8, 8), 8), :]
        wanted = (iota((capacity, LANES), 0) + 1).astype(F32)
        for block in range(blocks):
            picks[pl.ds(pl.multiple_of(d * capacity, 16), capacity), block * LANES:(block + 1) * LANES] = ones_where(
                place[block:block + 1, :] == wanted)
        return carry

    lax.fori_loop(0, lists, spread, 0)


def slot_codes(ids_row, span, first):
    value = ids_row.astype(F32)
    owner = jnp.floor((value + 0.5) * (1.0 / span))
    rel = value - owner * span
    high = jnp.floor(rel * (1.0 / LANES))
    owner = owner - first
    return owner, owner * 8 + high, rel - high * LANES


def owner_counts(ids_row, span, first, owners):
    slots = ids_row.shape[1]
    owner, row, lane = slot_codes(ids_row, span, first.astype(F32))
    rows = ones_where(iota((owners * 8, slots), 0).astype(F32) == row)
    lanes = ones_where(iota((LANES, slots), 0).astype(F32) == lane)
    return owner, rows, lanes, jnp.where(dot_nt(rows, lanes) > 0, 1.0, 0.0)


def slot_plan(ids_row, match, span, first, owners, turn, capacity):
    slots = ids_row.shape[1]
    owner, rows, lanes, used = owner_counts(ids_row, span, first, owners)
    place = in_round(positions(used), used, turn, capacity)
    mine = jnp.sum(dot_tn(place.astype(BF16), rows) * lanes.astype(F32), axis=0, keepdims=True)
    target = jnp.where(mine > 0, owner * capacity + mine - 1, -1.0)
    for owner_at in range(0, owners, 4):
        index = (iota((4 * capacity, slots), 0) + owner_at * capacity).astype(F32)
        match[owner_at * capacity:(owner_at + 4) * capacity, :] = ones_where(index == target)


def most_distinct(ids_all, span, owners, lists):
    def one(d, most):
        _, _, _, used = owner_counts(ids_all[d // 2, pl.ds(lax.rem(d, 2), 1), :], span, jnp.int32(0), owners)
        per_row = jnp.sum(used, axis=1, keepdims=True)
        per_owner = jnp.sum(per_row.reshape(owners, 8, 1), axis=1)
        return jnp.maximum(most, jnp.max(per_owner))

    return lax.fori_loop(0, lists, one, jnp.float32(0))


def device_at(index, columns):
    return (index // columns, lax.rem(index, columns))


def remote(src, dst, send, recv, peer):
    return pltpu.make_async_remote_copy(src, dst, send, recv, device_id=peer, device_id_type=MESH)


def lookup_rounds(columns, me, packed, landed, send, recv):
    lists, owners = 2 * columns, 4 * columns

    def target(d):
        return lax.rem(d, 2) * columns + d // 2

    def copy(d):
        return remote(packed.at[d], landed.at[me], send.at[d], recv.at[me], device_at(target(d), columns))

    def start(i, carry):
        d = lax.rem(i + 2 * lax.rem(me, columns), lists)

        @pl.when(target(d) != me)
        def _():
            copy(d).start()

        @pl.when(target(d) == me)
        def _():
            landed[me] = packed[d]
        return carry

    def arrive(o, carry):
        @pl.when(o != me)
        def _():
            remote(packed.at[0], landed.at[o], send.at[0], recv.at[o], device_at(o, columns)).wait_recv()
        return carry

    def left(d, carry):
        @pl.when(target(d) != me)
        def _():
            copy(d).wait_send()
        return carry

    return (lambda: lax.fori_loop(0, lists, start, 0), lambda: lax.fori_loop(0, owners, arrive, 0),
            lambda: lax.fori_loop(0, lists, left, 0))


def return_rounds(columns, me, parts, landed, send, recv):
    lists, owners = 2 * columns, 4 * columns
    slot = lax.rem(me, columns) * 2 + me // columns

    def copy(o):
        return remote(parts.at[o], landed.at[slot], send.at[o], recv.at[slot], device_at(o, columns))

    def start(i, carry):
        o = lax.rem(i + me, owners)

        @pl.when(o != me)
        def _():
            copy(o).start()

        @pl.when(o == me)
        def _():
            landed[slot] = parts[me]
        return carry

    def arrive(d, carry):
        source = lax.rem(d, 2) * columns + d // 2

        @pl.when(source != me)
        def _():
            remote(parts.at[0], landed.at[d], send.at[0], recv.at[d], device_at(source, columns)).wait_recv()
        return carry

    def left(o, carry):
        @pl.when(o != me)
        def _():
            copy(o).wait_send()
        return carry

    return (lambda: lax.fori_loop(0, owners, start, 0), lambda: lax.fori_loop(0, lists, arrive, 0),
            lambda: lax.fori_loop(0, owners, left, 0))


def greet_all(columns, me, others):
    barrier = pltpu.get_barrier_semaphore()

    def greet(o, carry):
        @pl.when(o != me)
        def _():
            pl.semaphore_signal(barrier, inc=1, device_id=device_at(o, columns), device_id_type=MESH)
        return carry

    lax.fori_loop(0, others, greet, 0)
    return barrier


def pack_rows(table, padded, picks, packed, span, capacity, lists):
    padded[pl.ds(0, span), :] = table[...]
    for d in range(0, lists, 4):
        rows = dot_nn(picks[d * capacity:(d + 4) * capacity, :], padded[...]).astype(BF16)
        packed[d:d + 4] = rows.reshape(4, capacity, rows.shape[1])


def lookup_kernel(
    columns, capacity,
    ids, table, cot_in, proj, vocab, gain_in, shift_in, bias_in, qkv_in, out_in, up_in, down_in,
    x_out, picks, ids_all, most_out, pool_out, gain_all, shift_all, bias_all, qkv_all, out_all, up_all, down_all,
    match, used_rows, padded, packed, landed, pool_send, pool_parts,
    i_send, i_recv, t_send, t_recv, w_send, w_recv, g_send, g_recv,
):
    section = lax.axis_index("section")
    column = lax.axis_index("dp")
    core = lax.rem(section, 2)
    me = section * columns + column
    owners, lists = 4 * columns, 2 * columns
    span, width = table.shape
    entries = cot_in.shape[0]
    core_peer = (section + 1 - 2 * core, column)
    barrier = greet_all(columns, me, owners)
    ids_all[column] = ids[...]
    padded[...] = jnp.zeros_like(padded)
    pl.semaphore_wait(barrier, owners - 1)

    def ids_copy(d):
        return remote(ids, ids_all.at[column], i_send.at[d - 1], i_recv.at[column],
                      (section, lax.rem(column + d, columns)))

    for d in range(1, columns):
        ids_copy(d).start()
    pairs = ((gain_in, gain_all), (shift_in, shift_all), (bias_in, bias_all),
             (qkv_in, qkv_all), (out_in, out_all), (up_in, up_all), (down_in, down_all))
    weight_copies = [
        remote(src, dst, w_send.at[i], w_recv.at[i], core_peer) for i, (src, dst) in enumerate(pairs)]
    for copy in weight_copies:
        copy.start()

    position = column * entries + iota((entries, cot_in.shape[1]), 0)
    cot = jnp.where(position < vocab[0], cot_in[...].astype(F32), 0.0).astype(BF16)
    part = dot_nt(cot, proj[...]).astype(BF16)
    pool_send[...] = part.reshape(2, entries // 2, width)

    def pool_copy(k):
        return remote(pool_send.at[k], pool_parts.at[section], g_send.at[k], g_recv.at[section], (2 + k, column))

    for k in range(2):
        @pl.when(section != 2 + k)
        def _(k=k):
            pool_copy(k).start()

        @pl.when(section == 2 + k)
        def _(k=k):
            pool_parts[section] = pool_send[k]

    for d in range(1, columns):
        source = lax.rem(column + d, columns)
        remote(ids, ids_all.at[source], i_send.at[d - 1], i_recv.at[source], (section, source)).wait_recv()
    turn = jnp.int32(0)
    owner_plan(ids_all, picks, used_rows, me * span, span, turn, capacity, lists)
    pack_rows(table, padded, picks, packed, span, capacity, lists)
    start, arrive, left = lookup_rounds(columns, me, packed, landed, t_send, t_recv)
    start()

    @pl.when(section < 2)
    def _():
        slot_plan(ids_all[column, pl.ds(core, 1), :], match, span, jnp.int32(0), owners, turn, capacity)

    most_out[...] = jnp.full(most_out.shape, most_distinct(ids_all, span, owners, lists), F32)

    @pl.when(section >= 2)
    def _():
        total = pool_parts[section].astype(F32)
        for d in range(1, 4):
            source = lax.rem(section + d, 4)
            remote(pool_send.at[0], pool_parts.at[source], g_send.at[0], g_recv.at[source],
                   (source, column)).wait_recv()
            total = total + pool_parts[source].astype(F32)
        pool_out[...] = total

    @pl.when(section < 2)
    def _():
        arrive()
        x_out[...] = dot_tn(match[...], landed[...].reshape(owners * capacity, width)).astype(BF16)

    left()
    for k in range(2):
        @pl.when(section != 2 + k)
        def _(k=k):
            pool_copy(k).wait_send()
    for d in range(1, columns):
        ids_copy(d).wait_send()
    for copy in weight_copies:
        copy.wait()


def lookup(columns, ids, table, cot, proj, vocab, gain, shift, bias, w_qkv, w_out, w_up, w_down):
    slots = ids.shape[1]
    span, width = table.shape
    owners, lists = 4 * columns, 2 * columns
    capacity = capacity_of(slots, owners)
    padded_span = -(-span // LANES) * LANES
    entries = cot.shape[0]
    vmem = pl.BlockSpec(memory_space=pltpu.VMEM)
    smem = pl.BlockSpec(memory_space=pltpu.SMEM)
    hbm = pl.BlockSpec(memory_space=pl.ANY)
    shape = jax.ShapeDtypeStruct
    params = (gain, shift, bias, w_qkv, w_out, w_up, w_down)
    outs = [
        shape((slots, width), BF16), shape((lists * capacity, padded_span), BF16), shape((columns, 2, slots), jnp.int32), shape((8, LANES), F32),
        shape((entries // 2, width), F32),
    ] + [shape(p.shape, p.dtype) for p in params]
    sem = pltpu.SemaphoreType.DMA
    return pl.pallas_call(
        functools.partial(lookup_kernel, columns, capacity),
        out_shape=outs,
        in_specs=[vmem] * 4 + [smem] + [hbm] * 7,
        out_specs=[vmem] * 5 + [hbm] * 7,
        scratch_shapes=[
            pltpu.VMEM((owners * capacity, slots), BF16),
            pltpu.VMEM((max(lists, owners) * 8, LANES), F32), pltpu.VMEM((padded_span, width), BF16),
            pltpu.VMEM((lists, capacity, width), BF16), pltpu.VMEM((owners, capacity, width), BF16),
            pltpu.VMEM((2, entries // 2, width), BF16), pltpu.VMEM((4, entries // 2, width), BF16),
            sem((columns - 1,)), sem((columns,)), sem((lists,)), sem((owners,)), sem((7,)), sem((7,)),
            sem((2,)), sem((4,)),
        ],
        compiler_params=pltpu.CompilerParams(collective_id=3, has_side_effects=True, vmem_limit_bytes=VMEM_BYTES),
    )(ids, table, cot, proj, vocab, *params)


def more_lookup_kernel(columns, capacity, turn, ids_all, table, x_out, match, picks, used_rows, padded, packed, landed,
                       t_send, t_recv):
    section = lax.axis_index("section")
    column = lax.axis_index("dp")
    me = section * columns + column
    owners, lists = 4 * columns, 2 * columns
    span, width = table.shape
    barrier = pltpu.get_barrier_semaphore()

    @pl.when(section < 2)
    def _():
        greet_all(columns, me, owners)
        pl.semaphore_wait(barrier, lists - 1)

    @pl.when(section >= 2)
    def _():
        pl.semaphore_wait(barrier, lists)

    padded[...] = jnp.zeros_like(padded)
    owner_plan(ids_all, picks, used_rows, me * span, span, turn[0], capacity, lists)
    pack_rows(table, padded, picks, packed, span, capacity, lists)
    start, arrive, left = lookup_rounds(columns, me, packed, landed, t_send, t_recv)
    start()
    x_out[...] = jnp.zeros_like(x_out)

    @pl.when(section < 2)
    def _():
        slot_plan(ids_all[column, pl.ds(lax.rem(section, 2), 1), :], match, span, jnp.int32(0), owners, turn[0], capacity)
        arrive()
        x_out[...] = dot_tn(match[...], landed[...].reshape(owners * capacity, width)).astype(BF16)

    left()


def more_lookup(columns, turn, ids_all, table):
    slots = ids_all.shape[2]
    span, width = table.shape
    owners, lists = 4 * columns, 2 * columns
    capacity = capacity_of(slots, owners)
    padded_span = -(-span // LANES) * LANES
    vmem = pl.BlockSpec(memory_space=pltpu.VMEM)
    sem = pltpu.SemaphoreType.DMA
    return pl.pallas_call(
        functools.partial(more_lookup_kernel, columns, capacity),
        out_shape=jax.ShapeDtypeStruct((slots, width), BF16),
        in_specs=[pl.BlockSpec(memory_space=pltpu.SMEM), vmem, vmem],
        out_specs=vmem,
        scratch_shapes=[
            pltpu.VMEM((owners * capacity, slots), BF16), pltpu.VMEM((lists * capacity, padded_span), BF16),
            pltpu.VMEM((max(lists, owners) * 8, LANES), F32), pltpu.VMEM((padded_span, width), BF16),
            pltpu.VMEM((lists, capacity, width), BF16), pltpu.VMEM((owners, capacity, width), BF16),
            sem((lists,)), sem((owners,)),
        ],
        compiler_params=pltpu.CompilerParams(collective_id=4, has_side_effects=True, vmem_limit_bytes=VMEM_BYTES),
    )(turn, ids_all, table)


def return_parts(match, dx, parts, owners, capacity):
    for o in range(0, owners, 4):
        rows = dot_nn(match[o * capacity:(o + 4) * capacity, :], dx[...]).astype(BF16)
        parts[o:o + 4] = rows.reshape(4, capacity, rows.shape[1])


def more_return_kernel(columns, capacity, turn, ids_all, dx, held, grad_out, match, picks, used_rows, parts, landed,
                       t_send, t_recv):
    section = lax.axis_index("section")
    column = lax.axis_index("dp")
    me = section * columns + column
    owners, lists = 4 * columns, 2 * columns
    span, width = held.shape
    slots = ids_all.shape[2]
    barrier = greet_all(columns, me, lists)

    @pl.when(section < 2)
    def _():
        pl.semaphore_wait(barrier, owners - 1)

    start, arrive, left = return_rounds(columns, me, parts, landed, t_send, t_recv)

    @pl.when(section < 2)
    def _():
        slot_plan(ids_all[column, pl.ds(lax.rem(section, 2), 1), :], match, span, jnp.int32(0), owners, turn[0], capacity)
        return_parts(match, dx, parts, owners, capacity)
        start()

    owner_plan(ids_all, picks, used_rows, me * span, span, turn[0], capacity, lists)
    arrive()
    grad = dot_tn(picks[...], landed[...].reshape(lists * capacity, width))
    grad_out[...] = held[...] + grad[:span]

    @pl.when(section < 2)
    def _():
        left()


def more_return(columns, turn, ids_all, dx, held):
    slots = ids_all.shape[2]
    span, width = held.shape
    owners, lists = 4 * columns, 2 * columns
    capacity = capacity_of(slots, owners)
    padded_span = -(-span // LANES) * LANES
    vmem = pl.BlockSpec(memory_space=pltpu.VMEM)
    sem = pltpu.SemaphoreType.DMA
    return pl.pallas_call(
        functools.partial(more_return_kernel, columns, capacity),
        out_shape=jax.ShapeDtypeStruct((span, width), F32),
        in_specs=[pl.BlockSpec(memory_space=pltpu.SMEM), vmem, vmem, vmem],
        out_specs=vmem,
        scratch_shapes=[
            pltpu.VMEM((owners * capacity, slots), BF16), pltpu.VMEM((lists * capacity, padded_span), BF16),
            pltpu.VMEM((max(lists, owners) * 8, LANES), F32),
            pltpu.VMEM((owners, capacity, width), BF16), pltpu.VMEM((lists, capacity, width), BF16),
            sem((owners,)), sem((lists,)),
        ],
        compiler_params=pltpu.CompilerParams(collective_id=5, has_side_effects=True, vmem_limit_bytes=VMEM_BYTES),
    )(turn, ids_all, dx, held)


PHASE_LAG = 2
PROJECT_AFTER = 5
ADD_LAG = 2
VEC_GAP = 3
SEND_NEAR = 1
SEND_FAR = 8
TABLE_STEP = 13
SWAPPED = (3, 7, 11)


def unit_order(u, bits):
    order = list(range(bits))
    if u in SWAPPED and bits > 1:
        order[0], order[1] = 1, 0
    return order


def slot_in(order, q):
    slot = 0
    for bit in order:
        slot = slot * 2 + (q >> bit) % 2
    return slot


def trunk_kernel(columns, width, hidden, micros, *refs):
    (x0, counts, pool_grad), refs = refs[:3], refs[3:]
    own, theirs, refs = refs[:7], refs[7:14], refs[14:]
    (cot_in, proj, picks, ids_all, vocab), refs = refs[:5], refs[5:]
    (emb_out, gain_out, shift_out, upb_out, qkv_out, out_out, up_out, down_out, proj_out, table_out, dx_out), refs = (
        refs[:11], refs[11:])
    bits = columns.bit_length() - 1
    recv, refs = refs[:bits], refs[bits:]
    (gains, shifts, up_bias, w_all, a, dqkv, att, dbr, h_in_all, dpre, act_all, dy_all,
     x_in, x_mid, resid, prob, y_out, dy_in, vec, upb, pooled,
     wide, s0_recv, proj_sums, v_buf, pool_all, cot, match, dxs, parts, landed,
     f_send, f_recv, b_send, b_recv, p_sem,
     c_send, c_recv, h_send, h_recv, v_send, v_recv, q_send, q_recv, t_send, t_recv, d_send, d_recv) = refs
    section = lax.axis_index("section")
    column = lax.axis_index("dp")
    core = lax.rem(section, 2)
    stage = section // 2
    core_peer = (section + 1 - 2 * core, column)
    far_peer = (lax.rem(section + 2, 4), column)
    blocks = MICRO // LANES
    score_scale = (width // HEADS) ** (-0.5)
    piece = width // columns
    tiles = hidden // width
    units = 4 + 2 * tiles
    first_down = 4 + tiles
    capacity = parts.shape[1] // 2
    lists = 2 * columns

    def tile_of(source, u):
        if u < 3:
            return source[3].at[0, :, u * width:(u + 1) * width]
        if u == 3:
            return source[4].at[0]
        if u < first_down:
            return source[5].at[0, :, (u - 4) * width:(u - 3) * width]
        return source[6].at[0, (u - first_down) * width:(u - first_down + 1) * width, :]

    def fetch(i, source, layer):
        src = source[i].at[0] if i < 3 else tile_of(source, i - 3)
        dst = (gains, shifts, up_bias)[i].at[layer] if i < 3 else w_all.at[layer, i - 3]
        return pltpu.make_async_copy(src, dst, p_sem.at[i, layer])

    for first in range(2):
        @pl.when(core == first)
        def _(first=first):
            for layer in range(2):
                for i in (0, 1, 3, 4, 5, 6, 2, *range(7, 3 + units)):
                    fetch(i, own if layer == first else theirs, layer).start()

    def need(m, layer, *indices):
        @pl.when(m == 0)
        def _():
            for i in indices:
                fetch(i, own, layer).wait()

    def section_peer(d):
        return (lax.rem(section + d, 4), column)

    def column_peer(d):
        return (section, lax.rem(column + d, columns))

    peers = [section_peer(d) for d in range(1, 4)] + [column_peer(d) for d in range(1, columns)]
    barrier = pltpu.get_barrier_semaphore()
    for peer in peers:
        pl.semaphore_signal(barrier, inc=1, device_id=peer, device_id_type=MESH)
    vec[...] = jnp.zeros_like(vec)
    upb[...] = jnp.zeros_like(upb)

    @pl.when(stage == 0)
    def _():
        x_in[...] = x0[...]

    pl.semaphore_wait(barrier, len(peers))

    def rows_of(m):
        return pl.ds(pl.multiple_of(m * MICRO, MICRO), MICRO)

    def forward_copy(m):
        return remote(y_out.at[rows_of(m)], x_in.at[rows_of(m)], f_send.at[m], f_recv.at[m], far_peer)

    def backward_copy(m):
        return remote(y_out.at[rows_of(m)], dy_in.at[rows_of(m)], b_send.at[m], b_recv.at[m], far_peer)

    def count_row(m, b):
        return counts[pl.ds(m * blocks + b, 1), :]

    def layer_forward(layer, m, x):
        rows = rows_of(m)
        masks, halves = entry_masks(), half_masks()
        xf = x.astype(F32)
        normed, _ = statistics(xf)
        need(m, layer, 0, 1, 3, 4, 5)
        a_low = (normed * gains[layer, pl.ds(0, 1), :] + shifts[layer, pl.ds(0, 1), :]).astype(BF16)
        a[layer, rows, :] = a_low
        for t in range(3):
            cols = slice(t * width, (t + 1) * width)
            dqkv[layer, rows, cols] = dot_nn(a_low, w_all[layer, t]).astype(BF16)
        for b in range(blocks):
            block = pl.ds(pl.multiple_of(m * MICRO + b * LANES, LANES), LANES)
            keys_on = head_mask(count_row(m, b))
            for pair in range(HEADS // 2):
                cols = slice(pair * LANES, (pair + 1) * LANES)
                q = dqkv[layer, block, cols]
                k = dqkv[layer, block, slice(width + pair * LANES, width + (pair + 1) * LANES)]
                v = dqkv[layer, block, slice(2 * width + pair * LANES, 2 * width + (pair + 1) * LANES)]
                flats = compress(dot_nt(by_head(k, halves), q), masks)
                wide = []
                for h in range(2):
                    s = jnp.where(keys_on, flats[h] * score_scale, MASKED)
                    e = jnp.exp(s - jnp.max(s, axis=0, keepdims=True))
                    p = e / jnp.sum(e, axis=0, keepdims=True)
                    prob[layer, m * blocks + b, pl.ds((2 * pair + h) * 8, 8), :] = p
                    wide.append(expand(p, masks))
                mixed = dot_tn(jnp.concatenate(wide, axis=0), by_head(v, halves))
                att[layer, block, cols] = mixed.astype(BF16)
        need(m, layer, 6)
        res = xf + dot_nn(att[layer, rows, :], w_all[layer, 3]) + shifts[layer, pl.ds(1, 1), :]
        resid[layer, rows, :] = res
        normed_two, _ = statistics(res)
        h_in = (normed_two * gains[layer, pl.ds(1, 1), :] + shifts[layer, pl.ds(2, 1), :]).astype(BF16)
        h_in_all[layer, rows, :] = h_in
        need(m, layer, 2, *range(7, 3 + units))
        total = res + shifts[layer, pl.ds(3, 1), :]
        for t in range(tiles):
            cols = slice(t * width, (t + 1) * width)
            pre = dot_nn(h_in, w_all[layer, 4 + t]) + up_bias[layer, :, cols]
            dpre[layer, rows, cols] = pre.astype(BF16)
            act = (pre * (0.5 * (1.0 + lax.erf(pre * ROOT_HALF)))).astype(BF16)
            total = total + dot_nn(act, w_all[layer, first_down + t])
        return total.astype(BF16)

    def layer_backward(layer, m, dy):
        rows = rows_of(m)
        masks, halves = entry_masks(), half_masks()
        dyf = dy.astype(F32)
        vec[layer, pl.ds(5, 1), :] += column_sum(dyf)
        d_hidden = jnp.zeros((MICRO, width), F32)
        for t in range(tiles):
            cols = slice(t * width, (t + 1) * width)
            d_act = dot_nt(dy, w_all[layer, first_down + t])
            pre = dpre[layer, rows, cols].astype(F32)
            phi = 0.5 * (1.0 + lax.erf(pre * ROOT_HALF))
            density = jnp.exp(-0.5 * pre * pre) * DENSITY_SCALE
            act_all[layer, rows, cols] = (pre * phi).astype(BF16)
            d_pre = (d_act * (phi + pre * density)).astype(BF16)
            dpre[layer, rows, cols] = d_pre
            upb[layer, :, cols] += column_sum(d_pre.astype(F32))
            d_hidden = d_hidden + dot_nt(d_pre, w_all[layer, 4 + t])
        normed_two, inverse_two = statistics(resid[layer, rows, :])
        vec[layer, pl.ds(1, 1), :] += column_sum(d_hidden * normed_two)
        vec[layer, pl.ds(4, 1), :] += column_sum(d_hidden)
        d_resid = dyf + norm_backward(d_hidden * gains[layer, pl.ds(1, 1), :], normed_two, inverse_two)
        d_branch = d_resid.astype(BF16)
        dbr[layer, rows, :] = d_branch
        vec[layer, pl.ds(3, 1), :] += column_sum(d_branch.astype(F32))
        d_att = dot_nt(d_branch, w_all[layer, 3]).astype(BF16)
        for b in range(blocks):
            block = pl.ds(pl.multiple_of(m * MICRO + b * LANES, LANES), LANES)
            for pair in range(HEADS // 2):
                c_q = slice(pair * LANES, (pair + 1) * LANES)
                c_k = slice(width + pair * LANES, width + (pair + 1) * LANES)
                c_v = slice(2 * width + pair * LANES, 2 * width + (pair + 1) * LANES)
                q = dqkv[layer, block, c_q]
                k = dqkv[layer, block, c_k]
                v = dqkv[layer, block, c_v]
                da = d_att[b * LANES:(b + 1) * LANES, c_q]
                flats = compress(dot_nt(by_head(v, halves), da), masks)
                wide_p, wide_s = [], []
                for h in range(2):
                    p = prob[layer, m * blocks + b, pl.ds((2 * pair + h) * 8, 8), :]
                    ds = p * (flats[h] - jnp.sum(flats[h] * p, axis=0, keepdims=True))
                    wide_p.append(expand(p, masks))
                    wide_s.append(expand(ds, masks))
                d_v = dot_nn(jnp.concatenate(wide_p, axis=1), by_head(da, halves))
                d_k = dot_nn(jnp.concatenate(wide_s, axis=1), by_head(q, halves)) * score_scale
                d_q = dot_tn(jnp.concatenate(wide_s, axis=0), by_head(k, halves)) * score_scale
                dqkv[layer, block, c_q] = d_q.astype(BF16)
                dqkv[layer, block, c_k] = d_k.astype(BF16)
                dqkv[layer, block, c_v] = d_v.astype(BF16)
        d_a = jnp.zeros((MICRO, width), F32)
        for t in range(3):
            cols = slice(t * width, (t + 1) * width)
            d_a = d_a + dot_nt(dqkv[layer, rows, cols], w_all[layer, t])
        x = jnp.where(layer == 0, x_in[rows, :], x_mid[rows, :])
        normed, inverse = statistics(x.astype(F32))
        vec[layer, pl.ds(0, 1), :] += column_sum(d_a * normed)
        vec[layer, pl.ds(2, 1), :] += column_sum(d_a)
        dx = d_resid + norm_backward(d_a * gains[layer, pl.ds(0, 1), :], normed, inverse)
        return dx.astype(BF16)


    def forward_layer(layer, m, x):
        @pl.when(layer == 1)
        def _():
            x_mid[rows_of(m), :] = x

        return layer_forward(layer, m, x)

    def forward_step(m, carry):
        rows = rows_of(m)

        @pl.when(stage == 1)
        def _():
            forward_copy(m).wait_recv()

        x = lax.fori_loop(0, 2, lambda layer, x: forward_layer(layer, m, x), x_in[rows, :])
        y_out[rows, :] = x

        @pl.when(stage == 0)
        def _():
            forward_copy(m).start()

        @pl.when(stage == 1)
        def _():
            for b in range(blocks):
                matrix = pool_matrix(count_row(m, b))
                summed = dot_nn(matrix.astype(BF16), x[b * LANES:(b + 1) * LANES, :])
                mean = summed / jnp.sum(matrix, axis=1, keepdims=True)
                entries = pl.ds(pl.multiple_of((m * blocks + b) * (LANES // 8), LANES // 8), LANES // 8)
                pooled[entries, :] = mean.astype(BF16)
        return carry

    lax.fori_loop(0, micros, forward_step, 0)

    def my_bit(b):
        return lax.rem(column // (1 << b), 2)

    def bit_peer(b):
        return (section, column + (1 << b) - my_bit(b) * (2 << b))

    def pool_copy(d):
        return remote(pooled, pool_all.at[core], q_send.at[d - 1], q_recv.at[core], section_peer(d))

    def pool_arrival(k):
        return remote(pooled, pool_all.at[k], q_send.at[0], q_recv.at[k], core_peer)

    @pl.when(stage == 1)
    def _():
        for d in range(1, 4):
            pool_copy(d).start()
        pool_all[core] = pooled[...]

    @pl.when(stage == 0)
    def _():
        for m in range(micros):
            forward_copy(m).wait_send()

    def core_copy(u):
        return remote(w_all.at[1 - core, u], s0_recv.at[u], c_send.at[u], c_recv.at[u], core_peer)

    def is_wide(k):
        return k < bits and (columns >> (k + 1)) * piece < 16

    def source_of(u, k):
        if is_wide(k):
            return wide.at[u]
        if k > 0:
            return recv[k - 1].at[u]
        return w_all.at[core, u] if u < units else proj_sums

    def side_rows(k, side):
        size = (columns >> (k + 1)) * piece
        return pl.ds(pl.multiple_of(side * size, size), size)

    def halving_copy(u, k):
        bit = unit_order(u, bits)[k]
        return remote(source_of(u, k).at[side_rows(k, 1 - my_bit(bit))], recv[k].at[u], h_send.at[k, u],
                      h_recv.at[k, u], bit_peer(bit))

    def absorb(u, k):
        halving_copy(u, k).wait_recv()
        bit = unit_order(u, bits)[k]
        return recv[k][u].astype(F32) + source_of(u, k)[side_rows(k, my_bit(bit)), :].astype(F32)

    def advance(u, k):
        if k < bits - 1:
            if is_wide(k + 1):
                wide[u] = absorb(u, k)
            else:
                recv[k][u] = absorb(u, k).astype(BF16)
            halving_copy(u, k + 1).start()
        else:
            finish(u, absorb(u, k))

    def cut(value, q):
        return value[q * piece:(q + 1) * piece, :]

    def rows_at(u, q):
        slot = slot_in(unit_order(u, bits), q)
        return slice(slot * piece, (slot + 1) * piece)

    def product(layer, u):
        if u < 3:
            return dot_tn(a[layer], dqkv[layer, :, u * width:(u + 1) * width])
        if u == 3:
            return dot_tn(att[layer], dbr[layer])
        t = u - 4
        return dot_tn(h_in_all[layer], dpre[layer, :, t * width:(t + 1) * width])

    def send_or_add(layer, u):
        @pl.when(core != layer)
        def _():
            core_copy(u).start()

        if u >= ADD_LAG:
            @pl.when(core == layer)
            def _():
                add_own(u - ADD_LAG)

    def add_own(u):
        core_copy(u).wait_recv()
        w_all[core, u] = (w_all[core, u].astype(F32) + s0_recv[u].astype(F32)).astype(BF16)
        halving_copy(u, 0).start()

    def weight_gradients(layer):
        for u in range(first_down):
            value = product(layer, u).astype(BF16)
            for q in range(columns):
                w_all[layer, u, rows_at(u, q), :] = cut(value, q)
            send_or_add(layer, u)
        for i in range(tiles):
            value = dot_tn(act_all[layer, :, i * width:(i + 1) * width], dy_all[layer]).astype(BF16)
            for j in range(columns):
                u, q = first_down + j % tiles, i * columns // tiles + j // tiles
                w_all[layer, u, rows_at(u, q), :] = cut(value, j)
        for u in range(first_down, units):
            send_or_add(layer, u)

        @pl.when(core == layer)
        def _():
            for u in range(units - ADD_LAG, units):
                add_own(u)

    def project():
        @pl.when(section >= 2)
        def _():
            pool_arrival(1 - core).wait_recv()

        @pl.when(section < 2)
        def _():
            pool_arrival(0).wait_recv()
            pool_arrival(1).wait_recv()

        entries = cot_in.shape[0]
        position = column * entries + iota((entries, cot_in.shape[1]), 0)
        live = position < vocab[0]
        cot[...] = jnp.where(live, cot_in[...].astype(F32), 0.0).astype(BF16)
        rows = pool_all[...].reshape(entries, width)
        emb_out[...] = jnp.where(live, dot_nn(rows, proj[...]), 0.0)
        value = dot_tn(rows, cot[...]).astype(BF16)
        for q in range(columns):
            proj_sums[rows_at(units, q), :] = cut(value, q)

        halving_copy(units, 0).start()

    def project_now():
        project()
        for k in range(bits):
            advance(units, k)

    def put_vec(slot, layer):
        v_buf[slot, :, slice(0, width)] = vec[layer]
        for t in range(2):
            v_buf[slot, pl.ds(6 + t, 1), :] = upb[layer, :, t * (hidden // 2):(t + 1) * (hidden // 2)]

    def vec_copy(src, index, peer):
        return remote(v_buf.at[src], v_buf.at[index], v_send.at[index], v_recv.at[index], peer)

    def vec_peer_copy(k):
        return vec_copy(1 + 2 * k + (k > 0), 3 + 2 * k, bit_peer(k))

    def share_copy(half, way, peer):
        return remote(dxs.at[half], dxs.at[half], d_send.at[way], d_recv.at[half], peer)

    def finish(u, total):
        if u < 3:
            qkv_out[0, :, u * width:(u + 1) * width] = total
        elif u == 3:
            out_out[0] = total
        elif u < first_down:
            up_out[0, :, (u - 4) * width:(u - 3) * width] = total
        elif u < units:
            t = u - first_down
            down_out[0, t * piece:(t + 1) * piece, :] = total
        else:
            proj_out[...] = total

    def vec_step(k):
        if k == 0:
            put_vec(0, 1 - core)
            put_vec(1, core)
            vec_copy(0, 2, core_peer).start()
            vec_copy(0, 2, core_peer).wait_recv()
            v_buf[1] = v_buf[1] + v_buf[2]
            vec_peer_copy(0).start()
            return
        vec_peer_copy(k - 1).wait_recv()
        source = 1 + 2 * (k - 1) + (k > 1)
        total = v_buf[source] + v_buf[3 + 2 * (k - 1)]
        if k < bits:
            v_buf[2 * k + 2] = total
            vec_peer_copy(k).start()
            return
        lanes = width // columns
        share = hidden // columns
        for q in range(columns):
            @pl.when(column == q)
            def _(q=q):
                gain_out[0] = total[0:2, q * lanes:(q + 1) * lanes]
                shift_out[0] = total[2:6, q * lanes:(q + 1) * lanes]
                row, start = divmod(q * share, hidden // 2)
                upb_out[...] = total[6 + row:7 + row, start:start + share]

    def table_copy(d):
        peer = column_peer(d)
        return remote(parts.at[peer[1]], landed.at[column], t_send.at[d - 1], t_recv.at[column], peer)

    def table_parts():
        share_copy(1 - core, 0, core_peer).wait_recv()
        for half in range(2):
            slot_plan(ids_all[column, pl.ds(half, 1), :], match, table_out.shape[0], section * columns, columns,
                      jnp.int32(0), capacity)
            rows = dot_nn(match[...], dxs[half]).astype(BF16)
            parts[:, half * capacity:(half + 1) * capacity, :] = rows.reshape(columns, capacity, width)
        for d in range(1, columns):
            table_copy(d).start()
        landed[column] = parts[column]

    def table_finish():
        for d in range(1, columns):
            source = lax.rem(column + d, columns)
            remote(parts.at[0], landed.at[source], t_send.at[0], t_recv.at[source], (section, source)).wait_recv()
        grad = dot_tn(picks[...], landed[...].reshape(lists * capacity, width))
        table_out[...] = grad[:table_out.shape[0]]

    pl.when(stage == 0)(project_now)

    def seed(m):
        rows = rows_of(m)

        @pl.when(stage == 0)
        def _():
            backward_copy(m).wait_recv()
            dy_all[1, rows, :] = dy_in[rows, :]

        @pl.when(stage == 1)
        def _():
            for b in range(blocks):
                matrix = pool_matrix(count_row(m, b))
                entries = pl.ds(pl.multiple_of((m * blocks + b) * (LANES // 8), LANES // 8), LANES // 8)
                share = (pool_grad[entries, :] / jnp.sum(matrix, axis=1, keepdims=True)).astype(BF16)
                block = pl.ds(pl.multiple_of(m * MICRO + b * LANES, LANES), LANES)
                dy_all[1, block, :] = dot_tn(matrix.astype(BF16), share).astype(BF16)

    def backward(layer, m):
        rows = rows_of(m)
        dx = layer_backward(layer, m, dy_all[layer, rows, :])

        @pl.when(layer == 1)
        def _():
            dy_all[0, rows, :] = dx

        @pl.when(layer == 0)
        def _():
            dx_out[rows, :] = dx
            dxs[core, rows, :] = dx

        @pl.when((layer == 0) & (stage == 1))
        def _():
            y_out[rows, :] = dx
            backward_copy(m).start()

    last = micros - 1

    def backward_step(i, carry):
        m, turn = jnp.minimum(i // 2, last), i - 2 * jnp.minimum(i // 2, last)

        @pl.when(turn == 0)
        def _():
            seed(m)

        @pl.when(turn < 2)
        def _():
            backward(1 - turn, m)

        layer = 1 - turn + stage

        @pl.when((m == last) & (turn == 1) & (stage == 0))
        def _():
            share_copy(core, 0, core_peer).start()
            share_copy(core, 1, far_peer).start()

        @pl.when((m == last) & (layer >= 0) & (layer < 2))
        def _():
            weight_gradients(layer)
        return carry

    lax.fori_loop(0, 2 * micros + 1, backward_step, 0)

    lags = [PHASE_LAG * k for k in range(bits)]
    for step in range(units + lags[-1]):
        if step == SEND_NEAR:
            pl.when(section < 2)(table_parts)
        if step == SEND_FAR - 1:
            @pl.when(section >= 2)
            def _():
                share_copy(core, 0, far_peer).wait_recv()
                share_copy(core, 0, core_peer).start()
        if step == SEND_FAR:
            pl.when(section >= 2)(table_parts)
        if step == TABLE_STEP:
            table_finish()
        if step % VEC_GAP == 0 and step // VEC_GAP <= bits:
            vec_step(step // VEC_GAP)
        if step == 0:
            pl.when(stage == 1)(project)
        for k in range(bits):
            u = step - lags[k]
            if 0 <= u < units:
                advance(u, k)
            if u == PROJECT_AFTER:
                @pl.when(stage == 1)
                def _(k=k):
                    advance(units, k)
    for k in range((units + lags[-1] - 1) // VEC_GAP + 1, bits + 1):
        vec_step(k)

    @pl.when(stage == 1)
    def _():
        for m in range(micros):
            backward_copy(m).wait_send()

    vec_copy(0, 2, core_peer).wait_send()
    for k in range(bits):
        vec_peer_copy(k).wait_send()
    for u in range(units):
        core_copy(u).wait_send()
    for u in range(units + 1):
        for k in range(bits):
            halving_copy(u, k).wait_send()
    for d in range(1, columns):
        table_copy(d).wait_send()
    share_copy(core, 0, core_peer).wait_send()

    @pl.when(section < 2)
    def _():
        share_copy(core, 1, far_peer).wait_send()

    @pl.when(section >= 2)
    def _():
        for d in range(1, 4):
            pool_copy(d).wait_send()


def trunk(columns, x0, counts, pool_grad, own, theirs, cot, proj, picks, ids_all, span, vocab):
    rows, width = x0.shape
    hidden = own[5].shape[2]
    micros = rows // MICRO
    entries, out_width = cot.shape
    piece, tiles = width // columns, hidden // width
    bits = columns.bit_length() - 1
    units = 4 + 2 * tiles
    sizes = [(columns >> (k + 1)) * piece for k in range(bits)]
    capacity = picks.shape[0] // (2 * columns)
    vmem = pl.BlockSpec(memory_space=pltpu.VMEM)
    smem = pl.BlockSpec(memory_space=pltpu.SMEM)
    hbm = pl.BlockSpec(memory_space=pl.ANY)
    shape, sem, space = jax.ShapeDtypeStruct, pltpu.SemaphoreType.DMA, pltpu.VMEM
    outs = [
        shape((entries, out_width), F32), shape((1, 2, piece), F32), shape((1, 4, piece), F32),
        shape((1, hidden // columns), F32), shape((1, piece, 3 * width), F32), shape((1, piece, width), F32),
        shape((1, piece, hidden), F32), shape((1, tiles * piece, width), F32), shape((piece, out_width), F32),
        shape((span, width), F32), shape((rows, width), BF16),
    ]
    return pl.pallas_call(
        functools.partial(trunk_kernel, columns, width, hidden, micros),
        out_shape=outs,
        in_specs=[vmem] * 3 + [hbm] * 14 + [vmem] * 4 + [smem],
        out_specs=[vmem] * len(outs),
        scratch_shapes=[space((units + 1, size, width), BF16 if size >= 16 else F32) for size in sizes] + [
            space((2,) + p.shape[1:], p.dtype) for p in own[:3]] + [
            space((2, units, width, width), BF16),
            space((2, rows, width), BF16), space((2, rows, 3 * width), BF16), space((2, rows, width), BF16),
            space((2, rows, width), BF16), space((2, rows, width), BF16), space((2, rows, hidden), BF16),
            space((2, rows, hidden), BF16), space((2, rows, width), BF16),
            space((rows, width), BF16), space((rows, width), BF16), space((2, rows, width), F32),
            space((2, rows // LANES, 8 * HEADS, LANES), F32), space((rows, width), BF16), space((rows, width), BF16),
            space((2, 8, width), F32), space((2, 1, hidden), F32), space((rows // 8, width), BF16),
            space((units + 1, 2 * piece, width) if sizes[-1] < 16 else (8, LANES), F32),
            space((units, width, width), BF16), space((width, width), BF16),
            space((3 + 2 * bits, 8, hidden // 2), F32), space((2, entries // 2, width), BF16),
            space((entries, out_width), BF16), space((columns * capacity, rows), BF16), space((2, rows, width), BF16),
            space((columns, 2 * capacity, width), BF16), space((columns, 2 * capacity, width), BF16),
            sem((micros,)), sem((micros,)), sem((micros,)), sem((micros,)), sem((3 + units, 2)),
            sem((units,)), sem((units,)), sem((bits, units + 1)), sem((bits, units + 1)),
            sem((3 + 2 * bits,)), sem((3 + 2 * bits,)), sem((3,)), sem((2,)), sem((columns - 1,)), sem((columns,)),
            sem((2,)), sem((2,)),
        ],
        compiler_params=pltpu.CompilerParams(collective_id=1, has_side_effects=True, vmem_limit_bytes=VMEM_BYTES),
    )(x0, counts, pool_grad, *own, *theirs, cot, proj, picks, ids_all, vocab)


def local(table, piece_ids, piece_counts, vocab_size, norm_gain, shift_bias, up_bias, qkv_weight, out_weight,
          up_weight, down_weight, proj_weight, embed_cotangent):
    section = lax.axis_index("section")
    columns = lax.axis_size("dp")
    core = lax.rem(section, 2)
    entries, pieces = piece_ids.shape
    half = entries // 2
    ids = piece_ids.reshape(2, half * pieces)
    my_counts = lax.dynamic_slice_in_dim(piece_counts, core * half, half, 0)
    count_rows = jnp.repeat(my_counts, pieces).reshape(-1, LANES)
    own = (norm_gain, shift_bias, up_bias[:, None, :], qkv_weight, out_weight, up_weight, down_weight)
    x0, picks, ids_all, most, pool_grad, *theirs = lookup(
        columns, ids, table, embed_cotangent, proj_weight, vocab_size, *own)
    capacity = picks.shape[0] // (2 * columns)
    turns = (most[0, 0].astype(jnp.int32) + capacity - 1) // capacity
    x0 = lax.fori_loop(
        1, turns, lambda turn, x: x + more_lookup(columns, turn.reshape(1), ids_all, table), x0)
    emb, g_gain, g_shift, g_bias, g_qkv, g_out, g_up, g_down, g_proj, g_table, dx = trunk(
        columns, x0, count_rows, pool_grad, own, theirs, embed_cotangent, proj_weight, picks, ids_all, table.shape[0],
        vocab_size)
    g_table = lax.fori_loop(
        1, turns, lambda turn, held: more_return(columns, turn.reshape(1), ids_all, dx, held), g_table)
    return emb, g_table, g_gain, g_shift, g_bias, g_qkv, g_out, g_up, g_down, g_proj


def solution(mesh):
    return jax.shard_map(
        local,
        mesh=mesh,
        in_specs=(
            P(("section", "dp"), None), P("dp", None), P("dp"), P(), P("section", None, None),
            P("section", None, None), P("section", None), P("section", None, None), P("section", None, None),
            P("section", None, None), P("section", None, None), P(None, "section"), P("dp", "section"),
        ),
        out_specs=(
            P("dp", "section"), P(("section", "dp"), None), P("section", None, "dp"), P("section", None, "dp"),
            P("section", "dp"), P("section", "dp", None), P("section", "dp", None), P("section", "dp", None),
            P("section", "dp", None), P("dp", "section"),
        ),
        check_vma=False,
    )
```

time: 1110 us -> 209 us (0.19)
  waiting for transfers between devices: 883 us -> 0 us
  Pallas kernels: 84.1 us -> 194 us
  other arithmetic: 67.7 us -> 0 us
  local copies, waits for them, and re-layouts: 34.6 us -> 12.5 us
  matrix products: 17.8 us -> 0 us
  between operations: 15.2 us -> 2.07 us
    reduce_scatter x6 -> x0, waiting for transfers between devices: 608 us -> none  [local(): lax.psum_scatter(value, 'dp', scatter_dimension=axis, tiled=True)]
    unnamed x15 -> x0, waiting for transfers between devices: 135 us -> none
    pallas_call x1 -> x2, Pallas kernels: 84.1 us -> 194 us  [the longest x1 164 us: trunk(): pl.pallas_call(functools.partial(trunk_kernel, columns, width, hidden, mi...]
    all_gather x2 -> x0, waiting for transfers between devices: 107 us -> none  [the longest x1 107 us: local(): quarter = lax.all_gather(table, 'dp', axis=0, tiled=True)]
    convert_element_type x11 -> x0, other arithmetic: 27.5 us -> none  [the longest x9 26 us: local(): low = lambda value, axis: scatter(value.astype(BF16), axis).astype(F32)]
    psum x1 -> x0, waiting for transfers between devices: 25.2 us -> none  [local(): embedded = lax.psum(picked, 'section')]
    select_n x10 -> x0, other arithmetic: 24.5 us -> none  [the longest x7 21 us: both(): jnp.where(core == 0, jnp.concatenate([value, swapped]), jnp.concatenate([...]
    dot_general x7 -> x0, matrix products: 17.8 us -> none  [the longest x4 13.8 us: local(): lax.dot_general(left, right, (((1,), (1,)), ((0,), (0,))), preferred_elem...]
  transfers between devices with their start and end apart: 25 -> 0, of which waited for: 14 -> 0; matrix products, arithmetic and copies ran while one was open for 10% -> 0% of each run, Pallas kernels for 0% -> 0%
where the time goes in v3:
time: 209 us; the launch traced here: 208 us
  Pallas kernels  194 us (93%)
  local copies, waits for them, and re-layouts  12.5 us (6%)
    pallas_call x1, Pallas kernels, trunk(): pl.pallas_call(functools.partial(trunk_kernel, columns, width, hidden, mi...  164 us
    pallas_call x1, Pallas kernels, lookup(): pl.pallas_call(functools.partial(lookup_kernel, columns, capacity), out_s...  29.8 us
    unnamed x33, local copies, waits for them, and re-layouts  9.72 us

profile of v3, /device:TPU:0, one launch (start us, length us, event | category | flops | bytes accessed | tf_op | source)
XLA Modules:
  0.0 208.5 jit_solution(10672437949779723122)
XLA Ops:
  1.3 0.8 copy.24
  2.1 0.7 reshape.34.ids
  2.8 0.0 copy-start
  2.8 29.8 %shard_map.204 = (bf16[512,512]{1,0:T(8,128)(2,1)S(1)}, bf16[512,1024]{1,0:T(8,128)(2,1)}, s32[8,2,512]{2,1,0:T(2,128)S(1)}, f32[8,128]{1,0:T(8,128)}, f32[64,51...) custom-call(s32[2,512]{1,0:T(2,128)} %reshape.34.ids, ...), custom_call_target="tpu_custom_call" | custom-call | tf_op jit(solution)/shard_map/pallas_call | solution.py:399
  32.6 1.2 slice.3
  34.5 0.0 copy-done
  34.5 0.0 copy-start.10
  34.5 0.6 copy-done.10
  35.1 0.1 dynamic_slice.3
  35.2 0.1 broadcast_in_dim.11
  35.3 0.1 broadcast_in_dim.12
  35.4 0.7 broadcast_in_dim.13.refs_1_
  36.0 164.1 %shard_map.205 = (f32[128,512]{1,0:T(8,128)}, f32[1,2,64]{2,1,0:T(2,128)}, f32[1,4,64]{2,1,0:T(4,128)}, f32[1,256]{1,0:T(1,128)}, f32[1,64,1536]{2,1,0:T(8,128)}...) custom-call(bf16[512,512]{1,0:T(8,128)(2,1)S(1)} %get-tuple-element., ...), custom_call_target="tpu_custom_call" | custom-call | tf_op jit(solution)/shard_map/pallas_call | solution.py:1132
  200.1 0.0 copy-start.4
  200.1 0.9 copy-done.4
  201.1 0.7 copy.50
  201.8 0.0 copy-start.9
  201.8 0.0 copy-start.7
  201.8 0.0 copy-start.8
  201.8 0.0 copy-start.3
  201.8 0.0 copy-start.6
  201.8 0.0 copy-start.2
  201.8 1.3 copy.51
  203.1 0.0 copy-done.9
  203.1 0.0 copy-start.1
  203.1 0.0 copy-start.5
  203.1 0.6 copy.52
  203.7 0.0 copy-done.7
  203.7 0.6 copy.53
  204.3 0.0 copy-done.8
  204.3 0.6 copy.54
  204.8 0.0 copy-done.3
  204.8 0.7 copy.55
  205.6 0.0 copy-done.6
  205.6 0.7 copy.56
  206.2 0.0 copy-done.2
  206.2 0.8 copy.57
  207.0 0.0 copy-done.1
  207.0 0.8 copy.58
  207.8 0.0 copy-done.5
  207.8 0.7 copy.59
  (2 shorter events, 0.0 us)
Async XLA Ops:
  2.8 31.7 %copy-start = (bf16[1000,512]{1,0:T(8,128)(2,1)S(1)}, bf16[1000,512]{1,0:T(8,128)(2,1)}, u32[]{:S(2)}) copy-start(bf16[1000,512]{1,0:T(8,128)(2,1)} %table.1) | copy-start | bytes 3072004
  34.5 0.7 copy-start.10
  200.1 1.0 copy-start.4
  201.8 1.3 copy-start.9
  201.8 1.9 copy-start.7
  201.8 2.5 %copy-start.8 = (f32[1,256]{1,0:T(1,128)S(1)}, f32[1,256]{1,0:T(1,128)}, u32[]{:S(2)}) copy-start(f32[1,256]{1,0:T(1,128)} %get-tuple-element.248) | copy-start | bytes 3076
  201.8 3.0 %copy-start.3 = (f32[1,64,1536]{2,1,0:T(8,128)S(1)}, f32[1,64,1536]{2,1,0:T(8,128)}, u32[]{:S(2)}) copy-start(f32[1,64,1536]{2,1,0:T(8,128)} %get-tuple-element.249) | copy-start | bytes 1179652
  201.8 3.8 %copy-start.6 = (f32[1,64,512]{2,1,0:T(8,128)S(1)}, f32[1,64,512]{2,1,0:T(8,128)}, u32[]{:S(2)}) copy-start(f32[1,64,512]{2,1,0:T(8,128)} %get-tuple-element.250) | copy-start | bytes 393220
  201.8 4.4 %copy-start.2 = (f32[1,64,2048]{2,1,0:T(8,128)S(1)}, f32[1,64,2048]{2,1,0:T(8,128)}, u32[]{:S(2)}) copy-start(f32[1,64,2048]{2,1,0:T(8,128)} %get-tuple-element.251) | copy-start | bytes 1572868
  203.1 3.9 %copy-start.1 = (f32[1,256,512]{2,1,0:T(8,128)S(1)}, f32[1,256,512]{2,1,0:T(8,128)}, u32[]{:S(2)}) copy-start(f32[1,256,512]{2,1,0:T(8,128)} %get-tuple-element.252) | copy-start | bytes 1572868
  203.1 4.7 %copy-start.5 = (f32[64,512]{1,0:T(8,128)S(1)}, f32[64,512]{1,0:T(8,128)}, u32[]{:S(2)}) copy-start(f32[64,512]{1,0:T(8,128)} %get-tuple-element.253) | copy-start | bytes 393220

commit v4 on v3

--- a/solution.py
+++ b/solution.py
@@ -351,7 +351,7 @@
     def _():
         slot_plan(ids_all[column, pl.ds(core, 1), :], match, span, jnp.int32(0), owners, turn, capacity)
 
-    most_out[...] = jnp.full(most_out.shape, most_distinct(ids_all, span, owners, lists), F32)
+    most_out[0] = most_distinct(ids_all, span, owners, lists).astype(jnp.int32)
 
     @pl.when(section >= 2)
     def _():
@@ -392,7 +392,7 @@
     shape = jax.ShapeDtypeStruct
     params = (gain, shift, bias, w_qkv, w_out, w_up, w_down)
     outs = [
-        shape((slots, width), BF16), shape((lists * capacity, padded_span), BF16), shape((columns, 2, slots), jnp.int32), shape((8, LANES), F32),
+        shape((slots, width), BF16), shape((lists * capacity, padded_span), BF16), shape((columns, 2, slots), jnp.int32), shape((1,), jnp.int32),
         shape((entries // 2, width), F32),
     ] + [shape(p.shape, p.dtype) for p in params]
     sem = pltpu.SemaphoreType.DMA
@@ -400,7 +400,7 @@
         functools.partial(lookup_kernel, columns, capacity),
         out_shape=outs,
         in_specs=[vmem] * 4 + [smem] + [hbm] * 7,
-        out_specs=[vmem] * 5 + [hbm] * 7,
+        out_specs=[vmem] * 3 + [smem, vmem] + [hbm] * 7,
         scratch_shapes=[
             pltpu.VMEM((owners * capacity, slots), BF16),
             pltpu.VMEM((max(lists, owners) * 8, LANES), F32), pltpu.VMEM((padded_span, width), BF16),
@@ -533,8 +533,8 @@
 
 PHASE_LAG = 2
 PROJECT_AFTER = 5
-ADD_LAG = 2
-VEC_GAP = 3
+ADD_LAG = 1
+VEC_GAP = 4
 SEND_NEAR = 1
 SEND_FAR = 8
 TABLE_STEP = 13
@@ -1109,6 +1109,37 @@
             pool_copy(d).wait_send()
 
 
+def deliver_kernel(*refs):
+    count = (len(refs) - 2) // 3
+    sources, targets, staged = refs[:count], refs[count:2 * count], refs[2 * count:3 * count]
+    in_sem, out_sem = refs[3 * count:]
+    arrivals = [pltpu.make_async_copy(sources[i], staged[i], in_sem.at[i]) for i in range(count)]
+    departures = [pltpu.make_async_copy(staged[i], targets[i], out_sem.at[i]) for i in range(count)]
+    for copy in arrivals:
+        copy.start()
+    for arrival, departure in zip(arrivals, departures):
+        arrival.wait()
+        departure.start()
+    for copy in departures:
+        copy.wait()
+
+
+def deliver(*values):
+    count = len(values)
+    hbm = pl.BlockSpec(memory_space=pl.ANY)
+    size = sum(4 * value.size for value in values)
+    return pl.pallas_call(
+        deliver_kernel,
+        out_shape=[jax.ShapeDtypeStruct(value.shape, value.dtype) for value in values],
+        in_specs=[hbm] * count,
+        out_specs=[hbm] * count,
+        scratch_shapes=[pltpu.VMEM(value.shape, value.dtype) for value in values] + [
+            pltpu.SemaphoreType.DMA((count,)), pltpu.SemaphoreType.DMA((count,))],
+        cost_estimate=pl.CostEstimate(flops=0, bytes_accessed=2 * size, transcendentals=0),
+        compiler_params=pltpu.CompilerParams(vmem_limit_bytes=VMEM_BYTES),
+    )(*values)
+
+
 def trunk(columns, x0, counts, pool_grad, own, theirs, cot, proj, picks, ids_all, span, vocab):
     rows, width = x0.shape
     hidden = own[5].shape[2]
@@ -1171,7 +1202,7 @@
     x0, picks, ids_all, most, pool_grad, *theirs = lookup(
         columns, ids, table, embed_cotangent, proj_weight, vocab_size, *own)
     capacity = picks.shape[0] // (2 * columns)
-    turns = (most[0, 0].astype(jnp.int32) + capacity - 1) // capacity
+    turns = (most[0] + capacity - 1) // capacity
     x0 = lax.fori_loop(
         1, turns, lambda turn, x: x + more_lookup(columns, turn.reshape(1), ids_all, table), x0)
     emb, g_gain, g_shift, g_bias, g_qkv, g_out, g_up, g_down, g_proj, g_table, dx = trunk(
@@ -1179,7 +1210,7 @@
         vocab_size)
     g_table = lax.fori_loop(
         1, turns, lambda turn, held: more_return(columns, turn.reshape(1), ids_all, dx, held), g_table)
-    return emb, g_table, g_gain, g_shift, g_bias, g_qkv, g_out, g_up, g_down, g_proj
+    return tuple(deliver(emb, g_table, g_gain, g_shift, g_bias, g_qkv, g_out, g_up, g_down, g_proj))
 
 
 def solution(mesh):

time: 209 us -> 202 us (0.967)
  local copies, waits for them, and re-layouts: 12.5 us -> 3.02 us
  Pallas kernels: 194 us -> 197 us
    unnamed x33 -> x5, local copies, waits for them, and re-layouts: 9.72 us -> 1.42 us
    pallas_call x0 -> x1, Pallas kernels: none -> 3.08 us  [deliver(): pl.pallas_call(deliver_kernel, out_shape=[jax.ShapeDtypeStruct(value.shap...]
where the time goes in v4:
time: 202 us
  Pallas kernels  197 us (98%)
  local copies, waits for them, and re-layouts  3.02 us (1%)
  between operations  2.24 us (1%)
    pallas_call x1, Pallas kernels, trunk(): pl.pallas_call(functools.partial(trunk_kernel, columns, width, hidden, mi...  164 us
    pallas_call x1, Pallas kernels, lookup(): pl.pallas_call(functools.partial(lookup_kernel, columns, capacity), out_s...  29.8 us

profile of v4, /device:TPU:0, one launch (start us, length us, event | category | flops | bytes accessed | tf_op | source)
XLA Modules:
  0.0 202.1 jit_solution(5614335696387197745)
XLA Ops:
  1.3 0.8 copy.24
  2.1 0.7 reshape.33.ids
  2.8 0.0 copy-start
  2.8 29.8 %shard_map.204 = (bf16[512,512]{1,0:T(8,128)(2,1)S(1)}, bf16[512,1024]{1,0:T(8,128)(2,1)}, s32[8,2,512]{2,1,0:T(2,128)S(1)}, s32[1]{0:T(128)}, f32[64,512]{1,0:T...) custom-call(s32[2,512]{1,0:T(2,128)} %reshape.33.ids, ...), custom_call_target="tpu_custom_call" | custom-call | tf_op jit(solution)/shard_map/pallas_call | solution.py:399
  33.3 0.0 copy-done
  33.3 0.0 copy-start.1
  33.4 0.6 copy-done.1
  34.0 0.1 dynamic_slice.3
  34.1 0.1 broadcast_in_dim.11
  34.2 0.1 broadcast_in_dim.12
  34.2 0.7 broadcast_in_dim.13.refs_1_
  34.9 163.9 %shard_map.205 = (f32[128,512]{1,0:T(8,128)}, f32[1,2,64]{2,1,0:T(2,128)}, f32[1,4,64]{2,1,0:T(4,128)}, f32[1,256]{1,0:T(1,128)}, f32[1,64,1536]{2,1,0:T(8,128)}...) custom-call(bf16[512,512]{1,0:T(8,128)(2,1)S(1)} %get-tuple-element., ...), custom_call_target="tpu_custom_call" | custom-call | tf_op jit(solution)/shard_map/pallas_call | solution.py:1163
  198.8 3.1 %shard_map.206 = (f32[128,512]{1,0:T(8,128)}, f32[1000,512]{1,0:T(8,128)}, f32[1,2,64]{2,1,0:T(2,128)}, f32[1,4,64]{2,1,0:T(4,128)}, f32[1,256]{1,0:T(1,128)}, /...) custom-call(f32[128,512]{1,0:T(8,128)} %get-tuple-element.102.refs_0, ...), custom_call_target="tpu_custom_call" | custom-call | bytes 8033280 | tf_op jit(solution)/shard_map/pallas_call | solution.py:1131
  (2 shorter events, 0.0 us)
Async XLA Ops:
  2.8 30.6 %copy-start = (bf16[1000,512]{1,0:T(8,128)(2,1)S(1)}, bf16[1000,512]{1,0:T(8,128)(2,1)}, u32[]{:S(2)}) copy-start(bf16[1000,512]{1,0:T(8,128)(2,1)} %table.1) | copy-start | bytes 3072004
  33.3 0.7 copy-start.1

commit v5 on v4

--- a/solution.py
+++ b/solution.py
@@ -133,7 +133,7 @@
         used_rows[pl.ds(pl.multiple_of(d * 8, 8), 8), :] = jnp.where(counts > 0, 1.0, 0.0)
         return carry
 
-    lax.fori_loop(0, lists, count, 0)
+    lax.fori_loop(0, lists, count, 0, unroll=8)
     used = used_rows[pl.ds(0, lists * 8), :]
     used_rows[pl.ds(0, lists * 8), :] = in_round(positions(used), used, turn, capacity)
 
@@ -145,7 +145,7 @@
                 place[block:block + 1, :] == wanted)
         return carry
 
-    lax.fori_loop(0, lists, spread, 0)
+    lax.fori_loop(0, lists, spread, 0, unroll=8)
 
 
 def slot_codes(ids_row, span, first):
@@ -281,8 +281,7 @@
     return barrier
 
 
-def pack_rows(table, padded, picks, packed, span, capacity, lists):
-    padded[pl.ds(0, span), :] = table[...]
+def pack_rows(padded, picks, packed, capacity, lists):
     for d in range(0, lists, 4):
         rows = dot_nn(picks[d * capacity:(d + 4) * capacity, :], padded[...]).astype(BF16)
         packed[d:d + 4] = rows.reshape(4, capacity, rows.shape[1])
@@ -306,6 +305,7 @@
     barrier = greet_all(columns, me, owners)
     ids_all[column] = ids[...]
     padded[...] = jnp.zeros_like(padded)
+    padded[pl.ds(0, span), :] = table[...]
     pl.semaphore_wait(barrier, owners - 1)
 
     def ids_copy(d):
@@ -343,7 +343,7 @@
         remote(ids, ids_all.at[source], i_send.at[d - 1], i_recv.at[source], (section, source)).wait_recv()
     turn = jnp.int32(0)
     owner_plan(ids_all, picks, used_rows, me * span, span, turn, capacity, lists)
-    pack_rows(table, padded, picks, packed, span, capacity, lists)
+    pack_rows(padded, picks, packed, capacity, lists)
     start, arrive, left = lookup_rounds(columns, me, packed, landed, t_send, t_recv)
     start()
 
@@ -432,8 +432,9 @@
         pl.semaphore_wait(barrier, lists)
 
     padded[...] = jnp.zeros_like(padded)
+    padded[pl.ds(0, span), :] = table[...]
     owner_plan(ids_all, picks, used_rows, me * span, span, turn[0], capacity, lists)
-    pack_rows(table, padded, picks, packed, span, capacity, lists)
+    pack_rows(padded, picks, packed, capacity, lists)
     start, arrive, left = lookup_rounds(columns, me, packed, landed, t_send, t_recv)
     start()
     x_out[...] = jnp.zeros_like(x_out)

time: 202 us -> 200 us (0.990)
  no operation moved by 1% of the time
where the time goes in v5:
time: 200 us
  Pallas kernels  195 us (98%)
  local copies, waits for them, and re-layouts  3.02 us (2%)
  between operations  2.24 us (1%)
    pallas_call x1, Pallas kernels, trunk(): pl.pallas_call(functools.partial(trunk_kernel, columns, width, hidden, mi...  164 us
    pallas_call x1, Pallas kernels, lookup(): pl.pallas_call(functools.partial(lookup_kernel, columns, capacity), out_s...  28.1 us

profile of v5, /device:TPU:0, one launch (start us, length us, event | category | flops | bytes accessed | tf_op | source)
XLA Modules:
  0.0 200.2 jit_solution(2545516041073679273)
XLA Ops:
  1.3 0.8 copy.24
  2.1 0.7 reshape.33.ids
  2.8 0.0 copy-start
  2.8 28.1 %shard_map.204 = (bf16[512,512]{1,0:T(8,128)(2,1)S(1)}, bf16[512,1024]{1,0:T(8,128)(2,1)}, s32[8,2,512]{2,1,0:T(2,128)S(1)}, s32[1]{0:T(128)}, f32[64,512]{1,0:T...) custom-call(s32[2,512]{1,0:T(2,128)} %reshape.33.ids, ...), custom_call_target="tpu_custom_call" | custom-call | tf_op jit(solution)/shard_map/pallas_call | solution.py:399
  31.5 0.0 copy-done
  31.6 0.0 copy-start.1
  31.6 0.6 copy-done.1
  32.2 0.1 dynamic_slice.3
  32.3 0.1 broadcast_in_dim.11
  32.4 0.1 broadcast_in_dim.12
  32.4 0.7 broadcast_in_dim.13.refs_1_
  33.1 163.8 %shard_map.205 = (f32[128,512]{1,0:T(8,128)}, f32[1,2,64]{2,1,0:T(2,128)}, f32[1,4,64]{2,1,0:T(4,128)}, f32[1,256]{1,0:T(1,128)}, f32[1,64,1536]{2,1,0:T(8,128)}...) custom-call(bf16[512,512]{1,0:T(8,128)(2,1)S(1)} %get-tuple-element., ...), custom_call_target="tpu_custom_call" | custom-call | tf_op jit(solution)/shard_map/pallas_call | solution.py:1164
  196.9 3.1 %shard_map.206 = (f32[128,512]{1,0:T(8,128)}, f32[1000,512]{1,0:T(8,128)}, f32[1,2,64]{2,1,0:T(2,128)}, f32[1,4,64]{2,1,0:T(4,128)}, f32[1,256]{1,0:T(1,128)}, /...) custom-call(f32[128,512]{1,0:T(8,128)} %get-tuple-element.102.refs_0, ...), custom_call_target="tpu_custom_call" | custom-call | bytes 8033280 | tf_op jit(solution)/shard_map/pallas_call | solution.py:1132
  (2 shorter events, 0.0 us)
Async XLA Ops:
  2.8 28.8 %copy-start = (bf16[1000,512]{1,0:T(8,128)(2,1)S(1)}, bf16[1000,512]{1,0:T(8,128)(2,1)}, u32[]{:S(2)}) copy-start(bf16[1000,512]{1,0:T(8,128)(2,1)} %table.1) | copy-start | bytes 3072004
  31.6 0.7 copy-start.1
